TPU v7x, 32 devices: a whole 2x2x4 slice. The times are simulated.
32 devices in a mesh: groups: 2 (over y), owner: 8 (over z, x), batch: 2 (over core).
Axes of the slice: x: 2, y: 2, z: 4, core: 2. Of those that a mesh axis runs over, the one named last changes fastest.
Arguments:
- features: bfloat16 [4096, 768], P('owner'), may hold values from -12 to 12
- w_first: bfloat16 [768, 512], replicated, may hold values from -0.21875 to 0.21875
- w_second: bfloat16 [512, 512], replicated, may hold values from -0.25 to 0.25
- w_third: bfloat16 [512, 153], replicated, may hold values from -0.25 to 0.25
- nbr_ids: int32 [512, 32], P(('groups', 'owner', 'batch')), parts along dimension 0, may hold values from 0 to 4095, as said below
- nbr_weight: float32 [512, 32], P(('groups', 'owner', 'batch')), parts along dimension 0, may hold values from 0.05 to 0.5
- labels: int32 [512], P(('groups', 'owner', 'batch')), parts along dimension 0, may hold values from 0 to 152
Outputs:
- grad_first: bfloat16 [1536, 512], P('groups'), parts along dimension 0
- grad_second: bfloat16 [1024, 512], P('groups'), parts along dimension 0
- grad_third: bfloat16 [1024, 153], P('groups'), parts along dimension 0
- target_loss: float32 [512], P(('groups', 'owner', 'batch')), parts along dimension 0
There are 2 independent parts, one for each index of `groups`. A program takes and returns all parts, laid end to end along the dimension named above; an argument that names none is the same for every part. Nothing has to cross between parts.
Inputs may be any that keep to these rules, and one draw needn't show every extreme that they name: `nbr_ids`: node n belongs to owner n // 512. In each device's block of 16 targets the 32 neighbour ids of all its targets fall at most 128 times in one owner's nodes, and exactly 128 times for at least one owner.
All inputs are finite; a program needn't handle non-finite values.
Results may differ from a plain program's by a relative error of at most 0.0063.
Values may be sent and summed in bfloat16 or wider, within the bound.
No kernel may reach another device: no remote copies, remote signals or barrier semaphores. Data moves between devices by JAX's collectives and lax.ppermute only.
A program may use at most 64 MiB of HBM per device.

v0:
```python
import jax
import jax.numpy as jnp
from jax import lax
from jax.sharding import PartitionSpec as P


def silu_slope(pre):
    sigma = jax.nn.sigmoid(pre)
    return sigma * (1.0 + pre * (1.0 - sigma))


def forward_rows(inputs, w_first, w_second, w_third):
    pre_one = jnp.dot(inputs, w_first, preferred_element_type=jnp.float32)
    hidden_one = jax.nn.silu(pre_one).astype(jnp.bfloat16)
    pre_two = jnp.dot(hidden_one, w_second, preferred_element_type=jnp.float32)
    hidden_two = jax.nn.silu(pre_two).astype(jnp.bfloat16)
    scores = jnp.dot(hidden_two, w_third, preferred_element_type=jnp.float32).astype(jnp.bfloat16)
    return (pre_one, hidden_one, pre_two, hidden_two, scores)


def body(features, w_first, w_second, w_third, nbr_ids, nbr_weight, labels):
    target_rows, fanout = nbr_ids.shape
    node_dev = features.shape[0]
    classes = w_third.shape[1]
    owners = lax.axis_size("owner")
    slots_per = 2 * target_rows * fanout // owners
    flat_ids = nbr_ids.reshape(-1)
    owner_of = flat_ids // node_dev
    member = (owner_of[:, None] == jnp.arange(owners, dtype=jnp.int32)[None, :]).astype(jnp.int32)
    within = jnp.sum((jnp.cumsum(member, axis=0) - 1) * member, axis=1)
    slot_index = owner_of * slots_per + within
    request = (
        jnp.full((owners * slots_per,), -1, jnp.int32)
        .at[slot_index]
        .set(flat_ids - owner_of * node_dev)
    )
    asked_rows = lax.all_to_all(
        request.reshape(owners, slots_per), "owner", split_axis=0, concat_axis=0, tiled=True
    ).reshape(-1)
    fetched = jnp.where(
        (asked_rows >= 0)[:, None],
        features[jnp.maximum(asked_rows, 0)],
        jnp.zeros((), jnp.bfloat16),
    )
    stored = forward_rows(fetched, w_first, w_second, w_third)
    returned = lax.all_to_all(
        stored[4].reshape(owners, slots_per, classes),
        "owner",
        split_axis=0,
        concat_axis=0,
        tiled=True,
    )
    entry_scores = returned.reshape(-1, classes)[slot_index]
    logits = jnp.sum(
        nbr_weight[:, :, None]
        * entry_scores.reshape(target_rows, fanout, classes).astype(jnp.float32),
        axis=1,
    )
    log_prob = jax.nn.log_softmax(logits)
    target = jax.nn.one_hot(labels, classes, dtype=jnp.float32)
    target_loss = -jnp.sum(target * log_prob, axis=1)
    grad_logits = jnp.exp(log_prob) - target
    entry_grads = (
        (nbr_weight[:, :, None] * grad_logits[:, None, :]).astype(jnp.bfloat16).reshape(-1, classes)
    )
    outgoing = (
        jnp.zeros((owners * slots_per, classes), jnp.bfloat16).at[slot_index].set(entry_grads)
    )
    upstream = lax.all_to_all(
        outgoing.reshape(owners, slots_per, classes),
        "owner",
        split_axis=0,
        concat_axis=0,
        tiled=True,
    ).reshape(-1, classes)
    pre_one, hidden_one, pre_two, hidden_two = (stored[0], stored[1], stored[2], stored[3])
    grad_third = jnp.einsum("rh,rc->hc", hidden_two, upstream, preferred_element_type=jnp.float32)
    back_two = (
        jnp.einsum("rc,hc->rh", upstream, w_third, preferred_element_type=jnp.float32)
        * silu_slope(pre_two)
    ).astype(jnp.bfloat16)
    grad_second = jnp.einsum("rg,rh->gh", hidden_one, back_two, preferred_element_type=jnp.float32)
    back_one = (
        jnp.einsum("rh,gh->rg", back_two, w_second, preferred_element_type=jnp.float32)
        * silu_slope(pre_one)
    ).astype(jnp.bfloat16)
    grad_first = jnp.einsum("rd,rh->dh", fetched, back_one, preferred_element_type=jnp.float32)
    grad_first, grad_second, grad_third = lax.psum(
        (grad_first, grad_second, grad_third), ("owner", "batch")
    )
    return (
        grad_first.astype(jnp.bfloat16),
        grad_second.astype(jnp.bfloat16),
        grad_third.astype(jnp.bfloat16),
        target_loss,
    )


def solution(mesh):
    in_specs = (
        P("owner", None),
        P(),
        P(),
        P(),
        P(("groups", "owner", "batch"), None),
        P(("groups", "owner", "batch"), None),
        P(("groups", "owner", "batch")),
    )
    out_specs = (
        P("groups", None),
        P("groups", None),
        P("groups", None),
        P(("groups", "owner", "batch")),
    )
    return jax.shard_map(body, mesh=mesh, in_specs=in_specs, out_specs=out_specs, check_vma=False)
```

profile of v0, /device:TPU:0, one launch (start us, length us, event | category | flops | bytes accessed | tf_op | source)
XLA Modules:
  0.0 148.7 jit_solution(1324929946650593220)
XLA Ops:
  0.6 0.8 reshape.233
  1.5 0.8 reshape.232
  2.3 0.8 reshape.231
  3.1 1.1 reduce-window.6
  4.6 2.4 %scatter_custom_fusion = s32[1024]{0:T(1024)S(1)} fusion(s32[512]{0:T(512)S(1)} %bitcast.61, s32[512]{0:T(512)S(1)} %get-tuple-element.9, s32[]{:T(128)} %constant.23.clone.1), kind=kCustom, calls=%fused_computation.54 | custom fusion | bytes 4100 | tf_op jit(solution)/shard_map/scatter | solution.py:35
  7.1 13.5 %all_to_all.19 = s32[8,1,128]{2,1,0:T(1,128)S(1)} all-to-all(s32[8,1,128]{2,1,0:T(1,128)S(1)} %bitcast.60), channel_id=1, replica_groups=mesh['groups'=2,'owner'=8,'batch'=2] {'owner'}, dimensions={0} | all-to-all | bytes 8192 | tf_op jit(solution)/shard_map/all_to_all | solution.py:37
  20.6 5.7 %gather_fusion = bf16[1024,768]{1,0:T(8,128)(2,1)S(1)} fusion(bf16[512,768]{1,0:T(8,128)(2,1)} %param.7, s32[1024]{0:T(1024)S(1)} %bitcast_clamp_fusion), kind=kCustom, calls=%fused_computation | custom fusion | bytes 3149824 | tf_op jit(solution)/shard_map/gather | solution.py:42
  26.3 2.6 %multiply_convert_fusion.3 = (bf16[1024,512]{1,0:T(8,128)(2,1)S(1)}, f32[1024,512]{1,0:T(8,128)}) fusion(bf16[768,512]{1,0:T(8,128)(2,1)S(1)} %copy-done, bf16[1024,768]{1,0:T(8,128)(2,1)S(1)} %gather_fusion, pred[1024]{0:T(1024)(128)(4,1)S(1)} %compare_bitcast_fusion), kind=kOutput, calls=%fused_computation.8 | convolution fusion | flops 808714240 | bytes 5506048 | tf_op jit(solution)/shard_map/dot_general | solution.py:13
  28.9 2.2 %multiply_convert_fusion.2 = (bf16[1024,512]{1,0:T(8,128)(2,1)S(1)}, f32[1024,512]{1,0:T(8,128)}) fusion(bf16[1024,512]{1,0:T(8,128)(2,1)S(1)} %get-tuple-element.11, bf16[512,512]{1,0:T(8,128)(2,1)S(1)} %copy-done.6), kind=kOutput, calls=%fused_computation.6 | convolution fusion | flops 539492352 | bytes 4718592 | tf_op jit(solution)/shard_map/dot_general | solution.py:15
  31.2 0.5 convolution_convert_fusion
  31.7 0.8 copy.25
  32.5 3.6 %all-to-all-start.1 = ((bf16[8,128,153]{1,2,0:T(8,128)(2,1)}), bf16[8,128,153]{1,2,0:T(8,128)(2,1)S(1)}, u32[]{:S(2)}, u32[]{:S(2)}) async-start(bf16[8,128,153]{1,2,0:T(8,128)(2,1)} %copy.25), calls=%async_computation.1 | async-start | bytes 655360 | tf_op jit(solution)/shard_map/all_to_all | solution.py:46
  36.2 9.0 %all-to-all-done.1 = bf16[8,128,153]{1,2,0:T(8,128)(2,1)S(1)} async-done(((bf16[8,128,153]{1,2,0:T(8,128)(2,1)}), bf16[8,128,153]{1,2,0:T(8,128)(2,1)S(1)}, u32[]{:S(2)}, u32[]{:S(2)}) %all-to-all-start.1) | async-done | bytes 313376 | tf_op jit(solution)/shard_map/all_to_all | solution.py:46
  45.4 2.0 %gather_fusion.1 = bf16[512,153]{1,0:T(8,128)(2,1)S(1)} fusion(bf16[1024,153]{1,0:T(8,128)(2,1)S(1)} %bitcast.50, s32[1024]{0:T(1024)S(1)} %pad_clamp_fusion), kind=kCustom, calls=%fused_computation.1 | custom fusion | bytes 315392 | tf_op jit(solution)/shard_map/gather | solution.py:53
  48.2 2.5 %scatter_custom_fusion.1 = bf16[1024,153]{1,0:T(8,128)(2,1)S(1)} fusion(s32[512]{0:T(512)S(1)} %bitcast.63, bf16[512,153]{1,0:T(8,128)(2,1)S(1)} %fusion.4, bf16[]{:T(256)} %constant.48.clone.1), kind=kCustom, calls=%fused_computation.21 | custom fusion | bytes 313346 | tf_op jit(solution)/shard_map/scatter | solution.py:67
  50.7 0.9 copy.28
  51.6 3.6 %all-to-all-start.2 = ((bf16[8,128,153]{1,2,0:T(8,128)(2,1)}), bf16[8,128,153]{1,2,0:T(8,128)(2,1)S(1)}, u32[]{:S(2)}, u32[]{:S(2)}) async-start(bf16[8,128,153]{1,2,0:T(8,128)(2,1)} %copy.28), calls=%async_computation.2 | async-start | bytes 655360 | tf_op jit(solution)/shard_map/all_to_all | solution.py:69
  55.2 0.5 neg.14
  55.7 9.1 %all-to-all-done.2 = bf16[8,128,153]{1,2,0:T(8,128)(2,1)S(1)} async-done(((bf16[8,128,153]{1,2,0:T(8,128)(2,1)}), bf16[8,128,153]{1,2,0:T(8,128)(2,1)S(1)}, u32[]{:S(2)}, u32[]{:S(2)}) %all-to-all-start.2) | async-done | bytes 313376 | tf_op jit(solution)/shard_map/all_to_all | solution.py:69
  65.0 1.1 fusion.19
  66.5 0.9 multiply_convert_fusion.1
  67.7 1.7 %fusion.18 = f32[512,512]{1,0:T(8,128)} fusion(bf16[1024,512]{1,0:T(8,128)(2,1)S(1)} %copy-done.9, bf16[1024,512]{1,0:T(8,128)(2,1)S(1)} %multiply_convert_fusion.1), kind=kOutput, calls=%fused_computation.61 | convolution fusion | flops 536870912 | bytes 3145728 | tf_op jit(solution)/shard_map/rg,rh->gh/dot_general | solution.py:82
  69.5 4.3 %fusion = f32[768,512]{1,0:T(8,128)S(1)} fusion(f32[1024,512]{1,0:T(8,128)} %get-tuple-element.12, bf16[1024,512]{1,0:T(8,128)(2,1)} %copy-done.10, bf16[512,512]{1,0:T(8,128)(2,1)S(1)} %copy-done.7, bf16[1024,768]{1,0:T(8,128)(2,1)} %copy-done.1, pred[1024]{0:T(1024)(128)(4,1)S(1)} %compare_bitcast_fusion), kind=kOutput, calls=%fused_computation.12 | convolution fusion | flops 1347682304 | bytes 6816768 | tf_op jit(solution)/shard_map/rd,rh->dh/dot_general | solution.py:87
  73.8 74.9 %all-reduce.2 = (bf16[768,512]{1,0:T(8,128)(2,1)}, bf16[512,512]{1,0:T(8,128)(2,1)}, bf16[512,153]{0,1:T(8,128)(2,1)}) all-reduce(f32[768,512]{1,0:T(8,128)S(1)} %fusion, f32[512,512]{1,0:T(8,128)} %fusion.18, f32[512,153]{0,1:T(8,128)S(1)} %copy-done.2), channel_id=1, replica_groups=mesh['groups'=2,'owner'=8,'batch'=2] {'owner','batch'}, use_global_device_ids=true, to_apply=%region_8.9 | all-reduce | flops 733696 | bytes 4402176 | tf_op jit(solution)/shard_map/psum | solution.py:88
  (48 shorter events, 2.6 us)
Async XLA Ops:
  0.6 25.7 %copy-start = (bf16[768,512]{1,0:T(8,128)(2,1)S(1)}, bf16[768,512]{1,0:T(8,128)(2,1)}, u32[]{:S(2)}) copy-start(bf16[768,512]{1,0:T(8,128)(2,1)} %param.8) | copy-start | bytes 2359300
  26.3 2.6 %copy-start.1 = (bf16[1024,768]{1,0:T(8,128)(2,1)}, bf16[1024,768]{1,0:T(8,128)(2,1)S(1)}, u32[]{:S(2)}) copy-start(bf16[1024,768]{1,0:T(8,128)(2,1)S(1)} %gather_fusion) | copy-start | bytes 4718596
  26.3 2.6 %copy-start.6 = (bf16[512,512]{1,0:T(8,128)(2,1)S(1)}, bf16[512,512]{1,0:T(8,128)(2,1)}, u32[]{:S(2)}) copy-start(bf16[512,512]{1,0:T(8,128)(2,1)} %param.9) | copy-start | bytes 1572868
  28.9 2.2 %copy-start.8 = (bf16[1024,512]{1,0:T(8,128)(2,1)}, bf16[1024,512]{1,0:T(8,128)(2,1)S(1)}, u32[]{:S(2)}) copy-start(bf16[1024,512]{1,0:T(8,128)(2,1)S(1)} %get-tuple-element.11) | copy-start | bytes 3145732
  28.9 2.2 %copy-start.3 = (bf16[512,153]{0,1:T(8,128)(2,1)S(1)}, bf16[512,153]{0,1:T(8,128)(2,1)}, u32[]{:S(2)}) copy-start(bf16[512,153]{0,1:T(8,128)(2,1)} %param.10) | copy-start | bytes 470020
  31.1 4.9 %copy-start.4 = (f32[16,32]{1,0:T(8,128)S(1)}, f32[16,32]{1,0:T(8,128)}, u32[]{:S(2)}) copy-start(f32[16,32]{1,0:T(8,128)} %param.12) | copy-start | bytes 6148
  32.5 15.3 %copy-start.5 = (s32[16]{0:T(128)S(1)}, s32[16]{0:T(128)}, u32[]{:S(2)}) copy-start(s32[16]{0:T(128)} %param.13) | copy-start | bytes 196
  32.5 12.7 %all-to-all-start.1 = ((bf16[8,128,153]{1,2,0:T(8,128)(2,1)}), bf16[8,128,153]{1,2,0:T(8,128)(2,1)S(1)}, u32[]{:S(2)}, u32[]{:S(2)}) async-start(bf16[8,128,153]{1,2,0:T(8,128)(2,1)} %copy.25), calls=%async_computation.1 | async-start | bytes 655360 | tf_op jit(solution)/shard_map/all_to_all | solution.py:46
  51.6 13.2 %all-to-all-start.2 = ((bf16[8,128,153]{1,2,0:T(8,128)(2,1)}), bf16[8,128,153]{1,2,0:T(8,128)(2,1)S(1)}, u32[]{:S(2)}, u32[]{:S(2)}) async-start(bf16[8,128,153]{1,2,0:T(8,128)(2,1)} %copy.28), calls=%async_computation.2 | async-start | bytes 655360 | tf_op jit(solution)/shard_map/all_to_all | solution.py:69
  64.8 1.7 %copy-start.11 = (f32[1024,512]{1,0:T(8,128)S(1)}, f32[1024,512]{1,0:T(8,128)}, u32[]{:S(2)}) copy-start(f32[1024,512]{1,0:T(8,128)} %get-tuple-element.14) | copy-start | bytes 6291460
  66.5 1.2 copy-start.9
  67.7 1.7 %copy-start.10 = (bf16[1024,512]{1,0:T(8,128)(2,1)}, bf16[1024,512]{1,0:T(8,128)(2,1)S(1)}, u32[]{:S(2)}) copy-start(bf16[1024,512]{1,0:T(8,128)(2,1)S(1)} %multiply_convert_fusion.1) | copy-start | bytes 3145732
  67.7 1.7 %copy-start.7 = (bf16[512,512]{1,0:T(8,128)(2,1)S(1)}, bf16[512,512]{1,0:T(8,128)(2,1)}, u32[]{:S(2)}) copy-start(bf16[512,512]{1,0:T(8,128)(2,1)} %param.9) | copy-start | bytes 1572868
  69.5 4.3 %copy-start.2 = (f32[512,153]{0,1:T(8,128)S(1)}, f32[512,153]{0,1:T(8,128)}, u32[]{:S(2)}) copy-start(f32[512,153]{0,1:T(8,128)} %fusion.19) | copy-start | bytes 940036
where the time goes:
time: 149 us
  blocking collectives  88.4 us (59%)
  local copies, waits for them, and re-layouts  18.3 us (12%)
  waiting for transfers between devices  18.1 us (12%)
  matrix products  13.2 us (9%)
  starting transfers between devices  7.15 us (5%)
  other arithmetic  2.64 us (2%)
    psum x1, blocking collectives, body(): lax.psum((grad_first, grad_second, grad_third), ('owner', 'batch'))  74.9 us
    all_to_all x1, blocking collectives, body(): lax.all_to_all(request.reshape(owners, slots_per), 'owner', split_axis=0,...  13.5 us
    all_to_all x1, waiting for transfers between devices, body(): lax.all_to_all(outgoing.reshape(owners, slots_per, classes), 'owner', spl...  9.1 us
    all_to_all x1, waiting for transfers between devices, body(): lax.all_to_all(stored[4].reshape(owners, slots_per, classes), 'owner', sp...  8.99 us
    gather x1, local copies, waits for them, and re-layouts, body(): features[jnp.maximum(asked_rows, 0)]  5.71 us
    dot_general x1, matrix products, body(): jnp.einsum('rd,rh->dh', fetched, back_one, preferred_element_type=jnp.flo...  4.28 us
    all_to_all x1, starting transfers between devices, body(): lax.all_to_all(outgoing.reshape(owners, slots_per, classes), 'owner', spl...  3.58 us
    all_to_all x1, starting transfers between devices, body(): lax.all_to_all(stored[4].reshape(owners, slots_per, classes), 'owner', sp...  3.56 us
  transfers between devices with their start and end apart: 2, of which 2 were waited for; matrix products, arithmetic and copies ran while one was open for 0% of the time, Pallas kernels for 0%

commit v1 on v0

v1 whole, which is shorter than its diff:
```python
import functools
import jax
import jax.numpy as jnp
from jax import lax
from jax.experimental import pallas as pl
from jax.experimental.pallas import tpu as pltpu
from jax.sharding import PartitionSpec as P

BF = jnp.bfloat16
F32 = jnp.float32
ROW = 16
LANE = 128


def nn(a, b):
    return lax.dot_general(a, b, (((1,), (0,)), ((), ())), preferred_element_type=F32)


def nt(a, b):
    return lax.dot_general(a, b, (((1,), (1,)), ((), ())), preferred_element_type=F32)


def tn(a, b):
    return lax.dot_general(a, b, (((0,), (0,)), ((), ())), preferred_element_type=F32)


def split(v):
    high = v.astype(BF)
    return high, (v - high.astype(F32)).astype(BF)


def device_slice():
    place = lax.rem(lax.axis_index("owner"), 2) * 2 + lax.axis_index("batch")
    return pl.multiple_of(place * LANE, LANE)


def layers(rows, w_first, w_second, h1, h2, s1, s2, one, two):
    pre = nn(rows, w_first)
    sigma = 1.0 / (1.0 + jnp.exp(-pre))
    hidden = (pre * sigma).astype(BF)
    h1[...] = hidden
    one[...] = sigma * (1.0 + pre * (1.0 - sigma))
    pre = nn(hidden, w_second)
    sigma = 1.0 / (1.0 + jnp.exp(-pre))
    hidden = (pre * sigma).astype(BF)
    two[...] = hidden.astype(F32)
    s2[...] = sigma * (1.0 + pre * (1.0 - sigma))
    cols = pl.ds(device_slice(), LANE)
    s1[...] = one[:, cols]
    h2[...] = two[:, cols].astype(BF)
    return hidden


def own_kernel(x, w_first, w_second, w3t, scores, h1, h2, s1, s2, one, two):
    hidden = layers(x[...], w_first[...], w_second[...], h1, h2, s1, s2, one, two)
    scores[...] = nt(w3t[...], hidden).astype(BF)


def peer_kernel(mine, theirs, w_first, w_second, x, h1, h2, s1, s2, one, two):
    half = mine.shape[0]
    core = lax.axis_index("batch")
    x[pl.ds(pl.multiple_of(core * half, half), half), :] = mine[...]
    x[pl.ds(pl.multiple_of((1 - core) * half, half), half), :] = theirs[...]
    layers(x[...], w_first[...], w_second[...], h1, h2, s1, s2, one, two)


def spread(nodes, packed, high, low, label, ids, wts):
    fanout = ids.shape[0]
    targets = ids.shape[1]
    rows = packed.shape[0]
    node_dev = high.shape[0] // 2
    p = packed[...]
    if rows < LANE:
        p = jnp.concatenate([p] * (LANE // rows), axis=0)
    t = p.T
    parts = [t[i * fanout : (i + 1) * fanout] for i in range(4)]
    if rows < LANE:
        lane = lax.broadcasted_iota(jnp.int32, (fanout, LANE), 1)
        coded = jnp.where(lane < rows, parts[0], parts[2])
        wts[...] = jnp.where(lane < rows, parts[1], parts[3])
    else:
        coded = jnp.concatenate([parts[0], parts[2]], axis=1)
        wts[...] = jnp.concatenate([parts[1], parts[3]], axis=1)
    cls = jnp.floor(coded * (1.0 / nodes))
    label[...] = cls[0:1].astype(jnp.int32)
    ids[...] = (coded - cls * nodes).astype(jnp.int32)
    me = lax.axis_index("owner")
    block = 64
    per_side = node_dev // block

    def step(i, carry):
        side = i // per_side
        owner = jnp.where(side == 0, me, me + 1 - 2 * lax.rem(me, 2))
        base = owner * node_dev + lax.rem(i, per_side) * block
        node = lax.broadcasted_iota(jnp.int32, (block, LANE), 0) + base
        at = pl.ds(pl.multiple_of(i * block, block), block)
        for c in range(targets // LANE):
            cols = slice(c * LANE, (c + 1) * LANE)
            total = jnp.zeros((block, LANE), F32)
            for k in range(fanout):
                total += jnp.where(ids[k : k + 1, cols] == node, wts[k : k + 1, cols], 0.0)
            top, rest = split(total)
            high[at, cols] = top
            low[at, cols] = rest
        return carry

    lax.fori_loop(0, 2 * per_side, step, 0)


def logit_kernel(nodes, packed, mine, theirs, high, low, label, part, send, ids, wts):
    spread(nodes, packed, high, low, label, ids, wts)
    n = mine.shape[1]
    total = nn(mine[...], high[:n]) + nn(mine[...], low[:n])
    total += nn(theirs[...], high[n:]) + nn(theirs[...], low[n:])
    part[...] = total
    send[...] = total.astype(BF)


def far_kernel(nodes, packed, high, low, label, ids, wts):
    spread(nodes, packed, high, low, label, ids, wts)


def softmax_kernel(logits, got, label, grad, send, loss):
    v = logits[...] + got[...].astype(F32)
    top = jnp.max(v, axis=0, keepdims=True)
    e = jnp.exp(v - top)
    total = jnp.sum(e, axis=0, keepdims=True)
    hit = lax.broadcasted_iota(jnp.int32, v.shape, 0) == label[...]
    loss[...] = jnp.log(total) + top - jnp.sum(jnp.where(hit, v, 0.0), axis=0, keepdims=True)
    g = e / total - jnp.where(hit, 1.0, 0.0)
    grad[...] = g
    send[...] = g.astype(BF)


def back_kernel(bit, grad, far_grad, high, low, far_high, far_low, x, px, h1, ph1, h2, ph2, s1, ps1, s2, ps2, w3t, w2, send, keep, acc, two):
    top, rest = split(grad[...])
    far = far_grad[...]
    n = x.shape[0]
    depth = x.shape[1]
    hidden = h1.shape[1]
    classes = w3t.shape[0]
    cols = pl.ds(device_slice(), LANE)
    w2_rows = w2[cols, :]
    for side, (x_, h1_, h2_, s1_, s2_) in enumerate(((x, h1, h2, s1, s2), (px, ph1, ph2, ps1, ps2))):
        at = slice(side * n, (side + 1) * n)
        hi, lo, fhi, flo = high[at], low[at], far_high[at], far_low[at]
        g = nt(hi, top) + nt(lo, top) + nt(hi, rest) + nt(fhi, far) + nt(flo, far)
        gt = nt(top, hi) + nt(top, lo) + nt(rest, hi) + nt(far, fhi) + nt(far, flo)
        b2 = nn(g.astype(BF), w3t[...]) * s2_[...]
        two[...] = b2
        b2 = b2.astype(BF)
        b2_cols = two[:, cols].astype(BF)
        b1 = (nt(b2, w2_rows) * s1_[...]).astype(BF)
        first = tn(x_[...], b1)
        second = tn(h1_[...], b2_cols)
        third = nn(gt.astype(BF), h2_[...])
        if side == 0:
            acc[:depth] = first
            acc[depth : depth + hidden] = second
            acc[depth + hidden : depth + hidden + classes] = third
        else:
            acc[:depth] += first
            acc[depth : depth + hidden] += second
            acc[depth + hidden : depth + hidden + classes] += third
    rest_rows = acc.shape[0] - (depth + hidden + classes)
    if rest_rows:
        acc[depth + hidden + classes :] = jnp.zeros((rest_rows, LANE), F32)
    halve(bit, acc, send, keep)


def halve(bit, acc, send, keep):
    rows = acc.shape[0] // 2
    up = lax.rem(lax.axis_index("owner") // bit, 2)
    send[...] = acc[pl.ds(pl.multiple_of((1 - up) * rows, 8), rows), :].astype(BF)
    keep[...] = acc[pl.ds(pl.multiple_of(up * rows, 8), rows), :]


def add_kernel(bit, kept, got, send, keep, acc):
    acc[...] = kept[...] + got[...].astype(F32)
    halve(bit, acc, send, keep)


def last_kernel(kept, got, out):
    out[...] = (kept[...] + got[...].astype(F32)).astype(BF)


def join_kernel(bit, mine, got, out):
    rows = mine.shape[0]
    up = lax.rem(lax.axis_index("owner") // bit, 2)
    out[pl.ds(pl.multiple_of(up * rows, ROW), rows), :] = mine[...]
    out[pl.ds(pl.multiple_of((1 - up) * rows, ROW), rows), :] = got[...]


def place_kernel(mine, across, core, both, first, second, third):
    side = lax.rem(lax.axis_index("owner"), 2)
    half = lax.axis_index("batch")
    depth, hidden, classes = first.shape[0], second.shape[0], third.shape[0]
    for ref, s, h in ((mine, side, half), (across, 1 - side, half), (core, side, 1 - half), (both, 1 - side, 1 - half)):
        cols = pl.ds(pl.multiple_of((2 * s + h) * LANE, LANE), LANE)
        first[:, cols] = ref[:depth]
        second[:, cols] = ref[depth : depth + hidden]
        third[:, cols] = ref[depth + hidden : depth + hidden + classes]


def whole(kernel, outs, scratch, *args, flops=1000000, limit=24):
    return pl.pallas_call(
        kernel,
        out_shape=[jax.ShapeDtypeStruct(shape, kind) for shape, kind in outs],
        in_specs=[pl.BlockSpec(memory_space=pltpu.VMEM)] * len(args),
        out_specs=[pl.BlockSpec(memory_space=pltpu.VMEM)] * len(outs),
        scratch_shapes=[pltpu.VMEM(shape, kind) for shape, kind in scratch],
        compiler_params=pltpu.CompilerParams(vmem_limit_bytes=limit << 20),
        cost_estimate=pl.CostEstimate(flops=flops, bytes_accessed=flops // 512, transcendentals=0),
    )(*args)


def body(features, w_first, w_second, w_third, nbr_ids, nbr_weight, labels):
    owners = lax.axis_size("owner")
    node_dev, depth = features.shape
    hidden, classes = w_third.shape
    rows, fanout = nbr_ids.shape
    nodes = owners * node_dev
    me = lax.axis_index("owner")
    core = lax.axis_index("batch")
    bits = [1 << i for i in range(1, owners.bit_length() - 1)]
    targets = owners * rows

    def over(x, bit):
        return lax.ppermute(x, "owner", [(i, i ^ bit) for i in range(owners)])

    def other_core(x):
        return lax.ppermute(x, "batch", [(0, 1), (1, 0)])

    w3t = w_third.T
    coded = nbr_ids.astype(F32) + (labels * nodes).astype(F32)[:, None]
    packed = jnp.concatenate([coded, nbr_weight], axis=1)
    got = other_core(packed)
    packed = jnp.where(core == 0, jnp.concatenate([packed, got], 1), jnp.concatenate([got, packed], 1))
    for bit in bits:
        got = over(packed, bit)
        up = (me // bit) % 2
        packed = jnp.where(up == 0, jnp.concatenate([packed, got], 0), jnp.concatenate([got, packed], 0))
    far_packed = over(packed, 1)

    kept = [
        ((node_dev, hidden), BF),
        ((node_dev, LANE), BF),
        ((node_dev, LANE), F32),
        ((node_dev, hidden), F32),
    ]
    wide = [((node_dev, hidden), F32)] * 2
    scores, h1, h2, s1, s2 = whole(
        own_kernel, [((classes, node_dev), BF)] + kept, wide, features, w_first, w_second, w3t
    )
    far_scores = over(scores, 1)
    half = node_dev // 2
    peer_half = over(lax.dynamic_slice_in_dim(features, core * half, half, 0), 1)
    peer_rest = other_core(peer_half)
    peer, ph1, ph2, ps1, ps2 = whole(
        peer_kernel, [((node_dev, depth), BF)] + kept, wide, peer_half, peer_rest, w_first, w_second
    )

    big = 24 if owners <= 8 else 56
    maps = [((2 * node_dev, targets), BF), ((2 * node_dev, targets), BF), ((1, targets), jnp.int32)]
    tables = [((fanout, targets), jnp.int32), ((fanout, targets), F32)]
    high, low, label, part, send = whole(
        functools.partial(logit_kernel, nodes),
        maps + [((classes, targets), F32), ((classes, targets), BF)],
        tables,
        packed,
        scores,
        far_scores,
        limit=big,
    )
    far_high, far_low, _ = whole(functools.partial(far_kernel, nodes), maps, tables, far_packed, limit=big)
    for bit in bits[:-1]:
        part = part + over(send, bit).astype(F32)
        send = part.astype(BF)
    grad, grad_send, loss = whole(
        softmax_kernel,
        [((classes, targets), F32), ((classes, targets), BF), ((1, targets), F32)],
        [],
        part,
        over(send, bits[-1]),
        label,
    )
    at = core * (targets // 2) + (me // 2) * rows
    target_loss = lax.dynamic_slice_in_dim(loss[0], at, rows, 0)
    far_grad = over(grad_send, 1)

    step = ROW << len(bits)
    stack = -(-(depth + hidden + classes) // step) * step

    def halves(n):
        return [((n // 2, LANE), BF), ((n // 2, LANE), F32)]

    send, keep = whole(
        functools.partial(back_kernel, bits[0]),
        halves(stack),
        [((stack, LANE), F32), ((node_dev, hidden), F32)],
        grad, far_grad, high, low, far_high, far_low,
        features, peer, h1, ph1, h2, ph2, s1, ps1, s2, ps2, w3t, w_second,
        limit=big,
    )
    size = stack // 2
    for at, bit in enumerate(bits[1:]):
        send, keep = whole(
            functools.partial(add_kernel, bit),
            halves(size),
            [((size, LANE), F32)],
            keep,
            over(send, bits[at]),
        )
        size //= 2
    (out,) = whole(last_kernel, [((size, LANE), BF)], [], keep, over(send, bits[-1]))
    for bit in reversed(bits):
        size *= 2
        (out,) = whole(functools.partial(join_kernel, bit), [((size, LANE), BF)], [], out, over(out, bit))
    across = over(out, 1)
    first, second, third = whole(
        place_kernel,
        [((depth, hidden), BF), ((hidden, hidden), BF), ((classes, hidden), BF)],
        [],
        out,
        across,
        other_core(out),
        other_core(across),
    )
    return first, second, third.T, target_loss


def solution(mesh):
    in_specs = (
        P("owner", None),
        P(),
        P(),
        P(),
        P(("groups", "owner", "batch"), None),
        P(("groups", "owner", "batch"), None),
        P(("groups", "owner", "batch")),
    )
    out_specs = (
        P("groups", None),
        P("groups", None),
        P("groups", None),
        P(("groups", "owner", "batch")),
    )
    return jax.shard_map(body, mesh=mesh, in_specs=in_specs, out_specs=out_specs, check_vma=False)
```

time: 149 us -> 84.8 us (0.57)
  blocking collectives: 88.4 us -> 0 us
  waiting for transfers between devices: 18.1 us -> 41.7 us
  Pallas kernels: 0 us -> 14.7 us
  matrix products: 13.2 us -> 0 us
  local copies, waits for them, and re-layouts: 18.3 us -> 8.3 us
  starting transfers between devices: 7.15 us -> 17 us
    psum x1 -> x0, blocking collectives: 74.9 us -> none  [body(): lax.psum((grad_first, grad_second, grad_third), ('owner', 'batch'))]
    ppermute x0 -> x17, waiting for transfers between devices: none -> 41.7 us  [the longest x13 39.4 us: over(): return lax.ppermute(x, 'owner', [(i, i ^ bit) for i in range(owners)])]
    all_to_all x2 -> x0, waiting for transfers between devices: 18.1 us -> none  [the longest x1 9.1 us: body(): lax.all_to_all(outgoing.reshape(owners, slots_per, classes), 'owner', spl...]
    ppermute x0 -> x17, starting transfers between devices: none -> 17 us  [the longest x13 17 us: over(): return lax.ppermute(x, 'owner', [(i, i ^ bit) for i in range(owners)])]
    pallas_call x0 -> x11, Pallas kernels: none -> 14.7 us  [whole(): pl.pallas_call(kernel, out_shape=[jax.ShapeDtypeStruct(shape, kind) for s...]
    all_to_all x1 -> x0, blocking collectives: 13.5 us -> none  [body(): lax.all_to_all(request.reshape(owners, slots_per), 'owner', split_axis=0,...]
    dot_general x7 -> x0, matrix products: 13.2 us -> none  [the longest x1 4.28 us: body(): jnp.einsum('rd,rh->dh', fetched, back_one, preferred_element_type=jnp.flo...]
    gather x2 -> x0, local copies, waits for them, and re-layouts: 7.66 us -> none  [the longest x1 5.71 us: body(): features[jnp.maximum(asked_rows, 0)]]
  transfers between devices with their start and end apart: 2 -> 17, of which waited for: 2 -> 11; matrix products, arithmetic and copies ran while one was open for 0% -> 3% of each run, Pallas kernels for 0% -> 12%
where the time goes in v1:
time: 84.8 us; the launch traced here: 84.3 us
  waiting for transfers between devices  41.7 us (49%)
  starting transfers between devices  17 us (20%)
  Pallas kernels  14.7 us (17%)
  local copies, waits for them, and re-layouts  8.3 us (10%)
  other arithmetic  1.82 us (2%)
    ppermute x13, waiting for transfers between devices, over(): return lax.ppermute(x, 'owner', [(i, i ^ bit) for i in range(owners)])  39.4 us
    ppermute x13, starting transfers between devices, over(): return lax.ppermute(x, 'owner', [(i, i ^ bit) for i in range(owners)])  17 us
    pallas_call x11, Pallas kernels, whole(): pl.pallas_call(kernel, out_shape=[jax.ShapeDtypeStruct(shape, kind) for s...  14.7 us
    unnamed x34, local copies, waits for them, and re-layouts  5.88 us
    ppermute x4, waiting for transfers between devices, other_core(): return lax.ppermute(x, 'batch', [(0, 1), (1, 0)])  2.27 us
    dynamic_slice x1, local copies, waits for them, and re-layouts, body(): lax.dynamic_slice_in_dim(features, core * half, half, 0)  1.84 us
  transfers between devices with their start and end apart: 17, of which 11 were waited for; matrix products, arithmetic and copies ran while one was open for 3% of the time, Pallas kernels for 12%

profile of v1, /device:TPU:0, one launch (start us, length us, event | category | flops | bytes accessed | tf_op | source)
XLA Modules:
  0.0 84.3 jit_solution(9685023186509219511)
XLA Ops:
  0.7 1.8 %constant_dynamic-slice_fusion = bf16[256,768]{1,0:T(8,128)(2,1)} fusion(bf16[512,768]{1,0:T(8,128)(2,1)} %x.3, s32[]{:T(128)S(6)} %select_n.59), kind=kLoop, calls=%fused_computation.8 | loop fusion | bytes 786436 | tf_op jit(solution)/shard_map/dynamic_slice | solution.py:257
  2.5 2.9 %collective-permute-start.8 = (bf16[256,768]{1,0:T(8,128)(2,1)}, bf16[256,768]{1,0:T(8,128)(2,1)S(1)}, u32[]{:S(2)}, u32[]{:S(2)}) collective-permute-start(bf16[256,768]{1,0:T(8,128)(2,1)} %constant_dynamic-slice_fusion), channel_id=1, source_target_pairs={{0,2},{2,0},{4,6},{6,4},{8,10},{10,8},{12,14},{14,12},{1,3},{3,1},... | collective-permute-start | bytes 1179656 | tf_op jit(solution)/shard_map/ppermute | solution.py:229
  6.3 1.2 %collective-permute-done = f32[16,64]{1,0:T(8,128)S(1)} collective-permute-done((f32[16,64]{1,0:T(8,128)S(1)}, f32[16,64]{1,0:T(8,128)S(1)}, u32[]{:S(2)}, u32[]{:S(2)}) %collective-permute-start) | collective-permute-done | bytes 4128 | tf_op jit(solution)/shard_map/ppermute | solution.py:232
  7.5 1.6 %collective-permute-start.1 = (f32[16,128]{1,0:T(8,128)S(1)}, f32[16,128]{1,0:T(8,128)}, u32[]{:S(2)}, u32[]{:S(2)}) collective-permute-start(f32[16,128]{1,0:T(8,128)S(1)} %maximum_select_fusion.2), channel_id=1, source_target_pairs={{0,4},{2,6},{4,0},{6,2},{8,12},{10,14},{12,8},{14,10},{1,5},{3,7},... | collective-permute-start | bytes 24584 | tf_op jit(solution)/shard_map/ppermute | solution.py:229
  12.2 2.4 %shard_map.102 = (bf16[153,512]{1,0:T(8,128)(2,1)}, bf16[512,512]{1,0:T(8,128)(2,1)S(1)}, bf16[512,128]{1,0:T(8,128)(2,1)S(1)}, f32[512,128]{1,0:T(8,128)S(1)}, f32[512,512]{1,0:T(8,128)S(1)}) custom-call(bf16[512,768]{1,0:T(8,128)(2,1)S(1)} %copy-done, bf16[768,512]{1,0:T(8,128)(2,1)S(1)} %copy-done.3, bf16[512,512]{1,0:T(8,128)(2,1)S(1)} %copy-done.1, ...), custom_call_target="tpu_custom_call" | custom-call | flops 1000000 | bytes 1953 | tf_op jit(solution)/shard_map/pallas_call | solution.py:206
  18.1 2.6 %collective-permute-start.2 = (f32[32,128]{1,0:T(8,128)S(1)}, f32[32,128]{1,0:T(8,128)}, u32[]{:S(2)}, u32[]{:S(2)}) collective-permute-start(f32[32,128]{1,0:T(8,128)S(1)} %maximum_select_fusion.1), channel_id=1, source_target_pairs={{0,8},{2,10},{4,12},{6,14},{8,0},{10,2},{12,4},{14,6},{1,9},{3,11}... | collective-permute-start | bytes 49160 | tf_op jit(solution)/shard_map/ppermute | solution.py:229
  20.7 2.2 %collective-permute-done.2 = f32[32,128]{1,0:T(8,128)} collective-permute-done((f32[32,128]{1,0:T(8,128)S(1)}, f32[32,128]{1,0:T(8,128)}, u32[]{:S(2)}, u32[]{:S(2)}) %collective-permute-start.2) | collective-permute-done | bytes 16416 | tf_op jit(solution)/shard_map/ppermute | solution.py:229
  23.6 3.4 %shard_map.103 = (bf16[1024,128]{1,0:T(8,128)(2,1)S(1)}, bf16[1024,128]{1,0:T(8,128)(2,1)S(1)}, s32[1,128]{1,0:T(1,128)S(1)}, f32[153,128]{1,0:T(8,128)S(1)}, bf16[153,128]{1,0:T(8,128)(2,1)S(1)}) custom-call(f32[64,128]{1,0:T(8,128)S(1)} %maximum_select_fusion.packed, bf16[153,512]{1,0:T(8,128)(2,1)} %get-tuple-element.31.mine, ...), custom_call_target="tpu_custom_call" | custom-call | flops 1000000 | bytes 1953 | tf_op jit(solution)/shard_map/pallas_call | solution.py:206
  27.2 3.9 %collective-permute-done.4 = bf16[153,128]{1,0:T(8,128)(2,1)S(1)} collective-permute-done((bf16[153,128]{1,0:T(8,128)(2,1)S(1)}, bf16[153,128]{1,0:T(8,128)(2,1)S(1)}, u32[]{:S(2)}, u32[]{:S(2)}) %collective-permute-start.4) | collective-permute-done | bytes 39200 | tf_op jit(solution)/shard_map/ppermute | solution.py:229
  31.1 2.6 %collective-permute-start.5 = (bf16[153,128]{1,0:T(8,128)(2,1)S(1)}, bf16[153,128]{1,0:T(8,128)(2,1)S(1)}, u32[]{:S(2)}, u32[]{:S(2)}) collective-permute-start(bf16[153,128]{1,0:T(8,128)(2,1)S(1)} %get-tuple-element.58), channel_id=1, source_target_pairs={{0,8},{2,10},{4,12},{6,14},{8,0},{10,2},{12,4},{14,6},{1,9},{3,11}... | collective-permute-start | bytes 117512 | tf_op jit(solution)/shard_map/ppermute | solution.py:229
  33.7 2.3 %collective-permute-done.5.got = bf16[153,128]{1,0:T(8,128)(2,1)S(1)} collective-permute-done((bf16[153,128]{1,0:T(8,128)(2,1)S(1)}, bf16[153,128]{1,0:T(8,128)(2,1)S(1)}, u32[]{:S(2)}, u32[]{:S(2)}) %collective-permute-start.5) | collective-permute-done | bytes 39200 | tf_op jit(solution)/shard_map/ppermute | solution.py:229
  36.1 1.9 %collective-permute-start.6 = (bf16[153,128]{1,0:T(8,128)(2,1)S(1)}, bf16[153,128]{1,0:T(8,128)(2,1)S(1)}, u32[]{:S(2)}, u32[]{:S(2)}) collective-permute-start(bf16[153,128]{1,0:T(8,128)(2,1)S(1)} %get-tuple-element.36), channel_id=1, source_target_pairs={{0,2},{2,0},{4,6},{6,4},{8,10},{10,8},{12,14},{14,12},{1,3},{3,1},... | collective-permute-start | bytes 117512 | tf_op jit(solution)/shard_map/ppermute | solution.py:229
  38.2 3.7 %collective-permute-done.7.packed = f32[64,128]{1,0:T(8,128)S(1)} collective-permute-done((f32[64,128]{1,0:T(8,128)S(1)}, f32[64,128]{1,0:T(8,128)S(1)}, u32[]{:S(2)}, u32[]{:S(2)}) %collective-permute-start.7) | collective-permute-done | bytes 32800 | tf_op jit(solution)/shard_map/ppermute | solution.py:229
  41.9 2.4 %shard_map.105 = (bf16[1024,128]{1,0:T(8,128)(2,1)S(1)}, bf16[1024,128]{1,0:T(8,128)(2,1)S(1)}, s32[1,128]{1,0:T(1,128)}) custom-call(f32[64,128]{1,0:T(8,128)S(1)} %collective-permute-done.7.packed), custom_call_target="tpu_custom_call" | custom-call | flops 1000000 | bytes 1953 | tf_op jit(solution)/shard_map/pallas_call | solution.py:206
  44.4 1.6 %shard_map.106 = (bf16[512,768]{1,0:T(8,128)(2,1)S(1)}, bf16[512,512]{1,0:T(8,128)(2,1)S(1)}, bf16[512,128]{1,0:T(8,128)(2,1)S(1)}, f32[512,128]{1,0:T(8,128)S(1)}, f32[512,512]{1,0:T(8,128)S(1)}) custom-call(bf16[256,768]{1,0:T(8,128)(2,1)S(1)} %collective-permute-done.8.mine, bf16[256,768]{1,0:T(8,128)(2,1)S(1)} %collective-permute-done.9.theirs, ...), custom_call_target="tpu_custom_call" | custom-call | flops 1000000 | bytes 1953 | tf_op jit(solution)/shard_map/pallas_call | solution.py:206
  46.0 3.4 %shard_map.107 = (bf16[736,128]{1,0:T(8,128)(2,1)S(1)}, f32[736,128]{1,0:T(8,128)S(1)}) custom-call(f32[153,128]{1,0:T(8,128)S(1)} %get-tuple-element.35.grad, bf16[153,128]{1,0:T(8,128)(2,1)S(1)} %collective-permute-done.6.far_grad, bf16[1024,128]{1,0:T(8,128)(2,1)S(1)} %get-tuple-element.37.high, bf16[1024,128]{1,0:T(8,128)(2,1)S(1)} %get-tuple-element.38.low, ...), custom_call_target="tpu_custom_call" | custom-call | flops 1000000 | bytes 1953 | tf_op jit(solution)/shard_map/pallas_call | solution.py:206
  49.6 6.4 %collective-permute-done.10.got = bf16[736,128]{1,0:T(8,128)(2,1)S(1)} collective-permute-done((bf16[736,128]{1,0:T(8,128)(2,1)S(1)}, bf16[736,128]{1,0:T(8,128)(2,1)S(1)}, u32[]{:S(2)}, u32[]{:S(2)}) %collective-permute-start.10) | collective-permute-done | bytes 188448 | tf_op jit(solution)/shard_map/ppermute | solution.py:229
  56.1 1.6 %collective-permute-start.11 = (bf16[368,128]{1,0:T(8,128)(2,1)S(1)}, bf16[368,128]{1,0:T(8,128)(2,1)S(1)}, u32[]{:S(2)}, u32[]{:S(2)}) collective-permute-start(bf16[368,128]{1,0:T(8,128)(2,1)S(1)} %get-tuple-element.53), channel_id=1, source_target_pairs={{0,8},{2,10},{4,12},{6,14},{8,0},{10,2},{12,4},{14,6},{1,9},{3,11}... | collective-permute-start | bytes 282632 | tf_op jit(solution)/shard_map/ppermute | solution.py:229
  57.6 4.7 %collective-permute-done.11.got = bf16[368,128]{1,0:T(8,128)(2,1)S(1)} collective-permute-done((bf16[368,128]{1,0:T(8,128)(2,1)S(1)}, bf16[368,128]{1,0:T(8,128)(2,1)S(1)}, u32[]{:S(2)}, u32[]{:S(2)}) %collective-permute-start.11) | collective-permute-done | bytes 94240 | tf_op jit(solution)/shard_map/ppermute | solution.py:229
  62.4 1.5 %collective-permute-start.12 = (bf16[368,128]{1,0:T(8,128)(2,1)S(1)}, bf16[368,128]{1,0:T(8,128)(2,1)S(1)}, u32[]{:S(2)}, u32[]{:S(2)}) collective-permute-start(bf16[368,128]{1,0:T(8,128)(2,1)S(1)} %shard_map.109.mine), channel_id=1, source_target_pairs={{0,8},{2,10},{4,12},{6,14},{8,0},{10,2},{12,4},{14,6},{1,9},{3,11}... | collective-permute-start | bytes 282632 | tf_op jit(solution)/shard_map/ppermute | solution.py:229
  63.9 4.0 %collective-permute-done.12.got = bf16[368,128]{1,0:T(8,128)(2,1)S(1)} collective-permute-done((bf16[368,128]{1,0:T(8,128)(2,1)S(1)}, bf16[368,128]{1,0:T(8,128)(2,1)S(1)}, u32[]{:S(2)}, u32[]{:S(2)}) %collective-permute-start.12) | collective-permute-done | bytes 94240 | tf_op jit(solution)/shard_map/ppermute | solution.py:229
  68.1 5.6 %collective-permute-done.13.got = bf16[736,128]{1,0:T(8,128)(2,1)S(1)} collective-permute-done((bf16[736,128]{1,0:T(8,128)(2,1)S(1)}, bf16[736,128]{1,0:T(8,128)(2,1)S(1)}, u32[]{:S(2)}, u32[]{:S(2)}) %collective-permute-start.13) | collective-permute-done | bytes 188448 | tf_op jit(solution)/shard_map/ppermute | solution.py:229
  74.7 6.6 %collective-permute-done.14.across = bf16[1472,128]{1,0:T(8,128)(2,1)S(1)} collective-permute-done((bf16[1472,128]{1,0:T(8,128)(2,1)S(1)}, bf16[1472,128]{1,0:T(8,128)(2,1)S(1)}, u32[]{:S(2)}, u32[]{:S(2)}) %collective-permute-start.14) | collective-permute-done | bytes 376864 | tf_op jit(solution)/shard_map/ppermute | solution.py:229
  83.1 1.3 %shard_map.112 = (bf16[768,512]{1,0:T(8,128)(2,1)}, bf16[512,512]{1,0:T(8,128)(2,1)}, bf16[153,512]{1,0:T(8,128)(2,1)}) custom-call(bf16[1472,128]{1,0:T(8,128)(2,1)S(1)} %shard_map.111.mine, bf16[1472,128]{1,0:T(8,128)(2,1)S(1)} %collective-permute-done.14.across, bf16[1472,128]{1,0:T(8,128)(2,1)S(1)} %collective-permute-done.15.core, ...), custom_call_target="tpu_custom_call" | custom-call | flops 1000000 | bytes 1953 | tf_op jit(solution)/shard_map/pallas_call | solution.py:206
  (64 shorter events, 11.9 us)
Async XLA Ops:
  0.6 8.5 %copy-start = (bf16[512,768]{1,0:T(8,128)(2,1)S(1)}, bf16[512,768]{1,0:T(8,128)(2,1)}, u32[]{:S(2)}) copy-start(bf16[512,768]{1,0:T(8,128)(2,1)} %x.3) | copy-start | bytes 2359300
  0.6 4.8 %copy-start.16 = (s32[16]{0:T(128)S(1)}, s32[16]{0:T(128)}, u32[]{:S(2)}) copy-start(s32[16]{0:T(128)} %param.13) | copy-start | bytes 196
  0.7 4.8 %copy-start.15 = (s32[16,32]{1,0:T(8,128)S(1)}, s32[16,32]{1,0:T(8,128)}, u32[]{:S(2)}) copy-start(s32[16,32]{1,0:T(8,128)} %param.11) | copy-start | bytes 6148
  2.5 18.2 %collective-permute-start.8 = (bf16[256,768]{1,0:T(8,128)(2,1)}, bf16[256,768]{1,0:T(8,128)(2,1)S(1)}, u32[]{:S(2)}, u32[]{:S(2)}) collective-permute-start(bf16[256,768]{1,0:T(8,128)(2,1)} %constant_dynamic-slice_fusion), channel_id=1, source_target_pairs={{0,2},{2,0},{4,6},{6,4},{8,10},{10,8},{12,14},{14,12},{1,3},{3,1},... | collective-permute-start | bytes 1179656 | tf_op jit(solution)/shard_map/ppermute | solution.py:229
  6.2 1.2 %collective-permute-start = (f32[16,64]{1,0:T(8,128)S(1)}, f32[16,64]{1,0:T(8,128)S(1)}, u32[]{:S(2)}, u32[]{:S(2)}) collective-permute-start(f32[16,64]{1,0:T(8,128)S(1)} %pad_maximum_fusion), channel_id=1, source_target_pairs={{0,1},{1,0},{2,3},{3,2},{4,5},{5,4},{6,7},{7,6},{8,9},{9,8},{10,11... | collective-permute-start | bytes 12296 | tf_op jit(solution)/shard_map/ppermute | solution.py:232
  7.5 7.1 %copy-start.14 = (f32[16,128]{1,0:T(8,128)}, f32[16,128]{1,0:T(8,128)S(1)}, u32[]{:S(2)}) copy-start(f32[16,128]{1,0:T(8,128)S(1)} %maximum_select_fusion.2) | copy-start | bytes 24580
  7.5 9.8 %collective-permute-start.1 = (f32[16,128]{1,0:T(8,128)S(1)}, f32[16,128]{1,0:T(8,128)}, u32[]{:S(2)}, u32[]{:S(2)}) collective-permute-start(f32[16,128]{1,0:T(8,128)S(1)} %maximum_select_fusion.2), channel_id=1, source_target_pairs={{0,4},{2,6},{4,0},{6,2},{8,12},{10,14},{12,8},{14,10},{1,5},{3,7},... | collective-permute-start | bytes 24584 | tf_op jit(solution)/shard_map/ppermute | solution.py:229
  12.2 32.2 %copy-start.4 = (bf16[768,512]{1,0:T(8,128)(2,1)S(1)}, bf16[768,512]{1,0:T(8,128)(2,1)}, u32[]{:S(2)}) copy-start(bf16[768,512]{1,0:T(8,128)(2,1)} %w_first.3) | copy-start | bytes 2359300
  16.7 27.6 %copy-start.2 = (bf16[512,512]{1,0:T(8,128)(2,1)S(1)}, bf16[512,512]{1,0:T(8,128)(2,1)}, u32[]{:S(2)}) copy-start(bf16[512,512]{1,0:T(8,128)(2,1)} %w2.1) | copy-start | bytes 1572868
  16.7 6.9 %collective-permute-start.3 = (bf16[153,512]{1,0:T(8,128)(2,1)}, bf16[153,512]{1,0:T(8,128)(2,1)}, u32[]{:S(2)}, u32[]{:S(2)}) collective-permute-start(bf16[153,512]{1,0:T(8,128)(2,1)} %get-tuple-element.31.mine), channel_id=1, source_target_pairs={{0,2},{2,0},{4,6},{6,4},{8,10},{10,8},{12,14},{14,12},{1,3},{3,1},... | collective-permute-start | bytes 470024 | tf_op jit(solution)/shard_map/ppermute | solution.py:229
  18.1 4.7 %collective-permute-start.2 = (f32[32,128]{1,0:T(8,128)S(1)}, f32[32,128]{1,0:T(8,128)}, u32[]{:S(2)}, u32[]{:S(2)}) collective-permute-start(f32[32,128]{1,0:T(8,128)S(1)} %maximum_select_fusion.1), channel_id=1, source_target_pairs={{0,8},{2,10},{4,12},{6,14},{8,0},{10,2},{12,4},{14,6},{1,9},{3,11}... | collective-permute-start | bytes 49160 | tf_op jit(solution)/shard_map/ppermute | solution.py:229
  20.7 23.7 %collective-permute-start.9 = (bf16[256,768]{1,0:T(8,128)(2,1)S(1)}, bf16[256,768]{1,0:T(8,128)(2,1)S(1)}, u32[]{:S(2)}, u32[]{:S(2)}) collective-permute-start(bf16[256,768]{1,0:T(8,128)(2,1)S(1)} %collective-permute-done.8.mine), channel_id=1, source_target_pairs={{0,1},{1,0},{2,3},{3,2},{4,5},{5,4},{6,7},{7,6},{8,9},{9,8},{10,11... | collective-permute-start | bytes 1179656 | tf_op jit(solution)/shard_map/ppermute | solution.py:232
  27.0 4.1 %collective-permute-start.4 = (bf16[153,128]{1,0:T(8,128)(2,1)S(1)}, bf16[153,128]{1,0:T(8,128)(2,1)S(1)}, u32[]{:S(2)}, u32[]{:S(2)}) collective-permute-start(bf16[153,128]{1,0:T(8,128)(2,1)S(1)} %get-tuple-element.33), channel_id=1, source_target_pairs={{0,4},{2,6},{4,0},{6,2},{8,12},{10,14},{12,8},{14,10},{1,5},{3,7},... | collective-permute-start | bytes 117512 | tf_op jit(solution)/shard_map/ppermute | solution.py:229
  31.1 5.0 %collective-permute-start.5 = (bf16[153,128]{1,0:T(8,128)(2,1)S(1)}, bf16[153,128]{1,0:T(8,128)(2,1)S(1)}, u32[]{:S(2)}, u32[]{:S(2)}) collective-permute-start(bf16[153,128]{1,0:T(8,128)(2,1)S(1)} %get-tuple-element.58), channel_id=1, source_target_pairs={{0,8},{2,10},{4,12},{6,14},{8,0},{10,2},{12,4},{14,6},{1,9},{3,11}... | collective-permute-start | bytes 117512 | tf_op jit(solution)/shard_map/ppermute | solution.py:229
  36.1 9.9 %collective-permute-start.6 = (bf16[153,128]{1,0:T(8,128)(2,1)S(1)}, bf16[153,128]{1,0:T(8,128)(2,1)S(1)}, u32[]{:S(2)}, u32[]{:S(2)}) collective-permute-start(bf16[153,128]{1,0:T(8,128)(2,1)S(1)} %get-tuple-element.36), channel_id=1, source_target_pairs={{0,2},{2,0},{4,6},{6,4},{8,10},{10,8},{12,14},{14,12},{1,3},{3,1},... | collective-permute-start | bytes 117512 | tf_op jit(solution)/shard_map/ppermute | solution.py:229
  38.0 3.9 %collective-permute-start.7 = (f32[64,128]{1,0:T(8,128)S(1)}, f32[64,128]{1,0:T(8,128)S(1)}, u32[]{:S(2)}, u32[]{:S(2)}) collective-permute-start(f32[64,128]{1,0:T(8,128)S(1)} %maximum_select_fusion.packed), channel_id=1, source_target_pairs={{0,2},{2,0},{4,6},{6,4},{8,10},{10,8},{12,14},{14,12},{1,3},{3,1},... | collective-permute-start | bytes 98312 | tf_op jit(solution)/shard_map/ppermute | solution.py:229
  44.3 1.7 %copy-start.12 = (bf16[512,128]{1,0:T(8,128)(2,1)S(1)}, bf16[512,128]{1,0:T(8,128)(2,1)}, u32[]{:S(2)}) copy-start(bf16[512,128]{1,0:T(8,128)(2,1)} %copy-done.11) | copy-start | bytes 393220
  49.4 6.6 %collective-permute-start.10 = (bf16[736,128]{1,0:T(8,128)(2,1)S(1)}, bf16[736,128]{1,0:T(8,128)(2,1)S(1)}, u32[]{:S(2)}, u32[]{:S(2)}) collective-permute-start(bf16[736,128]{1,0:T(8,128)(2,1)S(1)} %get-tuple-element.51), channel_id=1, source_target_pairs={{0,4},{2,6},{4,0},{6,2},{8,12},{10,14},{12,8},{14,10},{1,5},{3,7},... | collective-permute-start | bytes 565256 | tf_op jit(solution)/shard_map/ppermute | solution.py:229
  56.1 6.3 %collective-permute-start.11 = (bf16[368,128]{1,0:T(8,128)(2,1)S(1)}, bf16[368,128]{1,0:T(8,128)(2,1)S(1)}, u32[]{:S(2)}, u32[]{:S(2)}) collective-permute-start(bf16[368,128]{1,0:T(8,128)(2,1)S(1)} %get-tuple-element.53), channel_id=1, source_target_pairs={{0,8},{2,10},{4,12},{6,14},{8,0},{10,2},{12,4},{14,6},{1,9},{3,11}... | collective-permute-start | bytes 282632 | tf_op jit(solution)/shard_map/ppermute | solution.py:229
  62.4 5.5 %collective-permute-start.12 = (bf16[368,128]{1,0:T(8,128)(2,1)S(1)}, bf16[368,128]{1,0:T(8,128)(2,1)S(1)}, u32[]{:S(2)}, u32[]{:S(2)}) collective-permute-start(bf16[368,128]{1,0:T(8,128)(2,1)S(1)} %shard_map.109.mine), channel_id=1, source_target_pairs={{0,8},{2,10},{4,12},{6,14},{8,0},{10,2},{12,4},{14,6},{1,9},{3,11}... | collective-permute-start | bytes 282632 | tf_op jit(solution)/shard_map/ppermute | solution.py:229
  68.0 5.6 %collective-permute-start.13 = (bf16[736,128]{1,0:T(8,128)(2,1)S(1)}, bf16[736,128]{1,0:T(8,128)(2,1)S(1)}, u32[]{:S(2)}, u32[]{:S(2)}) collective-permute-start(bf16[736,128]{1,0:T(8,128)(2,1)S(1)} %shard_map.110.mine), channel_id=1, source_target_pairs={{0,4},{2,6},{4,0},{6,2},{8,12},{10,14},{12,8},{14,10},{1,5},{3,7},... | collective-permute-start | bytes 565256 | tf_op jit(solution)/shard_map/ppermute | solution.py:229
  73.7 7.7 %collective-permute-start.14 = (bf16[1472,128]{1,0:T(8,128)(2,1)S(1)}, bf16[1472,128]{1,0:T(8,128)(2,1)S(1)}, u32[]{:S(2)}, u32[]{:S(2)}) collective-permute-start(bf16[1472,128]{1,0:T(8,128)(2,1)S(1)} %shard_map.111.mine), channel_id=1, source_target_pairs={{0,2},{2,0},{4,6},{6,4},{8,10},{10,8},{12,14},{14,12},{1,3},{3,1},... | collective-permute-start | bytes 1130504 | tf_op jit(solution)/shard_map/ppermute | solution.py:229
  74.7 7.2 %collective-permute-start.15 = (bf16[1472,128]{1,0:T(8,128)(2,1)S(1)}, bf16[1472,128]{1,0:T(8,128)(2,1)S(1)}, u32[]{:S(2)}, u32[]{:S(2)}) collective-permute-start(bf16[1472,128]{1,0:T(8,128)(2,1)S(1)} %shard_map.111.mine), channel_id=1, source_target_pairs={{0,1},{1,0},{2,3},{3,2},{4,5},{5,4},{6,7},{7,6},{8,9},{9,8},{10,11... | collective-permute-start | bytes 1130504 | tf_op jit(solution)/shard_map/ppermute | solution.py:232
  81.4 1.7 %collective-permute-start.16 = (bf16[1472,128]{1,0:T(8,128)(2,1)S(1)}, bf16[1472,128]{1,0:T(8,128)(2,1)S(1)}, u32[]{:S(2)}, u32[]{:S(2)}) collective-permute-start(bf16[1472,128]{1,0:T(8,128)(2,1)S(1)} %collective-permute-done.14.across), channel_id=1, source_target_pairs={{0,1},{1,0},{2,3},{3,2},{4,5},{5,4},{6,7},{7,6},{8,9},{9,8},{10,11... | collective-permute-start | bytes 1130504 | tf_op jit(solution)/shard_map/ppermute | solution.py:232
  (10 other events, 10.9 us)

commit v2 on v1

--- a/solution.py
+++ b/solution.py
@@ -20,10 +20,6 @@
     return lax.dot_general(a, b, (((1,), (1,)), ((), ())), preferred_element_type=F32)
 
 
-def tn(a, b):
-    return lax.dot_general(a, b, (((0,), (0,)), ((), ())), preferred_element_type=F32)
-
-
 def split(v):
     high = v.astype(BF)
     return high, (v - high.astype(F32)).astype(BF)
@@ -34,34 +30,66 @@
     return pl.multiple_of(place * LANE, LANE)
 
 
-def layers(rows, w_first, w_second, h1, h2, s1, s2, one, two):
-    pre = nn(rows, w_first)
+def activate(pre):
     sigma = 1.0 / (1.0 + jnp.exp(-pre))
-    hidden = (pre * sigma).astype(BF)
-    h1[...] = hidden
-    one[...] = sigma * (1.0 + pre * (1.0 - sigma))
-    pre = nn(hidden, w_second)
-    sigma = 1.0 / (1.0 + jnp.exp(-pre))
-    hidden = (pre * sigma).astype(BF)
-    two[...] = hidden.astype(F32)
-    s2[...] = sigma * (1.0 + pre * (1.0 - sigma))
+    return (pre * sigma).astype(BF), sigma * (1.0 + pre * (1.0 - sigma))
+
+
+def launch(sem, pairs):
+    copies = [pltpu.make_async_copy(a, b, sem.at[i]) for i, (a, b) in enumerate(pairs)]
+    for c in copies:
+        c.start()
+    return copies
+
+
+def pack_kernel(nodes, ids, wts, labels, out):
+    rows, fanout = ids.shape
+    shape = (rows, rows)
+    same = lax.broadcasted_iota(jnp.int32, shape, 0) == lax.broadcasted_iota(jnp.int32, shape, 1)
+    label = jnp.sum(jnp.where(same, labels[...].astype(F32), 0.0), axis=1, keepdims=True)
+    out[:, :fanout] = ids[...].astype(F32) + label * nodes
+    out[:, fanout:] = wts[...]
+
+
+def own_kernel(x_hbm, w1_hbm, w2_hbm, w3_hbm, after, scores, half, x, w1, w2, w3, sem):
+    del after
+    into = launch(sem, ((x_hbm, x), (w1_hbm, w1), (w2_hbm, w2), (w3_hbm, w3)))
+    into[0].wait()
+    rows = half.shape[0]
+    half[...] = x[pl.ds(pl.multiple_of(lax.axis_index("batch") * rows, ROW), rows), :]
+    into[1].wait()
+    hidden = activate(nn(x[...], w1[...]))[0]
+    into[2].wait()
+    hidden = activate(nn(hidden, w2[...]))[0]
+    into[3].wait()
+    scores[...] = nt(w3[...], hidden).astype(BF)
+
+
+def layers(x, w1, w2, xt, h1t, h2, s1, s2, one, two):
     cols = pl.ds(device_slice(), LANE)
+    rows = x[...]
+    xt[...] = rows.T
+    hidden, slope = activate(nn(rows, w1[...]))
+    h1t[...] = hidden.T
+    one[...] = slope
     s1[...] = one[:, cols]
-    h2[...] = two[:, cols].astype(BF)
-    return hidden
-
-
-def own_kernel(x, w_first, w_second, w3t, scores, h1, h2, s1, s2, one, two):
-    hidden = layers(x[...], w_first[...], w_second[...], h1, h2, s1, s2, one, two)
-    scores[...] = nt(w3t[...], hidden).astype(BF)
-
-
-def peer_kernel(mine, theirs, w_first, w_second, x, h1, h2, s1, s2, one, two):
+    hidden, slope = activate(nn(hidden, w2[...]))
+    two[...] = hidden
+    s2[...] = slope
+    h2[...] = two[:, cols]
+
+
+def again_kernel(x, w1, w2, after, xt, h1t, h2, s1, s2, one, two):
+    del after
+    layers(x, w1, w2, xt, h1t, h2, s1, s2, one, two)
+
+
+def peer_kernel(mine, theirs, w1, w2, xt, h1t, h2, s1, s2, x, one, two):
     half = mine.shape[0]
     core = lax.axis_index("batch")
     x[pl.ds(pl.multiple_of(core * half, half), half), :] = mine[...]
     x[pl.ds(pl.multiple_of((1 - core) * half, half), half), :] = theirs[...]
-    layers(x[...], w_first[...], w_second[...], h1, h2, s1, s2, one, two)
+    layers(x, w1, w2, xt, h1t, h2, s1, s2, one, two)
 
 
 def spread(nodes, packed, high, low, label, ids, wts):
@@ -107,8 +135,7 @@
     lax.fori_loop(0, 2 * per_side, step, 0)
 
 
-def logit_kernel(nodes, packed, mine, theirs, high, low, label, part, send, ids, wts):
-    spread(nodes, packed, high, low, label, ids, wts)
+def logit_kernel(mine, theirs, high, low, part, send):
     n = mine.shape[1]
     total = nn(mine[...], high[:n]) + nn(mine[...], low[:n])
     total += nn(theirs[...], high[n:]) + nn(theirs[...], low[n:])
@@ -116,7 +143,7 @@
     send[...] = total.astype(BF)
 
 
-def far_kernel(nodes, packed, high, low, label, ids, wts):
+def spread_kernel(nodes, packed, high, low, label, ids, wts):
     spread(nodes, packed, high, low, label, ids, wts)
 
 
@@ -132,16 +159,15 @@
     send[...] = g.astype(BF)
 
 
-def back_kernel(bit, grad, far_grad, high, low, far_high, far_low, x, px, h1, ph1, h2, ph2, s1, ps1, s2, ps2, w3t, w2, send, keep, acc, two):
+def back_kernel(bit, grad, far_grad, high, low, far_high, far_low, xt, pxt, h1t, ph1t, h2, ph2, s1, ps1, s2, ps2, w3t, w2, send, keep, acc, two):
     top, rest = split(grad[...])
     far = far_grad[...]
-    n = x.shape[0]
-    depth = x.shape[1]
-    hidden = h1.shape[1]
+    depth, n = xt.shape
+    hidden = h1t.shape[0]
     classes = w3t.shape[0]
     cols = pl.ds(device_slice(), LANE)
     w2_rows = w2[cols, :]
-    for side, (x_, h1_, h2_, s1_, s2_) in enumerate(((x, h1, h2, s1, s2), (px, ph1, ph2, ps1, ps2))):
+    for side, (x_, h1_, h2_, s1_, s2_) in enumerate(((xt, h1t, h2, s1, s2), (pxt, ph1t, ph2, ps1, ps2))):
         at = slice(side * n, (side + 1) * n)
         hi, lo, fhi, flo = high[at], low[at], far_high[at], far_low[at]
         g = nt(hi, top) + nt(lo, top) + nt(hi, rest) + nt(fhi, far) + nt(flo, far)
@@ -151,8 +177,8 @@
         b2 = b2.astype(BF)
         b2_cols = two[:, cols].astype(BF)
         b1 = (nt(b2, w2_rows) * s1_[...]).astype(BF)
-        first = tn(x_[...], b1)
-        second = tn(h1_[...], b2_cols)
+        first = nn(x_[...], b1)
+        second = nn(h1_[...], b2_cols)
         third = nn(gt.astype(BF), h2_[...])
         if side == 0:
             acc[:depth] = first
@@ -191,24 +217,47 @@
     out[pl.ds(pl.multiple_of((1 - up) * rows, ROW), rows), :] = got[...]
 
 
-def place_kernel(mine, across, core, both, first, second, third):
-    side = lax.rem(lax.axis_index("owner"), 2)
-    half = lax.axis_index("batch")
-    depth, hidden, classes = first.shape[0], second.shape[0], third.shape[0]
-    for ref, s, h in ((mine, side, half), (across, 1 - side, half), (core, side, 1 - half), (both, 1 - side, 1 - half)):
-        cols = pl.ds(pl.multiple_of((2 * s + h) * LANE, LANE), LANE)
-        first[:, cols] = ref[:depth]
-        second[:, cols] = ref[depth : depth + hidden]
-        third[:, cols] = ref[depth + hidden : depth + hidden + classes]
-
-
-def whole(kernel, outs, scratch, *args, flops=1000000, limit=24):
+def place_kernel(bit, *refs):
+    halves, outs = refs[:8], refs[8:]
+    me = lax.axis_index("owner")
+    side = lax.rem(me, 2)
+    core = lax.axis_index("batch")
+    up = lax.rem(me // bit, 2)
+    rows = halves[0].shape[0]
+
+    def fill(order):
+        for i, (s, h) in enumerate(((side, core), (1 - side, core), (side, 1 - core), (1 - side, 1 - core))):
+            cols = pl.ds(pl.multiple_of((2 * s + h) * LANE, LANE), LANE)
+            for j in range(2):
+                ref = halves[2 * i + order[j]]
+                top = 0
+                for out in outs:
+                    low, high = max(top, j * rows), min(top + out.shape[0], (j + 1) * rows)
+                    if low < high:
+                        out[low - top : high - top, cols] = ref[low - j * rows : high - j * rows]
+                    top += out.shape[0]
+
+    @pl.when(up == 0)
+    def _():
+        fill((0, 1))
+
+    @pl.when(up == 1)
+    def _():
+        fill((1, 0))
+
+
+def whole(kernel, outs, scratch, *args, flops=1000000, limit=24, far_in=(), far_out=()):
+    def spec(i, far):
+        return pl.BlockSpec(memory_space=pltpu.HBM if i in far else pltpu.VMEM)
+
     return pl.pallas_call(
         kernel,
         out_shape=[jax.ShapeDtypeStruct(shape, kind) for shape, kind in outs],
-        in_specs=[pl.BlockSpec(memory_space=pltpu.VMEM)] * len(args),
-        out_specs=[pl.BlockSpec(memory_space=pltpu.VMEM)] * len(outs),
-        scratch_shapes=[pltpu.VMEM(shape, kind) for shape, kind in scratch],
+        in_specs=[spec(i, far_in) for i in range(len(args))],
+        out_specs=[spec(i, far_out) for i in range(len(outs))],
+        scratch_shapes=[
+            pltpu.SemaphoreType.DMA((s,)) if isinstance(s, int) else pltpu.VMEM(*s) for s in scratch
+        ],
         compiler_params=pltpu.CompilerParams(vmem_limit_bytes=limit << 20),
         cost_estimate=pl.CostEstimate(flops=flops, bytes_accessed=flops // 512, transcendentals=0),
     )(*args)
@@ -232,56 +281,95 @@
         return lax.ppermute(x, "batch", [(0, 1), (1, 0)])
 
     w3t = w_third.T
-    coded = nbr_ids.astype(F32) + (labels * nodes).astype(F32)[:, None]
-    packed = jnp.concatenate([coded, nbr_weight], axis=1)
+    (packed,) = whole(
+        functools.partial(pack_kernel, nodes),
+        [((rows, 2 * fanout), F32)],
+        [],
+        nbr_ids,
+        nbr_weight,
+        labels.reshape(1, rows),
+    )
     got = other_core(packed)
     packed = jnp.where(core == 0, jnp.concatenate([packed, got], 1), jnp.concatenate([got, packed], 1))
+    half = node_dev // 2
+    w1_type, w2_type, x_type = (w_first.shape, BF), (w_second.shape, BF), (features.shape, BF)
+    scores, my_half = whole(
+        own_kernel,
+        [((classes, node_dev), BF), ((half, depth), BF)],
+        [x_type, w1_type, w2_type, (w3t.shape, BF), 4],
+        features,
+        w_first,
+        w_second,
+        w3t,
+        packed,
+        flops=2000000000,
+        limit=60,
+        far_in=range(5),
+    )
     for bit in bits:
         got = over(packed, bit)
+        if bit == bits[0]:
+            got, scores = lax.optimization_barrier((got, scores))
         up = (me // bit) % 2
         packed = jnp.where(up == 0, jnp.concatenate([packed, got], 0), jnp.concatenate([got, packed], 0))
     far_packed = over(packed, 1)
-
+    far_scores = over(scores, 1)
+    my_half, packed = lax.optimization_barrier((my_half, packed))
+    peer_half = over(my_half, 1)
+
+    big = 24 if owners <= 8 else 48
+    maps = [((2 * node_dev, targets), BF), ((2 * node_dev, targets), BF), ((1, targets), jnp.int32)]
+    tables = [((fanout, targets), jnp.int32), ((fanout, targets), F32)]
+    spread_call = functools.partial(whole, functools.partial(spread_kernel, nodes), maps, tables, limit=big, flops=1000000000)
+    high, low, label = spread_call(packed)
+    part, send = whole(
+        logit_kernel,
+        [((classes, targets), F32), ((classes, targets), BF)],
+        [],
+        scores,
+        far_scores,
+        high,
+        low,
+        limit=big,
+    )
+    far_high, far_low, _ = spread_call(far_packed)
+    for bit in bits[:-1]:
+        got = over(send, bit)
+        if bit == bits[0]:
+            got, far_high, far_low = lax.optimization_barrier((got, far_high, far_low))
+        part = part + got.astype(F32)
+        send = part.astype(BF)
     kept = [
-        ((node_dev, hidden), BF),
+        ((depth, node_dev), BF),
+        ((hidden, node_dev), BF),
         ((node_dev, LANE), BF),
         ((node_dev, LANE), F32),
         ((node_dev, hidden), F32),
     ]
-    wide = [((node_dev, hidden), F32)] * 2
-    scores, h1, h2, s1, s2 = whole(
-        own_kernel, [((classes, node_dev), BF)] + kept, wide, features, w_first, w_second, w3t
-    )
-    far_scores = over(scores, 1)
-    half = node_dev // 2
-    peer_half = over(lax.dynamic_slice_in_dim(features, core * half, half, 0), 1)
+    work = [((node_dev, hidden), F32), ((node_dev, hidden), BF)]
+    xt, h1t, h2, s1, s2 = whole(
+        again_kernel, kept, work, features, w_first, w_second, send, flops=2000000000, far_in=(3,)
+    )
+    got = over(send, bits[-1])
+    peer_half = lax.optimization_barrier((peer_half, got))[0]
     peer_rest = other_core(peer_half)
-    peer, ph1, ph2, ps1, ps2 = whole(
-        peer_kernel, [((node_dev, depth), BF)] + kept, wide, peer_half, peer_rest, w_first, w_second
-    )
-
-    big = 24 if owners <= 8 else 56
-    maps = [((2 * node_dev, targets), BF), ((2 * node_dev, targets), BF), ((1, targets), jnp.int32)]
-    tables = [((fanout, targets), jnp.int32), ((fanout, targets), F32)]
-    high, low, label, part, send = whole(
-        functools.partial(logit_kernel, nodes),
-        maps + [((classes, targets), F32), ((classes, targets), BF)],
-        tables,
-        packed,
-        scores,
-        far_scores,
-        limit=big,
-    )
-    far_high, far_low, _ = whole(functools.partial(far_kernel, nodes), maps, tables, far_packed, limit=big)
-    for bit in bits[:-1]:
-        part = part + over(send, bit).astype(F32)
-        send = part.astype(BF)
+    pxt, ph1t, ph2, ps1, ps2 = whole(
+        peer_kernel,
+        kept,
+        [x_type] + work,
+        peer_half,
+        peer_rest,
+        w_first,
+        w_second,
+        flops=2000000000,
+    )
+    got = lax.optimization_barrier((got, s1))[0]
     grad, grad_send, loss = whole(
         softmax_kernel,
         [((classes, targets), F32), ((classes, targets), BF), ((1, targets), F32)],
         [],
         part,
-        over(send, bits[-1]),
+        got,
         label,
     )
     at = core * (targets // 2) + (me // 2) * rows
@@ -299,7 +387,7 @@
         halves(stack),
         [((stack, LANE), F32), ((node_dev, hidden), F32)],
         grad, far_grad, high, low, far_high, far_low,
-        features, peer, h1, ph1, h2, ph2, s1, ps1, s2, ps2, w3t, w_second,
+        xt, pxt, h1t, ph1t, h2, ph2, s1, ps1, s2, ps2, w3t, w_second,
         limit=big,
     )
     size = stack // 2
@@ -313,18 +401,21 @@
         )
         size //= 2
     (out,) = whole(last_kernel, [((size, LANE), BF)], [], keep, over(send, bits[-1]))
-    for bit in reversed(bits):
+    for bit in reversed(bits[1:]):
         size *= 2
         (out,) = whole(functools.partial(join_kernel, bit), [((size, LANE), BF)], [], out, over(out, bit))
-    across = over(out, 1)
+    pair = (out, over(out, bits[0]))
+    across = [over(p, 1) for p in pair]
+    cores = [other_core(p) for p in pair]
+    both = [other_core(p) for p in across]
     first, second, third = whole(
-        place_kernel,
+        functools.partial(place_kernel, bits[0]),
         [((depth, hidden), BF), ((hidden, hidden), BF), ((classes, hidden), BF)],
         [],
-        out,
-        across,
-        other_core(out),
-        other_core(across),
+        *pair,
+        *across,
+        *cores,
+        *both,
     )
     return first, second, third.T, target_loss
 

time: 84.8 us -> 73.2 us (0.86)
  waiting for transfers between devices: 41.7 us -> 32.8 us
  local copies, waits for them, and re-layouts: 8.3 us -> 2.66 us
  Pallas kernels: 14.7 us -> 16.7 us
  starting transfers between devices: 17 us -> 19 us
  other arithmetic: 1.82 us -> 0.87 us
    ppermute x13 -> x14, waiting for transfers between devices: 39.4 us -> 31.1 us  [over(): return lax.ppermute(x, 'owner', [(i, i ^ bit) for i in range(owners)])]
    unnamed x34 -> x18, local copies, waits for them, and re-layouts: 5.88 us -> 2.07 us
    pallas_call x11 -> x13, Pallas kernels: 14.7 us -> 16.7 us  [whole(): pl.pallas_call(kernel, out_shape=[jax.ShapeDtypeStruct(shape, kind) for s...]
    dynamic_slice x1 -> x0, local copies, waits for them, and re-layouts: 1.84 us -> none  [body(): lax.dynamic_slice_in_dim(features, core * half, half, 0)]
    ppermute x13 -> x14, starting transfers between devices: 17 us -> 18 us  [over(): return lax.ppermute(x, 'owner', [(i, i ^ bit) for i in range(owners)])]
    ppermute x4 -> x6, starting transfers between devices: 0.02 us -> 0.99 us  [other_core(): return lax.ppermute(x, 'batch', [(0, 1), (1, 0)])]
    ppermute x4 -> x6, waiting for transfers between devices: 2.27 us -> 1.67 us  [other_core(): return lax.ppermute(x, 'batch', [(0, 1), (1, 0)])]
  transfers between devices with their start and end apart: 17 -> 20, of which waited for: 11 -> 12; matrix products, arithmetic and copies ran while one was open for 3% -> 1% of each run, Pallas kernels for 12% -> 16%
where the time goes in v2:
time: 73.2 us; the launch traced here: 72.8 us
  waiting for transfers between devices  32.8 us (45%)
  starting transfers between devices  19 us (26%)
  Pallas kernels  16.7 us (23%)
  local copies, waits for them, and re-layouts  2.66 us (4%)
  other arithmetic  0.87 us (1%)
  between operations  0.79 us (1%)
    ppermute x14, waiting for transfers between devices, over(): return lax.ppermute(x, 'owner', [(i, i ^ bit) for i in range(owners)])  31.1 us
    ppermute x14, starting transfers between devices, over(): return lax.ppermute(x, 'owner', [(i, i ^ bit) for i in range(owners)])  18 us
    pallas_call x13, Pallas kernels, whole(): pl.pallas_call(kernel, out_shape=[jax.ShapeDtypeStruct(shape, kind) for s...  16.7 us
    unnamed x18, local copies, waits for them, and re-layouts  2.07 us
    ppermute x6, waiting for transfers between devices, other_core(): return lax.ppermute(x, 'batch', [(0, 1), (1, 0)])  1.67 us
  transfers between devices with their start and end apart: 20, of which 12 were waited for; matrix products, arithmetic and copies ran while one was open for 1% of the time, Pallas kernels for 16%

profile of v2, /device:TPU:0, one launch (start us, length us, event | category | flops | bytes accessed | tf_op | source)
XLA Modules:
  0.0 72.8 jit_solution(4401879343368444549)
XLA Ops:
  4.1 2.9 %collective-permute-start.1 = (f32[16,128]{1,0:T(8,128)S(1)}, f32[16,128]{1,0:T(8,128)S(1)}, u32[]{:S(2)}, u32[]{:S(2)}) collective-permute-start(f32[16,128]{1,0:T(8,128)S(1)} %maximum_select_fusion.2.after), channel_id=1, source_target_pairs={{0,4},{2,6},{4,0},{6,2},{8,12},{10,14},{12,8},{14,10},{1,5},{3,7},... | collective-permute-start | bytes 24584 | tf_op jit(solution)/shard_map/ppermute | solution.py:278
  7.1 3.7 %shard_map.103 = (bf16[153,512]{1,0:T(8,128)(2,1)}, bf16[256,768]{1,0:T(8,128)(2,1)}) custom-call(bf16[512,768]{1,0:T(8,128)(2,1)} %x.1, bf16[768,512]{1,0:T(8,128)(2,1)} %w1.3, bf16[512,512]{1,0:T(8,128)(2,1)} %w2.5, bf16[153,512]{1,0:T(8,128)(2,1)} %bitcast.5, f32[16,128]{1,0:T(8,128)} %copy-done.8), custom_call_target="tpu_custom_call" | custom-call | flops 2000000000 | bytes 3906250 | tf_op jit(solution)/shard_map/pallas_call | solution.py:253
  11.6 2.6 %collective-permute-start.3 = (f32[32,128]{1,0:T(8,128)S(1)}, f32[32,128]{1,0:T(8,128)S(1)}, u32[]{:S(2)}, u32[]{:S(2)}) collective-permute-start(f32[32,128]{1,0:T(8,128)S(1)} %maximum_select_fusion.1), channel_id=1, source_target_pairs={{0,8},{2,10},{4,12},{6,14},{8,0},{10,2},{12,4},{14,6},{1,9},{3,11}... | collective-permute-start | bytes 49160 | tf_op jit(solution)/shard_map/ppermute | solution.py:278
  14.2 1.5 %collective-permute-start.2 = (bf16[153,512]{1,0:T(8,128)(2,1)}, bf16[153,512]{1,0:T(8,128)(2,1)S(1)}, u32[]{:S(2)}, u32[]{:S(2)}) collective-permute-start(bf16[153,512]{1,0:T(8,128)(2,1)} %get-tuple-element.43.mine), channel_id=1, source_target_pairs={{0,2},{2,0},{4,6},{6,4},{8,10},{10,8},{12,14},{14,12},{1,3},{3,1},... | collective-permute-start | bytes 470024 | tf_op jit(solution)/shard_map/ppermute | solution.py:278
  16.4 1.5 %collective-permute-start.5 = (f32[64,128]{1,0:T(8,128)S(1)}, f32[64,128]{1,0:T(8,128)S(1)}, u32[]{:S(2)}, u32[]{:S(2)}) collective-permute-start(f32[64,128]{1,0:T(8,128)S(1)} %maximum_select_fusion.packed), channel_id=1, source_target_pairs={{0,2},{2,0},{4,6},{6,4},{8,10},{10,8},{12,14},{14,12},{1,3},{3,1},... | collective-permute-start | bytes 98312 | tf_op jit(solution)/shard_map/ppermute | solution.py:278
  18.4 2.0 %shard_map.104 = (bf16[1024,128]{1,0:T(8,128)(2,1)S(1)}, bf16[1024,128]{1,0:T(8,128)(2,1)S(1)}, s32[1,128]{1,0:T(1,128)S(1)}) custom-call(f32[64,128]{1,0:T(8,128)S(1)} %maximum_select_fusion.packed), custom_call_target="tpu_custom_call" | custom-call | flops 1000000000 | bytes 1953125 | tf_op jit(solution)/shard_map/pallas_call | solution.py:253
  20.4 1.0 %collective-permute-done.2.theirs = bf16[153,512]{1,0:T(8,128)(2,1)S(1)} collective-permute-done((bf16[153,512]{1,0:T(8,128)(2,1)}, bf16[153,512]{1,0:T(8,128)(2,1)S(1)}, u32[]{:S(2)}, u32[]{:S(2)}) %collective-permute-start.2) | collective-permute-done | bytes 156704 | tf_op jit(solution)/shard_map/ppermute | solution.py:278
  22.5 2.4 %shard_map.106 = (bf16[1024,128]{1,0:T(8,128)(2,1)S(1)}, bf16[1024,128]{1,0:T(8,128)(2,1)S(1)}, s32[1,128]{1,0:T(1,128)}) custom-call(f32[64,128]{1,0:T(8,128)S(1)} %collective-permute-done.5.packed), custom_call_target="tpu_custom_call" | custom-call | flops 1000000000 | bytes 1953125 | tf_op jit(solution)/shard_map/pallas_call | solution.py:253
  24.9 1.0 %collective-permute-done.4 = bf16[153,128]{1,0:T(8,128)(2,1)S(1)} collective-permute-done((bf16[153,128]{1,0:T(8,128)(2,1)S(1)}, bf16[153,128]{1,0:T(8,128)(2,1)S(1)}, u32[]{:S(2)}, u32[]{:S(2)}) %collective-permute-start.4) | collective-permute-done | bytes 39200 | tf_op jit(solution)/shard_map/ppermute | solution.py:278
  25.9 1.7 %collective-permute-start.6 = (bf16[153,128]{1,0:T(8,128)(2,1)S(1)}, bf16[153,128]{1,0:T(8,128)(2,1)S(1)}, u32[]{:S(2)}, u32[]{:S(2)}) collective-permute-start(bf16[153,128]{1,0:T(8,128)(2,1)S(1)} %get-tuple-element.80.after), channel_id=1, source_target_pairs={{0,8},{2,10},{4,12},{6,14},{8,0},{10,2},{12,4},{14,6},{1,9},{3,11}... | collective-permute-start | bytes 117512 | tf_op jit(solution)/shard_map/ppermute | solution.py:278
  27.6 3.7 %collective-permute-done.6.got = bf16[153,128]{1,0:T(8,128)(2,1)S(1)} collective-permute-done((bf16[153,128]{1,0:T(8,128)(2,1)S(1)}, bf16[153,128]{1,0:T(8,128)(2,1)S(1)}, u32[]{:S(2)}, u32[]{:S(2)}) %collective-permute-start.6) | collective-permute-done | bytes 39200 | tf_op jit(solution)/shard_map/ppermute | solution.py:278
  31.4 1.6 %shard_map.107 = (bf16[768,512]{1,0:T(8,128)(2,1)S(1)}, bf16[512,512]{1,0:T(8,128)(2,1)S(1)}, bf16[512,128]{1,0:T(8,128)(2,1)S(1)}, f32[512,128]{1,0:T(8,128)S(1)}, f32[512,512]{1,0:T(8,128)S(1)}) custom-call(bf16[512,768]{1,0:T(8,128)(2,1)S(1)} %copy-done.6, bf16[768,512]{1,0:T(8,128)(2,1)S(1)} %copy-done.7, bf16[512,512]{1,0:T(8,128)(2,1)S(1)} %copy-done, ...), custom_call_target="tpu_custom_call" | custom-call | flops 2000000000 | bytes 3906250 | tf_op jit(solution)/shard_map/pallas_call | solution.py:253
  33.0 1.6 %collective-permute-start.7 = (bf16[153,128]{1,0:T(8,128)(2,1)S(1)}, bf16[153,128]{1,0:T(8,128)(2,1)S(1)}, u32[]{:S(2)}, u32[]{:S(2)}) collective-permute-start(bf16[153,128]{1,0:T(8,128)(2,1)S(1)} %get-tuple-element.58), channel_id=1, source_target_pairs={{0,2},{2,0},{4,6},{6,4},{8,10},{10,8},{12,14},{14,12},{1,3},{3,1},... | collective-permute-start | bytes 117512 | tf_op jit(solution)/shard_map/ppermute | solution.py:278
  34.6 1.6 %shard_map.109 = (bf16[768,512]{1,0:T(8,128)(2,1)S(1)}, bf16[512,512]{1,0:T(8,128)(2,1)S(1)}, bf16[512,128]{1,0:T(8,128)(2,1)S(1)}, f32[512,128]{1,0:T(8,128)S(1)}, f32[512,512]{1,0:T(8,128)S(1)}) custom-call(bf16[256,768]{1,0:T(8,128)(2,1)S(1)} %collective-permute-done.8.mine, bf16[256,768]{1,0:T(8,128)(2,1)S(1)} %collective-permute-done.9.theirs, ...), custom_call_target="tpu_custom_call" | custom-call | flops 2000000000 | bytes 3906250 | tf_op jit(solution)/shard_map/pallas_call | solution.py:253
  37.1 3.3 %shard_map.110 = (bf16[736,128]{1,0:T(8,128)(2,1)S(1)}, f32[736,128]{1,0:T(8,128)S(1)}) custom-call(f32[153,128]{1,0:T(8,128)S(1)} %get-tuple-element.57.grad, bf16[153,128]{1,0:T(8,128)(2,1)S(1)} %collective-permute-done.7.far_grad, bf16[1024,128]{1,0:T(8,128)(2,1)S(1)} %get-tuple-element.47.high, bf16[1024,128]{1,0:T(8,128)(2,1)S(1)} %get-tuple-element.48.low, ...), custom_call_target="tpu_custom_call" | custom-call | flops 1000000 | bytes 1953 | tf_op jit(solution)/shard_map/pallas_call | solution.py:253
  40.6 5.9 %collective-permute-done.10.got = bf16[736,128]{1,0:T(8,128)(2,1)S(1)} collective-permute-done((bf16[736,128]{1,0:T(8,128)(2,1)S(1)}, bf16[736,128]{1,0:T(8,128)(2,1)S(1)}, u32[]{:S(2)}, u32[]{:S(2)}) %collective-permute-start.10) | collective-permute-done | bytes 188448 | tf_op jit(solution)/shard_map/ppermute | solution.py:278
  46.6 1.3 %collective-permute-start.11 = (bf16[368,128]{1,0:T(8,128)(2,1)S(1)}, bf16[368,128]{1,0:T(8,128)(2,1)S(1)}, u32[]{:S(2)}, u32[]{:S(2)}) collective-permute-start(bf16[368,128]{1,0:T(8,128)(2,1)S(1)} %get-tuple-element.75), channel_id=1, source_target_pairs={{0,8},{2,10},{4,12},{6,14},{8,0},{10,2},{12,4},{14,6},{1,9},{3,11}... | collective-permute-start | bytes 282632 | tf_op jit(solution)/shard_map/ppermute | solution.py:278
  47.8 5.0 %collective-permute-done.11.got = bf16[368,128]{1,0:T(8,128)(2,1)S(1)} collective-permute-done((bf16[368,128]{1,0:T(8,128)(2,1)S(1)}, bf16[368,128]{1,0:T(8,128)(2,1)S(1)}, u32[]{:S(2)}, u32[]{:S(2)}) %collective-permute-start.11) | collective-permute-done | bytes 94240 | tf_op jit(solution)/shard_map/ppermute | solution.py:278
  53.4 5.2 %collective-permute-done.12.got = bf16[368,128]{1,0:T(8,128)(2,1)S(1)} collective-permute-done((bf16[368,128]{1,0:T(8,128)(2,1)S(1)}, bf16[368,128]{1,0:T(8,128)(2,1)S(1)}, u32[]{:S(2)}, u32[]{:S(2)}) %collective-permute-start.12) | collective-permute-done | bytes 94240 | tf_op jit(solution)/shard_map/ppermute | solution.py:278
  58.8 1.6 %collective-permute-start.14 = (bf16[736,128]{1,0:T(8,128)(2,1)S(1)}, bf16[736,128]{1,0:T(8,128)(2,1)S(1)}, u32[]{:S(2)}, u32[]{:S(2)}) collective-permute-start(bf16[736,128]{1,0:T(8,128)(2,1)S(1)} %shard_map.113.refs_0_), channel_id=1, source_target_pairs={{0,2},{2,0},{4,6},{6,4},{8,10},{10,8},{12,14},{14,12},{1,3},{3,1},... | collective-permute-start | bytes 565256 | tf_op jit(solution)/shard_map/ppermute | solution.py:278
  60.3 4.0 %collective-permute-done.13.refs_1_ = bf16[736,128]{1,0:T(8,128)(2,1)S(1)} collective-permute-done((bf16[736,128]{1,0:T(8,128)(2,1)S(1)}, bf16[736,128]{1,0:T(8,128)(2,1)S(1)}, u32[]{:S(2)}, u32[]{:S(2)}) %collective-permute-start.13) | collective-permute-done | bytes 188448 | tf_op jit(solution)/shard_map/ppermute | solution.py:278
  64.4 1.5 %collective-permute-start.15 = (bf16[736,128]{1,0:T(8,128)(2,1)S(1)}, bf16[736,128]{1,0:T(8,128)(2,1)S(1)}, u32[]{:S(2)}, u32[]{:S(2)}) collective-permute-start(bf16[736,128]{1,0:T(8,128)(2,1)S(1)} %collective-permute-done.13.refs_1_), channel_id=1, source_target_pairs={{0,2},{2,0},{4,6},{6,4},{8,10},{10,8},{12,14},{14,12},{1,3},{3,1},... | collective-permute-start | bytes 565256 | tf_op jit(solution)/shard_map/ppermute | solution.py:278
  66.4 3.6 %collective-permute-done.15.refs_3_ = bf16[736,128]{1,0:T(8,128)(2,1)S(1)} collective-permute-done((bf16[736,128]{1,0:T(8,128)(2,1)S(1)}, bf16[736,128]{1,0:T(8,128)(2,1)S(1)}, u32[]{:S(2)}, u32[]{:S(2)}) %collective-permute-start.15) | collective-permute-done | bytes 188448 | tf_op jit(solution)/shard_map/ppermute | solution.py:278
  71.4 1.4 %shard_map.114 = (bf16[768,512]{1,0:T(8,128)(2,1)}, bf16[512,512]{1,0:T(8,128)(2,1)}, bf16[153,512]{1,0:T(8,128)(2,1)}) custom-call(bf16[736,128]{1,0:T(8,128)(2,1)S(1)} %shard_map.113.refs_0_, bf16[736,128]{1,0:T(8,128)(2,1)S(1)} %collective-permute-done.13.refs_1_, bf16[736,128]{1,0:T(8,128)(2,1)S(1)} %collective-permute-done.14.refs_2_, ...), custom_call_target="tpu_custom_call" | custom-call | flops 1000000 | bytes 1953 | tf_op jit(solution)/shard_map/pallas_call | solution.py:253
  (52 shorter events, 10.4 us)
Async XLA Ops:
  2.8 1.3 %collective-permute-start = (f32[16,64]{1,0:T(8,128)S(1)}, f32[16,64]{1,0:T(8,128)S(1)}, u32[]{:S(2)}, u32[]{:S(2)}) collective-permute-start(f32[16,64]{1,0:T(8,128)S(1)} %shard_map.102), channel_id=1, source_target_pairs={{0,1},{1,0},{2,3},{3,2},{4,5},{5,4},{6,7},{7,6},{8,9},{9,8},{10,11... | collective-permute-start | bytes 12296 | tf_op jit(solution)/shard_map/ppermute | solution.py:281
  4.1 6.6 %collective-permute-start.1 = (f32[16,128]{1,0:T(8,128)S(1)}, f32[16,128]{1,0:T(8,128)S(1)}, u32[]{:S(2)}, u32[]{:S(2)}) collective-permute-start(f32[16,128]{1,0:T(8,128)S(1)} %maximum_select_fusion.2.after), channel_id=1, source_target_pairs={{0,4},{2,6},{4,0},{6,2},{8,12},{10,14},{12,8},{14,10},{1,5},{3,7},... | collective-permute-start | bytes 24584 | tf_op jit(solution)/shard_map/ppermute | solution.py:278
  11.6 4.8 %collective-permute-start.3 = (f32[32,128]{1,0:T(8,128)S(1)}, f32[32,128]{1,0:T(8,128)S(1)}, u32[]{:S(2)}, u32[]{:S(2)}) collective-permute-start(f32[32,128]{1,0:T(8,128)S(1)} %maximum_select_fusion.1), channel_id=1, source_target_pairs={{0,8},{2,10},{4,12},{6,14},{8,0},{10,2},{12,4},{14,6},{1,9},{3,11}... | collective-permute-start | bytes 49160 | tf_op jit(solution)/shard_map/ppermute | solution.py:278
  14.2 7.3 %collective-permute-start.2 = (bf16[153,512]{1,0:T(8,128)(2,1)}, bf16[153,512]{1,0:T(8,128)(2,1)S(1)}, u32[]{:S(2)}, u32[]{:S(2)}) collective-permute-start(bf16[153,512]{1,0:T(8,128)(2,1)} %get-tuple-element.43.mine), channel_id=1, source_target_pairs={{0,2},{2,0},{4,6},{6,4},{8,10},{10,8},{12,14},{14,12},{1,3},{3,1},... | collective-permute-start | bytes 470024 | tf_op jit(solution)/shard_map/ppermute | solution.py:278
  16.4 6.1 %collective-permute-start.5 = (f32[64,128]{1,0:T(8,128)S(1)}, f32[64,128]{1,0:T(8,128)S(1)}, u32[]{:S(2)}, u32[]{:S(2)}) collective-permute-start(f32[64,128]{1,0:T(8,128)S(1)} %maximum_select_fusion.packed), channel_id=1, source_target_pairs={{0,2},{2,0},{4,6},{6,4},{8,10},{10,8},{12,14},{14,12},{1,3},{3,1},... | collective-permute-start | bytes 98312 | tf_op jit(solution)/shard_map/ppermute | solution.py:278
  17.9 13.5 %collective-permute-start.8 = (bf16[256,768]{1,0:T(8,128)(2,1)}, bf16[256,768]{1,0:T(8,128)(2,1)S(1)}, u32[]{:S(2)}, u32[]{:S(2)}) collective-permute-start(bf16[256,768]{1,0:T(8,128)(2,1)} %get-tuple-element.62), channel_id=1, source_target_pairs={{0,2},{2,0},{4,6},{6,4},{8,10},{10,8},{12,14},{14,12},{1,3},{3,1},... | collective-permute-start | bytes 1179656 | tf_op jit(solution)/shard_map/ppermute | solution.py:278
  21.8 9.5 %copy-start = (bf16[512,512]{1,0:T(8,128)(2,1)S(1)}, bf16[512,512]{1,0:T(8,128)(2,1)}, u32[]{:S(2)}) copy-start(bf16[512,512]{1,0:T(8,128)(2,1)} %w2.5) | copy-start | bytes 1572868
  21.8 9.5 %copy-start.6 = (bf16[512,768]{1,0:T(8,128)(2,1)S(1)}, bf16[512,768]{1,0:T(8,128)(2,1)}, u32[]{:S(2)}) copy-start(bf16[512,768]{1,0:T(8,128)(2,1)} %x.1) | copy-start | bytes 2359300
  21.8 9.5 %copy-start.7 = (bf16[768,512]{1,0:T(8,128)(2,1)S(1)}, bf16[768,512]{1,0:T(8,128)(2,1)}, u32[]{:S(2)}) copy-start(bf16[768,512]{1,0:T(8,128)(2,1)} %w1.3) | copy-start | bytes 2359300
  21.8 4.1 %collective-permute-start.4 = (bf16[153,128]{1,0:T(8,128)(2,1)S(1)}, bf16[153,128]{1,0:T(8,128)(2,1)S(1)}, u32[]{:S(2)}, u32[]{:S(2)}) collective-permute-start(bf16[153,128]{1,0:T(8,128)(2,1)S(1)} %get-tuple-element.50), channel_id=1, source_target_pairs={{0,4},{2,6},{4,0},{6,2},{8,12},{10,14},{12,8},{14,10},{1,5},{3,7},... | collective-permute-start | bytes 117512 | tf_op jit(solution)/shard_map/ppermute | solution.py:278
  25.9 5.4 %collective-permute-start.6 = (bf16[153,128]{1,0:T(8,128)(2,1)S(1)}, bf16[153,128]{1,0:T(8,128)(2,1)S(1)}, u32[]{:S(2)}, u32[]{:S(2)}) collective-permute-start(bf16[153,128]{1,0:T(8,128)(2,1)S(1)} %get-tuple-element.80.after), channel_id=1, source_target_pairs={{0,8},{2,10},{4,12},{6,14},{8,0},{10,2},{12,4},{14,6},{1,9},{3,11}... | collective-permute-start | bytes 117512 | tf_op jit(solution)/shard_map/ppermute | solution.py:278
  31.3 3.3 %collective-permute-start.9 = (bf16[256,768]{1,0:T(8,128)(2,1)S(1)}, bf16[256,768]{1,0:T(8,128)(2,1)S(1)}, u32[]{:S(2)}, u32[]{:S(2)}) collective-permute-start(bf16[256,768]{1,0:T(8,128)(2,1)S(1)} %collective-permute-done.8.mine), channel_id=1, source_target_pairs={{0,1},{1,0},{2,3},{3,2},{4,5},{5,4},{6,7},{7,6},{8,9},{9,8},{10,11... | collective-permute-start | bytes 1179656 | tf_op jit(solution)/shard_map/ppermute | solution.py:281
  33.0 4.1 %copy-start.2 = (bf16[512,153]{0,1:T(8,128)(2,1)S(1)}, bf16[512,153]{0,1:T(8,128)(2,1)}, u32[]{:S(2)}) copy-start(bf16[512,153]{0,1:T(8,128)(2,1)} %param.10) | copy-start | bytes 470020
  33.0 4.1 %collective-permute-start.7 = (bf16[153,128]{1,0:T(8,128)(2,1)S(1)}, bf16[153,128]{1,0:T(8,128)(2,1)S(1)}, u32[]{:S(2)}, u32[]{:S(2)}) collective-permute-start(bf16[153,128]{1,0:T(8,128)(2,1)S(1)} %get-tuple-element.58), channel_id=1, source_target_pairs={{0,2},{2,0},{4,6},{6,4},{8,10},{10,8},{12,14},{14,12},{1,3},{3,1},... | collective-permute-start | bytes 117512 | tf_op jit(solution)/shard_map/ppermute | solution.py:278
  40.4 6.1 %collective-permute-start.10 = (bf16[736,128]{1,0:T(8,128)(2,1)S(1)}, bf16[736,128]{1,0:T(8,128)(2,1)S(1)}, u32[]{:S(2)}, u32[]{:S(2)}) collective-permute-start(bf16[736,128]{1,0:T(8,128)(2,1)S(1)} %get-tuple-element.73), channel_id=1, source_target_pairs={{0,4},{2,6},{4,0},{6,2},{8,12},{10,14},{12,8},{14,10},{1,5},{3,7},... | collective-permute-start | bytes 565256 | tf_op jit(solution)/shard_map/ppermute | solution.py:278
  46.6 6.3 %collective-permute-start.11 = (bf16[368,128]{1,0:T(8,128)(2,1)S(1)}, bf16[368,128]{1,0:T(8,128)(2,1)S(1)}, u32[]{:S(2)}, u32[]{:S(2)}) collective-permute-start(bf16[368,128]{1,0:T(8,128)(2,1)S(1)} %get-tuple-element.75), channel_id=1, source_target_pairs={{0,8},{2,10},{4,12},{6,14},{8,0},{10,2},{12,4},{14,6},{1,9},{3,11}... | collective-permute-start | bytes 282632 | tf_op jit(solution)/shard_map/ppermute | solution.py:278
  52.9 5.8 %collective-permute-start.12 = (bf16[368,128]{1,0:T(8,128)(2,1)S(1)}, bf16[368,128]{1,0:T(8,128)(2,1)S(1)}, u32[]{:S(2)}, u32[]{:S(2)}) collective-permute-start(bf16[368,128]{1,0:T(8,128)(2,1)S(1)} %shard_map.112.mine), channel_id=1, source_target_pairs={{0,8},{2,10},{4,12},{6,14},{8,0},{10,2},{12,4},{14,6},{1,9},{3,11}... | collective-permute-start | bytes 282632 | tf_op jit(solution)/shard_map/ppermute | solution.py:278
  58.7 5.6 %collective-permute-start.13 = (bf16[736,128]{1,0:T(8,128)(2,1)S(1)}, bf16[736,128]{1,0:T(8,128)(2,1)S(1)}, u32[]{:S(2)}, u32[]{:S(2)}) collective-permute-start(bf16[736,128]{1,0:T(8,128)(2,1)S(1)} %shard_map.113.refs_0_), channel_id=1, source_target_pairs={{0,4},{2,6},{4,0},{6,2},{8,12},{10,14},{12,8},{14,10},{1,5},{3,7},... | collective-permute-start | bytes 565256 | tf_op jit(solution)/shard_map/ppermute | solution.py:278
  58.8 7.6 %collective-permute-start.14 = (bf16[736,128]{1,0:T(8,128)(2,1)S(1)}, bf16[736,128]{1,0:T(8,128)(2,1)S(1)}, u32[]{:S(2)}, u32[]{:S(2)}) collective-permute-start(bf16[736,128]{1,0:T(8,128)(2,1)S(1)} %shard_map.113.refs_0_), channel_id=1, source_target_pairs={{0,2},{2,0},{4,6},{6,4},{8,10},{10,8},{12,14},{14,12},{1,3},{3,1},... | collective-permute-start | bytes 565256 | tf_op jit(solution)/shard_map/ppermute | solution.py:278
  64.4 5.6 %collective-permute-start.15 = (bf16[736,128]{1,0:T(8,128)(2,1)S(1)}, bf16[736,128]{1,0:T(8,128)(2,1)S(1)}, u32[]{:S(2)}, u32[]{:S(2)}) collective-permute-start(bf16[736,128]{1,0:T(8,128)(2,1)S(1)} %collective-permute-done.13.refs_1_), channel_id=1, source_target_pairs={{0,2},{2,0},{4,6},{6,4},{8,10},{10,8},{12,14},{14,12},{1,3},{3,1},... | collective-permute-start | bytes 565256 | tf_op jit(solution)/shard_map/ppermute | solution.py:278
  65.8 4.7 %collective-permute-start.16 = (bf16[736,128]{1,0:T(8,128)(2,1)S(1)}, bf16[736,128]{1,0:T(8,128)(2,1)S(1)}, u32[]{:S(2)}, u32[]{:S(2)}) collective-permute-start(bf16[736,128]{1,0:T(8,128)(2,1)S(1)} %shard_map.113.refs_0_), channel_id=1, source_target_pairs={{0,1},{1,0},{2,3},{3,2},{4,5},{5,4},{6,7},{7,6},{8,9},{9,8},{10,11... | collective-permute-start | bytes 565256 | tf_op jit(solution)/shard_map/ppermute | solution.py:281
  65.8 4.7 %collective-permute-start.17 = (bf16[736,128]{1,0:T(8,128)(2,1)S(1)}, bf16[736,128]{1,0:T(8,128)(2,1)S(1)}, u32[]{:S(2)}, u32[]{:S(2)}) collective-permute-start(bf16[736,128]{1,0:T(8,128)(2,1)S(1)} %collective-permute-done.13.refs_1_), channel_id=1, source_target_pairs={{0,1},{1,0},{2,3},{3,2},{4,5},{5,4},{6,7},{7,6},{8,9},{9,8},{10,11... | collective-permute-start | bytes 565256 | tf_op jit(solution)/shard_map/ppermute | solution.py:281
  66.4 4.2 %collective-permute-start.18 = (bf16[736,128]{1,0:T(8,128)(2,1)S(1)}, bf16[736,128]{1,0:T(8,128)(2,1)S(1)}, u32[]{:S(2)}, u32[]{:S(2)}) collective-permute-start(bf16[736,128]{1,0:T(8,128)(2,1)S(1)} %collective-permute-done.14.refs_2_), channel_id=1, source_target_pairs={{0,1},{1,0},{2,3},{3,2},{4,5},{5,4},{6,7},{7,6},{8,9},{9,8},{10,11... | collective-permute-start | bytes 565256 | tf_op jit(solution)/shard_map/ppermute | solution.py:281
  69.9 1.4 %collective-permute-start.19 = (bf16[736,128]{1,0:T(8,128)(2,1)S(1)}, bf16[736,128]{1,0:T(8,128)(2,1)S(1)}, u32[]{:S(2)}, u32[]{:S(2)}) collective-permute-start(bf16[736,128]{1,0:T(8,128)(2,1)S(1)} %collective-permute-done.15.refs_3_), channel_id=1, source_target_pairs={{0,1},{1,0},{2,3},{3,2},{4,5},{5,4},{6,7},{7,6},{8,9},{9,8},{10,11... | collective-permute-start | bytes 565256 | tf_op jit(solution)/shard_map/ppermute | solution.py:281
  (5 other events, 8.6 us)

commit v3 on v2

--- a/solution.py
+++ b/solution.py
@@ -10,6 +10,7 @@
 F32 = jnp.float32
 ROW = 16
 LANE = 128
+PACK = 16
 
 
 def nn(a, b):
@@ -31,7 +32,7 @@
 
 
 def activate(pre):
-    sigma = 1.0 / (1.0 + jnp.exp(-pre))
+    sigma = 0.5 * jnp.tanh(0.5 * pre) + 0.5
     return (pre * sigma).astype(BF), sigma * (1.0 + pre * (1.0 - sigma))
 
 
@@ -42,26 +43,27 @@
     return copies
 
 
-def pack_kernel(nodes, ids, wts, labels, out):
+def pack_kernel(nodes, ids_hbm, wts_hbm, labels_hbm, x_hbm, w1_hbm, w2_hbm, w3_hbm, out, half, x, w1, w2, w3, ids, wts, labels, sem):
     rows, fanout = ids.shape
+    part = half.shape[0]
+    mine = x_hbm.at[pl.ds(pl.multiple_of(lax.axis_index("batch") * part, ROW), part), :]
+    small = ((labels_hbm, labels), (ids_hbm, ids), (wts_hbm, wts))
+    into = launch(sem, small + ((mine, half), (x_hbm, x), (w1_hbm, w1), (w2_hbm, w2), (w3_hbm, w3)))
+    for c in into[:3]:
+        c.wait()
     shape = (rows, rows)
     same = lax.broadcasted_iota(jnp.int32, shape, 0) == lax.broadcasted_iota(jnp.int32, shape, 1)
     label = jnp.sum(jnp.where(same, labels[...].astype(F32), 0.0), axis=1, keepdims=True)
     out[:, :fanout] = ids[...].astype(F32) + label * nodes
     out[:, fanout:] = wts[...]
-
-
-def own_kernel(x_hbm, w1_hbm, w2_hbm, w3_hbm, after, scores, half, x, w1, w2, w3, sem):
+    for c in into[3:]:
+        c.wait()
+
+
+def own_kernel(x, w1, w2, w3, after, scores):
     del after
-    into = launch(sem, ((x_hbm, x), (w1_hbm, w1), (w2_hbm, w2), (w3_hbm, w3)))
-    into[0].wait()
-    rows = half.shape[0]
-    half[...] = x[pl.ds(pl.multiple_of(lax.axis_index("batch") * rows, ROW), rows), :]
-    into[1].wait()
     hidden = activate(nn(x[...], w1[...]))[0]
-    into[2].wait()
     hidden = activate(nn(hidden, w2[...]))[0]
-    into[3].wait()
     scores[...] = nt(w3[...], hidden).astype(BF)
 
 
@@ -167,30 +169,21 @@
     classes = w3t.shape[0]
     cols = pl.ds(device_slice(), LANE)
     w2_rows = w2[cols, :]
-    for side, (x_, h1_, h2_, s1_, s2_) in enumerate(((xt, h1t, h2, s1, s2), (pxt, ph1t, ph2, ps1, ps2))):
-        at = slice(side * n, (side + 1) * n)
-        hi, lo, fhi, flo = high[at], low[at], far_high[at], far_low[at]
-        g = nt(hi, top) + nt(lo, top) + nt(hi, rest) + nt(fhi, far) + nt(flo, far)
-        gt = nt(top, hi) + nt(top, lo) + nt(rest, hi) + nt(far, fhi) + nt(far, flo)
-        b2 = nn(g.astype(BF), w3t[...]) * s2_[...]
-        two[...] = b2
-        b2 = b2.astype(BF)
-        b2_cols = two[:, cols].astype(BF)
-        b1 = (nt(b2, w2_rows) * s1_[...]).astype(BF)
-        first = nn(x_[...], b1)
-        second = nn(h1_[...], b2_cols)
-        third = nn(gt.astype(BF), h2_[...])
-        if side == 0:
-            acc[:depth] = first
-            acc[depth : depth + hidden] = second
-            acc[depth + hidden : depth + hidden + classes] = third
-        else:
-            acc[:depth] += first
-            acc[depth : depth + hidden] += second
-            acc[depth + hidden : depth + hidden + classes] += third
-    rest_rows = acc.shape[0] - (depth + hidden + classes)
-    if rest_rows:
-        acc[depth + hidden + classes :] = jnp.zeros((rest_rows, LANE), F32)
+    sides = (slice(0, n), slice(n, 2 * n))
+    left = [jnp.concatenate([high[at], low[at], high[at], far_high[at], far_low[at]], axis=1) for at in sides]
+    right = jnp.concatenate([top, top, rest, far, far], axis=1)
+    g = [nt(v, right).astype(BF) for v in left]
+    b2 = [(nn(v, w3t[...]) * s[...]).astype(BF) for v, s in zip(g, (s2, ps2))]
+    two[0] = b2[0]
+    two[1] = b2[1]
+    b1 = [(nt(v, w2_rows) * s[...]).astype(BF) for v, s in zip(b2, (s1, ps1))]
+    gt = [nt(right, v).astype(BF) for v in left]
+    acc[depth + hidden : depth + hidden + classes] = nn(gt[0], h2[...]) + nn(gt[1], ph2[...])
+    acc[depth : depth + hidden] = nn(h1t[...], two[0, :, cols]) + nn(ph1t[...], two[1, :, cols])
+    acc[:depth] = nn(xt[...], b1[0]) + nn(pxt[...], b1[1])
+    blank = acc.shape[0] - (depth + hidden + classes)
+    if blank:
+        acc[depth + hidden + classes :] = jnp.zeros((blank, LANE), F32)
     halve(bit, acc, send, keep)
 
 
@@ -206,8 +199,8 @@
     halve(bit, acc, send, keep)
 
 
-def last_kernel(kept, got, out):
-    out[...] = (kept[...] + got[...].astype(F32)).astype(BF)
+def sum_kernel(kept, got, out):
+    out[...] = (kept[...].astype(F32) + got[...].astype(F32)).astype(BF)
 
 
 def join_kernel(bit, mine, got, out):
@@ -215,6 +208,22 @@
     up = lax.rem(lax.axis_index("owner") // bit, 2)
     out[pl.ds(pl.multiple_of(up * rows, ROW), rows), :] = mine[...]
     out[pl.ds(pl.multiple_of((1 - up) * rows, ROW), rows), :] = got[...]
+
+
+def fill(order, halves, sides, outs):
+    rows = halves[0].shape[0]
+    for i, (s, h) in enumerate(sides):
+        cols = pl.ds(pl.multiple_of((2 * s + h) * LANE, LANE), LANE)
+        for j in range(2):
+            ref = halves[2 * i + order[j]]
+            if ref is None:
+                continue
+            top = 0
+            for out in outs:
+                low, high = max(top, j * rows), min(top + out.shape[0], (j + 1) * rows)
+                if low < high:
+                    out[low - top : high - top, cols] = ref[low - j * rows : high - j * rows]
+                top += out.shape[0]
 
 
 def place_kernel(bit, *refs):
@@ -223,33 +232,24 @@
     side = lax.rem(me, 2)
     core = lax.axis_index("batch")
     up = lax.rem(me // bit, 2)
-    rows = halves[0].shape[0]
-
-    def fill(order):
-        for i, (s, h) in enumerate(((side, core), (1 - side, core), (side, 1 - core), (1 - side, 1 - core))):
-            cols = pl.ds(pl.multiple_of((2 * s + h) * LANE, LANE), LANE)
-            for j in range(2):
-                ref = halves[2 * i + order[j]]
-                top = 0
-                for out in outs:
-                    low, high = max(top, j * rows), min(top + out.shape[0], (j + 1) * rows)
-                    if low < high:
-                        out[low - top : high - top, cols] = ref[low - j * rows : high - j * rows]
-                    top += out.shape[0]
+    sides = ((side, core), (1 - side, core), (side, 1 - core), (1 - side, 1 - core))
 
     @pl.when(up == 0)
     def _():
-        fill((0, 1))
+        fill((0, 1), halves, sides, outs)
 
     @pl.when(up == 1)
     def _():
-        fill((1, 0))
+        fill((1, 0), halves, sides, outs)
 
 
 def whole(kernel, outs, scratch, *args, flops=1000000, limit=24, far_in=(), far_out=()):
     def spec(i, far):
         return pl.BlockSpec(memory_space=pltpu.HBM if i in far else pltpu.VMEM)
 
+    args = [
+        pltpu.with_memory_space_constraint(x, pltpu.HBM) if i in far_in else x for i, x in enumerate(args)
+    ]
     return pl.pallas_call(
         kernel,
         out_shape=[jax.ShapeDtypeStruct(shape, kind) for shape, kind in outs],
@@ -281,30 +281,37 @@
         return lax.ppermute(x, "batch", [(0, 1), (1, 0)])
 
     w3t = w_third.T
-    (packed,) = whole(
+    half = node_dev // 2
+    w1_type, w2_type, x_type = (w_first.shape, BF), (w_second.shape, BF), (features.shape, BF)
+    packed, my_half, features, w_first, w_second, w3t = whole(
         functools.partial(pack_kernel, nodes),
-        [((rows, 2 * fanout), F32)],
-        [],
+        [((rows, 2 * fanout), F32), ((half, depth), BF), x_type, w1_type, w2_type, (w3t.shape, BF)],
+        [((rows, fanout), jnp.int32), ((rows, fanout), F32), ((1, rows), jnp.int32), 8],
         nbr_ids,
         nbr_weight,
         labels.reshape(1, rows),
-    )
+        features,
+        w_first,
+        w_second,
+        w3t,
+        limit=PACK,
+        far_in=range(7),
+    )
+    peer_half = over(my_half, 1)
     got = other_core(packed)
     packed = jnp.where(core == 0, jnp.concatenate([packed, got], 1), jnp.concatenate([got, packed], 1))
-    half = node_dev // 2
-    w1_type, w2_type, x_type = (w_first.shape, BF), (w_second.shape, BF), (features.shape, BF)
-    scores, my_half = whole(
+    (scores,) = whole(
         own_kernel,
-        [((classes, node_dev), BF), ((half, depth), BF)],
-        [x_type, w1_type, w2_type, (w3t.shape, BF), 4],
+        [((classes, node_dev), BF)],
+        [],
         features,
         w_first,
         w_second,
         w3t,
         packed,
         flops=2000000000,
-        limit=60,
-        far_in=range(5),
+        limit=16,
+        far_in=(4,),
     )
     for bit in bits:
         got = over(packed, bit)
@@ -312,10 +319,7 @@
             got, scores = lax.optimization_barrier((got, scores))
         up = (me // bit) % 2
         packed = jnp.where(up == 0, jnp.concatenate([packed, got], 0), jnp.concatenate([got, packed], 0))
-    far_packed = over(packed, 1)
     far_scores = over(scores, 1)
-    my_half, packed = lax.optimization_barrier((my_half, packed))
-    peer_half = over(my_half, 1)
 
     big = 24 if owners <= 8 else 48
     maps = [((2 * node_dev, targets), BF), ((2 * node_dev, targets), BF), ((1, targets), jnp.int32)]
@@ -332,13 +336,6 @@
         low,
         limit=big,
     )
-    far_high, far_low, _ = spread_call(far_packed)
-    for bit in bits[:-1]:
-        got = over(send, bit)
-        if bit == bits[0]:
-            got, far_high, far_low = lax.optimization_barrier((got, far_high, far_low))
-        part = part + got.astype(F32)
-        send = part.astype(BF)
     kept = [
         ((depth, node_dev), BF),
         ((hidden, node_dev), BF),
@@ -347,12 +344,23 @@
         ((node_dev, hidden), F32),
     ]
     work = [((node_dev, hidden), F32), ((node_dev, hidden), BF)]
+    packed = lax.optimization_barrier((packed, send))[0]
+    far_packed = over(packed, 1)
+    peer_half = lax.optimization_barrier((peer_half, send))[0]
+    peer_rest = other_core(peer_half)
     xt, h1t, h2, s1, s2 = whole(
         again_kernel, kept, work, features, w_first, w_second, send, flops=2000000000, far_in=(3,)
     )
+    for bit in bits[:-1]:
+        got = over(send, bit)
+        if bit == bits[0]:
+            got = lax.optimization_barrier((got, s1))[0]
+        part = part + got.astype(F32)
+        send = part.astype(BF)
+    far_packed = lax.optimization_barrier((far_packed, send))[0]
+    far_high, far_low, _ = spread_call(far_packed)
     got = over(send, bits[-1])
-    peer_half = lax.optimization_barrier((peer_half, got))[0]
-    peer_rest = other_core(peer_half)
+    peer_rest = lax.optimization_barrier((peer_rest, got))[0]
     pxt, ph1t, ph2, ps1, ps2 = whole(
         peer_kernel,
         kept,
@@ -363,7 +371,7 @@
         w_second,
         flops=2000000000,
     )
-    got = lax.optimization_barrier((got, s1))[0]
+    got = lax.optimization_barrier((got, far_high))[0]
     grad, grad_send, loss = whole(
         softmax_kernel,
         [((classes, targets), F32), ((classes, targets), BF), ((1, targets), F32)],
@@ -376,7 +384,7 @@
     target_loss = lax.dynamic_slice_in_dim(loss[0], at, rows, 0)
     far_grad = over(grad_send, 1)
 
-    step = ROW << len(bits)
+    step = ROW << (len(bits) - 1)
     stack = -(-(depth + hidden + classes) // step) * step
 
     def halves(n):
@@ -385,13 +393,13 @@
     send, keep = whole(
         functools.partial(back_kernel, bits[0]),
         halves(stack),
-        [((stack, LANE), F32), ((node_dev, hidden), F32)],
+        [((stack, LANE), F32), ((2, node_dev, hidden), BF)],
         grad, far_grad, high, low, far_high, far_low,
         xt, pxt, h1t, ph1t, h2, ph2, s1, ps1, s2, ps2, w3t, w_second,
         limit=big,
     )
     size = stack // 2
-    for at, bit in enumerate(bits[1:]):
+    for at, bit in enumerate(bits[1:-1]):
         send, keep = whole(
             functools.partial(add_kernel, bit),
             halves(size),
@@ -400,8 +408,11 @@
             over(send, bits[at]),
         )
         size //= 2
-    (out,) = whole(last_kernel, [((size, LANE), BF)], [], keep, over(send, bits[-1]))
-    for bit in reversed(bits[1:]):
+    for mine, bit in ((keep, bits[-2]), (None, bits[-1])):
+        got = over(send, bit)
+        (send,) = whole(sum_kernel, [((size, LANE), BF)], [], send if mine is None else mine, got)
+    out = send
+    for bit in reversed(bits[1:-1]):
         size *= 2
         (out,) = whole(functools.partial(join_kernel, bit), [((size, LANE), BF)], [], out, over(out, bit))
     pair = (out, over(out, bits[0]))

time: 73.2 us -> 65 us (0.89)
  waiting for transfers between devices: 32.8 us -> 23.3 us
  starting transfers between devices: 19 us -> 24.4 us
  local copies, waits for them, and re-layouts: 2.66 us -> 0.59 us
  Pallas kernels: 16.7 us -> 14.9 us
    ppermute x14 -> x13, waiting for transfers between devices: 31.1 us -> 22.5 us  [over(): return lax.ppermute(x, 'owner', [(i, i ^ bit) for i in range(owners)])]
    ppermute x14 -> x13, starting transfers between devices: 18 us -> 23.4 us  [over(): return lax.ppermute(x, 'owner', [(i, i ^ bit) for i in range(owners)])]
    unnamed x18 -> x4, local copies, waits for them, and re-layouts: 2.07 us -> 0.01 us
    pallas_call x13 -> x12, Pallas kernels: 16.7 us -> 14.9 us  [whole(): pl.pallas_call(kernel, out_shape=[jax.ShapeDtypeStruct(shape, kind) for s...]
    ppermute x6, waiting for transfers between devices: 1.67 us -> 0.84 us  [other_core(): return lax.ppermute(x, 'batch', [(0, 1), (1, 0)])]
  transfers between devices with their start and end apart: 20 -> 19, of which waited for: 12 -> 9; matrix products, arithmetic and copies ran while one was open for 1% -> 2% of each run, Pallas kernels for 16% -> 14%
where the time goes in v3:
time: 65 us; the launch traced here: 64.8 us
  starting transfers between devices  24.4 us (38%)
  waiting for transfers between devices  23.3 us (36%)
  Pallas kernels  14.9 us (23%)
  other arithmetic  0.87 us (1%)
  between operations  0.72 us (1%)
    ppermute x13, starting transfers between devices, over(): return lax.ppermute(x, 'owner', [(i, i ^ bit) for i in range(owners)])  23.4 us
    ppermute x13, waiting for transfers between devices, over(): return lax.ppermute(x, 'owner', [(i, i ^ bit) for i in range(owners)])  22.5 us
    pallas_call x12, Pallas kernels, whole(): pl.pallas_call(kernel, out_shape=[jax.ShapeDtypeStruct(shape, kind) for s...  14.9 us
  transfers between devices with their start and end apart: 19, of which 9 were waited for; matrix products, arithmetic and copies ran while one was open for 2% of the time, Pallas kernels for 14%

profile of v3, /device:TPU:0, one launch (start us, length us, event | category | flops | bytes accessed | tf_op | source)
XLA Modules:
  0.0 64.8 jit_solution(8246101970588144012)
XLA Ops:
  0.6 1.8 %shard_map.102 = (f32[16,64]{1,0:T(8,128)S(1)}, bf16[256,768]{1,0:T(8,128)(2,1)S(1)}, bf16[512,768]{1,0:T(8,128)(2,1)S(1)}, bf16[768,512]{1,0:T(8,128)(2,1)S(1)}...) custom-call(s32[16,32]{1,0:T(8,128)} %ids_hbm.1, f32[16,32]{1,0:T(8,128)} %wts_hbm.1, s32[1,16]{1,0:T(1,128)} %bitcast.6, ...), custom_call_target="tpu_custom_call" | custom-call | flops 1000000 | bytes 1953 | tf_op jit(solution)/shard_map/pallas_call | solution.py:253
  2.9 2.6 %collective-permute-start.8 = (bf16[256,768]{1,0:T(8,128)(2,1)S(1)}, bf16[256,768]{1,0:T(8,128)(2,1)S(1)}, u32[]{:S(2)}, u32[]{:S(2)}) collective-permute-start(bf16[256,768]{1,0:T(8,128)(2,1)S(1)} %get-tuple-element.65), channel_id=1, source_target_pairs={{0,2},{2,0},{4,6},{6,4},{8,10},{10,8},{12,14},{14,12},{1,3},{3,1},... | collective-permute-start | bytes 1179656 | tf_op jit(solution)/shard_map/ppermute | solution.py:278
  5.6 1.6 %collective-permute-start.1 = (f32[16,128]{1,0:T(8,128)S(1)}, f32[16,128]{1,0:T(8,128)S(1)}, u32[]{:S(2)}, u32[]{:S(2)}) collective-permute-start(f32[16,128]{1,0:T(8,128)S(1)} %maximum_select_fusion.2.after), channel_id=1, source_target_pairs={{0,4},{2,6},{4,0},{6,2},{8,12},{10,14},{12,8},{14,10},{1,5},{3,7},... | collective-permute-start | bytes 24584 | tf_op jit(solution)/shard_map/ppermute | solution.py:278
  7.2 1.2 %shard_map.103.mine = bf16[153,512]{1,0:T(8,128)(2,1)S(1)} custom-call(bf16[512,768]{1,0:T(8,128)(2,1)S(1)} %get-tuple-element.44.x, bf16[768,512]{1,0:T(8,128)(2,1)S(1)} %get-tuple-element.45.w1, bf16[512,512]{1,0:T(8,128)(2,1)S(1)} %get-tuple-element.46.w2, bf16[153,512]{1,0:T(8,128)(2,1)S(1)} %get-tuple-element.47.w3.w3t, f32[16,128]{1,0:T(8,128)} %copy-done.1), custom_call_target="tpu_custom_call" | custom-call | flops 2000000000 | bytes 3906250 | tf_op jit(solution)/shard_map/pallas_call | solution.py:253
  10.0 2.6 %collective-permute-start.3 = (f32[32,128]{1,0:T(8,128)S(1)}, f32[32,128]{1,0:T(8,128)S(1)}, u32[]{:S(2)}, u32[]{:S(2)}) collective-permute-start(f32[32,128]{1,0:T(8,128)S(1)} %maximum_select_fusion.1), channel_id=1, source_target_pairs={{0,8},{2,10},{4,12},{6,14},{8,0},{10,2},{12,4},{14,6},{1,9},{3,11}... | collective-permute-start | bytes 49160 | tf_op jit(solution)/shard_map/ppermute | solution.py:278
  14.7 2.0 %shard_map.104 = (bf16[1024,128]{1,0:T(8,128)(2,1)S(1)}, bf16[1024,128]{1,0:T(8,128)(2,1)S(1)}, s32[1,128]{1,0:T(1,128)S(1)}) custom-call(f32[64,128]{1,0:T(8,128)S(1)} %maximum_select_fusion.packed), custom_call_target="tpu_custom_call" | custom-call | flops 1000000000 | bytes 1953125 | tf_op jit(solution)/shard_map/pallas_call | solution.py:253
  16.7 2.0 %collective-permute-done.2.theirs = bf16[153,512]{1,0:T(8,128)(2,1)S(1)} collective-permute-done((bf16[153,512]{1,0:T(8,128)(2,1)S(1)}, bf16[153,512]{1,0:T(8,128)(2,1)S(1)}, u32[]{:S(2)}, u32[]{:S(2)}) %collective-permute-start.2) | collective-permute-done | bytes 156704 | tf_op jit(solution)/shard_map/ppermute | solution.py:278
  19.1 1.9 %collective-permute-start.4 = (bf16[153,128]{1,0:T(8,128)(2,1)S(1)}, bf16[153,128]{1,0:T(8,128)(2,1)S(1)}, u32[]{:S(2)}, u32[]{:S(2)}) collective-permute-start(bf16[153,128]{1,0:T(8,128)(2,1)S(1)} %get-tuple-element.53.after), channel_id=1, source_target_pairs={{0,4},{2,6},{4,0},{6,2},{8,12},{10,14},{12,8},{14,10},{1,5},{3,7},... | collective-permute-start | bytes 117512 | tf_op jit(solution)/shard_map/ppermute | solution.py:278
  21.0 1.4 %shard_map.106 = (bf16[768,512]{1,0:T(8,128)(2,1)S(1)}, bf16[512,512]{1,0:T(8,128)(2,1)S(1)}, bf16[512,128]{1,0:T(8,128)(2,1)S(1)}, f32[512,128]{1,0:T(8,128)S(1)}, f32[512,512]{1,0:T(8,128)S(1)}) custom-call(bf16[512,768]{1,0:T(8,128)(2,1)S(1)} %get-tuple-element.44.x, bf16[768,512]{1,0:T(8,128)(2,1)S(1)} %get-tuple-element.45.w1, ...), custom_call_target="tpu_custom_call" | custom-call | flops 2000000000 | bytes 3906250 | tf_op jit(solution)/shard_map/pallas_call | solution.py:253
  22.4 1.6 %collective-permute-start.6 = (f32[64,128]{1,0:T(8,128)S(1)}, f32[64,128]{1,0:T(8,128)S(1)}, u32[]{:S(2)}, u32[]{:S(2)}) collective-permute-start(f32[64,128]{1,0:T(8,128)S(1)} %maximum_select_fusion.packed), channel_id=1, source_target_pairs={{0,2},{2,0},{4,6},{6,4},{8,10},{10,8},{12,14},{14,12},{1,3},{3,1},... | collective-permute-start | bytes 98312 | tf_op jit(solution)/shard_map/ppermute | solution.py:278
  24.0 2.7 %collective-permute-start.5 = (bf16[153,128]{1,0:T(8,128)(2,1)S(1)}, bf16[153,128]{1,0:T(8,128)(2,1)S(1)}, u32[]{:S(2)}, u32[]{:S(2)}) collective-permute-start(bf16[153,128]{1,0:T(8,128)(2,1)S(1)} %get-tuple-element.82), channel_id=1, source_target_pairs={{0,8},{2,10},{4,12},{6,14},{8,0},{10,2},{12,4},{14,6},{1,9},{3,11}... | collective-permute-start | bytes 117512 | tf_op jit(solution)/shard_map/ppermute | solution.py:278
  26.7 2.4 %shard_map.107 = (bf16[1024,128]{1,0:T(8,128)(2,1)S(1)}, bf16[1024,128]{1,0:T(8,128)(2,1)S(1)}, s32[1,128]{1,0:T(1,128)}) custom-call(f32[64,128]{1,0:T(8,128)S(1)} %collective-permute-done.6.packed), custom_call_target="tpu_custom_call" | custom-call | flops 1000000000 | bytes 1953125 | tf_op jit(solution)/shard_map/pallas_call | solution.py:253
  29.2 1.3 %collective-permute-start.7 = (bf16[153,128]{1,0:T(8,128)(2,1)S(1)}, bf16[153,128]{1,0:T(8,128)(2,1)S(1)}, u32[]{:S(2)}, u32[]{:S(2)}) collective-permute-start(bf16[153,128]{1,0:T(8,128)(2,1)S(1)} %get-tuple-element.62), channel_id=1, source_target_pairs={{0,2},{2,0},{4,6},{6,4},{8,10},{10,8},{12,14},{14,12},{1,3},{3,1},... | collective-permute-start | bytes 117512 | tf_op jit(solution)/shard_map/ppermute | solution.py:278
  30.5 1.5 %shard_map.109 = (bf16[768,512]{1,0:T(8,128)(2,1)S(1)}, bf16[512,512]{1,0:T(8,128)(2,1)S(1)}, bf16[512,128]{1,0:T(8,128)(2,1)S(1)}, f32[512,128]{1,0:T(8,128)S(1)}, f32[512,512]{1,0:T(8,128)S(1)}) custom-call(bf16[256,768]{1,0:T(8,128)(2,1)S(1)} %collective-permute-done.8.mine, bf16[256,768]{1,0:T(8,128)(2,1)S(1)} %collective-permute-done.9.theirs, ...), custom_call_target="tpu_custom_call" | custom-call | flops 2000000000 | bytes 3906250 | tf_op jit(solution)/shard_map/pallas_call | solution.py:253
  32.0 1.3 %collective-permute-done.7.far_grad = bf16[153,128]{1,0:T(8,128)(2,1)S(1)} collective-permute-done((bf16[153,128]{1,0:T(8,128)(2,1)S(1)}, bf16[153,128]{1,0:T(8,128)(2,1)S(1)}, u32[]{:S(2)}, u32[]{:S(2)}) %collective-permute-start.7) | collective-permute-done | bytes 39200 | tf_op jit(solution)/shard_map/ppermute | solution.py:278
  33.3 2.7 %shard_map.110 = (bf16[720,128]{1,0:T(8,128)(2,1)S(1)}, f32[720,128]{1,0:T(8,128)S(1)}) custom-call(f32[153,128]{1,0:T(8,128)S(1)} %get-tuple-element.61.grad, bf16[153,128]{1,0:T(8,128)(2,1)S(1)} %collective-permute-done.7.far_grad, bf16[1024,128]{1,0:T(8,128)(2,1)S(1)} %get-tuple-element.50.high, bf16[1024,128]{1,0:T(8,128)(2,1)S(1)} %get-tuple-element.51.low, ...), custom_call_target="tpu_custom_call" | custom-call | flops 1000000 | bytes 1953 | tf_op jit(solution)/shard_map/pallas_call | solution.py:253
  37.0 4.6 %collective-permute-done.10.got = bf16[720,128]{1,0:T(8,128)(2,1)S(1)} collective-permute-done((bf16[720,128]{1,0:T(8,128)(2,1)S(1)}, bf16[720,128]{1,0:T(8,128)(2,1)S(1)}, u32[]{:S(2)}, u32[]{:S(2)}) %collective-permute-start.10) | collective-permute-done | bytes 184352 | tf_op jit(solution)/shard_map/ppermute | solution.py:278
  41.6 3.2 %collective-permute-start.11 = (bf16[720,128]{1,0:T(8,128)(2,1)S(1)}, bf16[720,128]{1,0:T(8,128)(2,1)S(1)}, u32[]{:S(2)}, u32[]{:S(2)}) collective-permute-start(bf16[720,128]{1,0:T(8,128)(2,1)S(1)} %shard_map.111.kept), channel_id=1, source_target_pairs={{0,8},{2,10},{4,12},{6,14},{8,0},{10,2},{12,4},{14,6},{1,9},{3,11}... | collective-permute-start | bytes 552968 | tf_op jit(solution)/shard_map/ppermute | solution.py:278
  44.8 6.0 %collective-permute-done.11.got = bf16[720,128]{1,0:T(8,128)(2,1)S(1)} collective-permute-done((bf16[720,128]{1,0:T(8,128)(2,1)S(1)}, bf16[720,128]{1,0:T(8,128)(2,1)S(1)}, u32[]{:S(2)}, u32[]{:S(2)}) %collective-permute-start.11) | collective-permute-done | bytes 184352 | tf_op jit(solution)/shard_map/ppermute | solution.py:278
  51.5 1.3 %collective-permute-start.13 = (bf16[720,128]{1,0:T(8,128)(2,1)S(1)}, bf16[720,128]{1,0:T(8,128)(2,1)S(1)}, u32[]{:S(2)}, u32[]{:S(2)}) collective-permute-start(bf16[720,128]{1,0:T(8,128)(2,1)S(1)} %shard_map.112.refs_0_), channel_id=1, source_target_pairs={{0,2},{2,0},{4,6},{6,4},{8,10},{10,8},{12,14},{14,12},{1,3},{3,1},... | collective-permute-start | bytes 552968 | tf_op jit(solution)/shard_map/ppermute | solution.py:278
  52.8 3.6 %collective-permute-done.12.refs_1_ = bf16[720,128]{1,0:T(8,128)(2,1)S(1)} collective-permute-done((bf16[720,128]{1,0:T(8,128)(2,1)S(1)}, bf16[720,128]{1,0:T(8,128)(2,1)S(1)}, u32[]{:S(2)}, u32[]{:S(2)}) %collective-permute-start.12) | collective-permute-done | bytes 184352 | tf_op jit(solution)/shard_map/ppermute | solution.py:278
  56.5 1.8 %collective-permute-start.14 = (bf16[720,128]{1,0:T(8,128)(2,1)S(1)}, bf16[720,128]{1,0:T(8,128)(2,1)S(1)}, u32[]{:S(2)}, u32[]{:S(2)}) collective-permute-start(bf16[720,128]{1,0:T(8,128)(2,1)S(1)} %collective-permute-done.12.refs_1_), channel_id=1, source_target_pairs={{0,2},{2,0},{4,6},{6,4},{8,10},{10,8},{12,14},{14,12},{1,3},{3,1},... | collective-permute-start | bytes 552968 | tf_op jit(solution)/shard_map/ppermute | solution.py:278
  58.8 3.2 %collective-permute-done.14.refs_3_ = bf16[720,128]{1,0:T(8,128)(2,1)S(1)} collective-permute-done((bf16[720,128]{1,0:T(8,128)(2,1)S(1)}, bf16[720,128]{1,0:T(8,128)(2,1)S(1)}, u32[]{:S(2)}, u32[]{:S(2)}) %collective-permute-start.14) | collective-permute-done | bytes 184352 | tf_op jit(solution)/shard_map/ppermute | solution.py:278
  63.4 1.4 %shard_map.113 = (bf16[768,512]{1,0:T(8,128)(2,1)}, bf16[512,512]{1,0:T(8,128)(2,1)}, bf16[153,512]{1,0:T(8,128)(2,1)}) custom-call(bf16[720,128]{1,0:T(8,128)(2,1)S(1)} %shard_map.112.refs_0_, bf16[720,128]{1,0:T(8,128)(2,1)S(1)} %collective-permute-done.12.refs_1_, bf16[720,128]{1,0:T(8,128)(2,1)S(1)} %collective-permute-done.13.refs_2_, ...), custom_call_target="tpu_custom_call" | custom-call | flops 1000000 | bytes 1953 | tf_op jit(solution)/shard_map/pallas_call | solution.py:253
  (35 shorter events, 8.4 us)
Async XLA Ops:
  2.4 3.1 %collective-permute-start = (f32[16,64]{1,0:T(8,128)S(1)}, f32[16,64]{1,0:T(8,128)S(1)}, u32[]{:S(2)}, u32[]{:S(2)}) collective-permute-start(f32[16,64]{1,0:T(8,128)S(1)} %get-tuple-element.43), channel_id=1, source_target_pairs={{0,1},{1,0},{2,3},{3,2},{4,5},{5,4},{6,7},{7,6},{8,9},{9,8},{10,11... | collective-permute-start | bytes 12296 | tf_op jit(solution)/shard_map/ppermute | solution.py:281
  2.9 18.0 %collective-permute-start.8 = (bf16[256,768]{1,0:T(8,128)(2,1)S(1)}, bf16[256,768]{1,0:T(8,128)(2,1)S(1)}, u32[]{:S(2)}, u32[]{:S(2)}) collective-permute-start(bf16[256,768]{1,0:T(8,128)(2,1)S(1)} %get-tuple-element.65), channel_id=1, source_target_pairs={{0,2},{2,0},{4,6},{6,4},{8,10},{10,8},{12,14},{14,12},{1,3},{3,1},... | collective-permute-start | bytes 1179656 | tf_op jit(solution)/shard_map/ppermute | solution.py:278
  5.6 1.6 %copy-start.1 = (f32[16,128]{1,0:T(8,128)}, f32[16,128]{1,0:T(8,128)S(1)}, u32[]{:S(2)}) copy-start(f32[16,128]{1,0:T(8,128)S(1)} %maximum_select_fusion.2.after) | copy-start | bytes 24580
  5.6 3.7 %collective-permute-start.1 = (f32[16,128]{1,0:T(8,128)S(1)}, f32[16,128]{1,0:T(8,128)S(1)}, u32[]{:S(2)}, u32[]{:S(2)}) collective-permute-start(f32[16,128]{1,0:T(8,128)S(1)} %maximum_select_fusion.2.after), channel_id=1, source_target_pairs={{0,4},{2,6},{4,0},{6,2},{8,12},{10,14},{12,8},{14,10},{1,5},{3,7},... | collective-permute-start | bytes 24584 | tf_op jit(solution)/shard_map/ppermute | solution.py:278
  10.0 4.6 %collective-permute-start.3 = (f32[32,128]{1,0:T(8,128)S(1)}, f32[32,128]{1,0:T(8,128)S(1)}, u32[]{:S(2)}, u32[]{:S(2)}) collective-permute-start(f32[32,128]{1,0:T(8,128)S(1)} %maximum_select_fusion.1), channel_id=1, source_target_pairs={{0,8},{2,10},{4,12},{6,14},{8,0},{10,2},{12,4},{14,6},{1,9},{3,11}... | collective-permute-start | bytes 49160 | tf_op jit(solution)/shard_map/ppermute | solution.py:278
  12.6 6.1 %collective-permute-start.2 = (bf16[153,512]{1,0:T(8,128)(2,1)S(1)}, bf16[153,512]{1,0:T(8,128)(2,1)S(1)}, u32[]{:S(2)}, u32[]{:S(2)}) collective-permute-start(bf16[153,512]{1,0:T(8,128)(2,1)S(1)} %shard_map.103.mine), channel_id=1, source_target_pairs={{0,2},{2,0},{4,6},{6,4},{8,10},{10,8},{12,14},{14,12},{1,3},{3,1},... | collective-permute-start | bytes 470024 | tf_op jit(solution)/shard_map/ppermute | solution.py:278
  19.1 1.9 %copy-start = (bf16[153,128]{1,0:T(8,128)(2,1)}, bf16[153,128]{1,0:T(8,128)(2,1)S(1)}, u32[]{:S(2)}) copy-start(bf16[153,128]{1,0:T(8,128)(2,1)S(1)} %get-tuple-element.53.after) | copy-start | bytes 117508
  19.1 5.0 %collective-permute-start.4 = (bf16[153,128]{1,0:T(8,128)(2,1)S(1)}, bf16[153,128]{1,0:T(8,128)(2,1)S(1)}, u32[]{:S(2)}, u32[]{:S(2)}) collective-permute-start(bf16[153,128]{1,0:T(8,128)(2,1)S(1)} %get-tuple-element.53.after), channel_id=1, source_target_pairs={{0,4},{2,6},{4,0},{6,2},{8,12},{10,14},{12,8},{14,10},{1,5},{3,7},... | collective-permute-start | bytes 117512 | tf_op jit(solution)/shard_map/ppermute | solution.py:278
  21.0 9.5 %collective-permute-start.9 = (bf16[256,768]{1,0:T(8,128)(2,1)S(1)}, bf16[256,768]{1,0:T(8,128)(2,1)S(1)}, u32[]{:S(2)}, u32[]{:S(2)}) collective-permute-start(bf16[256,768]{1,0:T(8,128)(2,1)S(1)} %collective-permute-done.8.mine), channel_id=1, source_target_pairs={{0,1},{1,0},{2,3},{3,2},{4,5},{5,4},{6,7},{7,6},{8,9},{9,8},{10,11... | collective-permute-start | bytes 1179656 | tf_op jit(solution)/shard_map/ppermute | solution.py:281
  22.4 4.3 %collective-permute-start.6 = (f32[64,128]{1,0:T(8,128)S(1)}, f32[64,128]{1,0:T(8,128)S(1)}, u32[]{:S(2)}, u32[]{:S(2)}) collective-permute-start(f32[64,128]{1,0:T(8,128)S(1)} %maximum_select_fusion.packed), channel_id=1, source_target_pairs={{0,2},{2,0},{4,6},{6,4},{8,10},{10,8},{12,14},{14,12},{1,3},{3,1},... | collective-permute-start | bytes 98312 | tf_op jit(solution)/shard_map/ppermute | solution.py:278
  24.0 5.1 %collective-permute-start.5 = (bf16[153,128]{1,0:T(8,128)(2,1)S(1)}, bf16[153,128]{1,0:T(8,128)(2,1)S(1)}, u32[]{:S(2)}, u32[]{:S(2)}) collective-permute-start(bf16[153,128]{1,0:T(8,128)(2,1)S(1)} %get-tuple-element.82), channel_id=1, source_target_pairs={{0,8},{2,10},{4,12},{6,14},{8,0},{10,2},{12,4},{14,6},{1,9},{3,11}... | collective-permute-start | bytes 117512 | tf_op jit(solution)/shard_map/ppermute | solution.py:278
  29.2 4.1 %collective-permute-start.7 = (bf16[153,128]{1,0:T(8,128)(2,1)S(1)}, bf16[153,128]{1,0:T(8,128)(2,1)S(1)}, u32[]{:S(2)}, u32[]{:S(2)}) collective-permute-start(bf16[153,128]{1,0:T(8,128)(2,1)S(1)} %get-tuple-element.62), channel_id=1, source_target_pairs={{0,2},{2,0},{4,6},{6,4},{8,10},{10,8},{12,14},{14,12},{1,3},{3,1},... | collective-permute-start | bytes 117512 | tf_op jit(solution)/shard_map/ppermute | solution.py:278
  36.0 5.6 %collective-permute-start.10 = (bf16[720,128]{1,0:T(8,128)(2,1)S(1)}, bf16[720,128]{1,0:T(8,128)(2,1)S(1)}, u32[]{:S(2)}, u32[]{:S(2)}) collective-permute-start(bf16[720,128]{1,0:T(8,128)(2,1)S(1)} %get-tuple-element.77), channel_id=1, source_target_pairs={{0,4},{2,6},{4,0},{6,2},{8,12},{10,14},{12,8},{14,10},{1,5},{3,7},... | collective-permute-start | bytes 552968 | tf_op jit(solution)/shard_map/ppermute | solution.py:278
  41.6 9.2 %collective-permute-start.11 = (bf16[720,128]{1,0:T(8,128)(2,1)S(1)}, bf16[720,128]{1,0:T(8,128)(2,1)S(1)}, u32[]{:S(2)}, u32[]{:S(2)}) collective-permute-start(bf16[720,128]{1,0:T(8,128)(2,1)S(1)} %shard_map.111.kept), channel_id=1, source_target_pairs={{0,8},{2,10},{4,12},{6,14},{8,0},{10,2},{12,4},{14,6},{1,9},{3,11}... | collective-permute-start | bytes 552968 | tf_op jit(solution)/shard_map/ppermute | solution.py:278
  50.9 5.6 %collective-permute-start.12 = (bf16[720,128]{1,0:T(8,128)(2,1)S(1)}, bf16[720,128]{1,0:T(8,128)(2,1)S(1)}, u32[]{:S(2)}, u32[]{:S(2)}) collective-permute-start(bf16[720,128]{1,0:T(8,128)(2,1)S(1)} %shard_map.112.refs_0_), channel_id=1, source_target_pairs={{0,4},{2,6},{4,0},{6,2},{8,12},{10,14},{12,8},{14,10},{1,5},{3,7},... | collective-permute-start | bytes 552968 | tf_op jit(solution)/shard_map/ppermute | solution.py:278
  51.5 7.3 %collective-permute-start.13 = (bf16[720,128]{1,0:T(8,128)(2,1)S(1)}, bf16[720,128]{1,0:T(8,128)(2,1)S(1)}, u32[]{:S(2)}, u32[]{:S(2)}) collective-permute-start(bf16[720,128]{1,0:T(8,128)(2,1)S(1)} %shard_map.112.refs_0_), channel_id=1, source_target_pairs={{0,2},{2,0},{4,6},{6,4},{8,10},{10,8},{12,14},{14,12},{1,3},{3,1},... | collective-permute-start | bytes 552968 | tf_op jit(solution)/shard_map/ppermute | solution.py:278
  56.5 5.5 %collective-permute-start.14 = (bf16[720,128]{1,0:T(8,128)(2,1)S(1)}, bf16[720,128]{1,0:T(8,128)(2,1)S(1)}, u32[]{:S(2)}, u32[]{:S(2)}) collective-permute-start(bf16[720,128]{1,0:T(8,128)(2,1)S(1)} %collective-permute-done.12.refs_1_), channel_id=1, source_target_pairs={{0,2},{2,0},{4,6},{6,4},{8,10},{10,8},{12,14},{14,12},{1,3},{3,1},... | collective-permute-start | bytes 552968 | tf_op jit(solution)/shard_map/ppermute | solution.py:278
  58.3 4.3 %collective-permute-start.15 = (bf16[720,128]{1,0:T(8,128)(2,1)S(1)}, bf16[720,128]{1,0:T(8,128)(2,1)S(1)}, u32[]{:S(2)}, u32[]{:S(2)}) collective-permute-start(bf16[720,128]{1,0:T(8,128)(2,1)S(1)} %shard_map.112.refs_0_), channel_id=1, source_target_pairs={{0,1},{1,0},{2,3},{3,2},{4,5},{5,4},{6,7},{7,6},{8,9},{9,8},{10,11... | collective-permute-start | bytes 552968 | tf_op jit(solution)/shard_map/ppermute | solution.py:281
  58.3 4.3 %collective-permute-start.16 = (bf16[720,128]{1,0:T(8,128)(2,1)S(1)}, bf16[720,128]{1,0:T(8,128)(2,1)S(1)}, u32[]{:S(2)}, u32[]{:S(2)}) collective-permute-start(bf16[720,128]{1,0:T(8,128)(2,1)S(1)} %collective-permute-done.12.refs_1_), channel_id=1, source_target_pairs={{0,1},{1,0},{2,3},{3,2},{4,5},{5,4},{6,7},{7,6},{8,9},{9,8},{10,11... | collective-permute-start | bytes 552968 | tf_op jit(solution)/shard_map/ppermute | solution.py:281
  58.8 3.8 %collective-permute-start.17 = (bf16[720,128]{1,0:T(8,128)(2,1)S(1)}, bf16[720,128]{1,0:T(8,128)(2,1)S(1)}, u32[]{:S(2)}, u32[]{:S(2)}) collective-permute-start(bf16[720,128]{1,0:T(8,128)(2,1)S(1)} %collective-permute-done.13.refs_2_), channel_id=1, source_target_pairs={{0,1},{1,0},{2,3},{3,2},{4,5},{5,4},{6,7},{7,6},{8,9},{9,8},{10,11... | collective-permute-start | bytes 552968 | tf_op jit(solution)/shard_map/ppermute | solution.py:281
  62.0 1.4 %collective-permute-start.18 = (bf16[720,128]{1,0:T(8,128)(2,1)S(1)}, bf16[720,128]{1,0:T(8,128)(2,1)S(1)}, u32[]{:S(2)}, u32[]{:S(2)}) collective-permute-start(bf16[720,128]{1,0:T(8,128)(2,1)S(1)} %collective-permute-done.14.refs_3_), channel_id=1, source_target_pairs={{0,1},{1,0},{2,3},{3,2},{4,5},{5,4},{6,7},{7,6},{8,9},{9,8},{10,11... | collective-permute-start | bytes 552968 | tf_op jit(solution)/shard_map/ppermute | solution.py:281

commit v4 on v3

--- a/solution.py
+++ b/solution.py
@@ -43,12 +43,11 @@
     return copies
 
 
-def pack_kernel(nodes, ids_hbm, wts_hbm, labels_hbm, x_hbm, w1_hbm, w2_hbm, w3_hbm, out, half, x, w1, w2, w3, ids, wts, labels, sem):
+def pack_kernel(nodes, ids_hbm, wts_hbm, labels_hbm, x_hbm, out, half, ids, wts, labels, sem):
     rows, fanout = ids.shape
     part = half.shape[0]
     mine = x_hbm.at[pl.ds(pl.multiple_of(lax.axis_index("batch") * part, ROW), part), :]
-    small = ((labels_hbm, labels), (ids_hbm, ids), (wts_hbm, wts))
-    into = launch(sem, small + ((mine, half), (x_hbm, x), (w1_hbm, w1), (w2_hbm, w2), (w3_hbm, w3)))
+    into = launch(sem, ((labels_hbm, labels), (ids_hbm, ids), (wts_hbm, wts), (mine, half)))
     for c in into[:3]:
         c.wait()
     shape = (rows, rows)
@@ -56,7 +55,13 @@
     label = jnp.sum(jnp.where(same, labels[...].astype(F32), 0.0), axis=1, keepdims=True)
     out[:, :fanout] = ids[...].astype(F32) + label * nodes
     out[:, fanout:] = wts[...]
-    for c in into[3:]:
+    into[3].wait()
+
+
+def load_kernel(after, *refs):
+    del after
+    count = len(refs) // 2
+    for c in launch(refs[-1], tuple(zip(refs[:count], refs[count:-1]))):
         c.wait()
 
 
@@ -283,23 +288,32 @@
     w3t = w_third.T
     half = node_dev // 2
     w1_type, w2_type, x_type = (w_first.shape, BF), (w_second.shape, BF), (features.shape, BF)
-    packed, my_half, features, w_first, w_second, w3t = whole(
+    packed, my_half = whole(
         functools.partial(pack_kernel, nodes),
-        [((rows, 2 * fanout), F32), ((half, depth), BF), x_type, w1_type, w2_type, (w3t.shape, BF)],
-        [((rows, fanout), jnp.int32), ((rows, fanout), F32), ((1, rows), jnp.int32), 8],
+        [((rows, 2 * fanout), F32), ((half, depth), BF)],
+        [((rows, fanout), jnp.int32), ((rows, fanout), F32), ((1, rows), jnp.int32), 4],
         nbr_ids,
         nbr_weight,
         labels.reshape(1, rows),
+        features,
+        limit=PACK,
+        far_in=range(4),
+    )
+    peer_half = over(my_half, 1)
+    got = other_core(packed)
+    packed = jnp.where(core == 0, jnp.concatenate([packed, got], 1), jnp.concatenate([got, packed], 1))
+    features, w_first, w_second, w3t = whole(
+        load_kernel,
+        [x_type, w1_type, w2_type, (w3t.shape, BF)],
+        [4],
+        packed,
         features,
         w_first,
         w_second,
         w3t,
         limit=PACK,
-        far_in=range(7),
-    )
-    peer_half = over(my_half, 1)
-    got = other_core(packed)
-    packed = jnp.where(core == 0, jnp.concatenate([packed, got], 1), jnp.concatenate([got, packed], 1))
+        far_in=range(1, 5),
+    )
     (scores,) = whole(
         own_kernel,
         [((classes, node_dev), BF)],
@@ -311,7 +325,6 @@
         packed,
         flops=2000000000,
         limit=16,
-        far_in=(4,),
     )
     for bit in bits:
         got = over(packed, bit)
@@ -349,7 +362,7 @@
     peer_half = lax.optimization_barrier((peer_half, send))[0]
     peer_rest = other_core(peer_half)
     xt, h1t, h2, s1, s2 = whole(
-        again_kernel, kept, work, features, w_first, w_second, send, flops=2000000000, far_in=(3,)
+        again_kernel, kept, work, features, w_first, w_second, send, flops=2000000000
     )
     for bit in bits[:-1]:
         got = over(send, bit)

time: 65 us -> 64.2 us (0.988)
  Pallas kernels: 14.9 us -> 15.8 us
  waiting for transfers between devices: 23.3 us -> 22.5 us
  other arithmetic: 0.87 us -> 0.1 us
    pallas_call x12 -> x13, Pallas kernels: 14.9 us -> 15.8 us  [whole(): pl.pallas_call(kernel, out_shape=[jax.ShapeDtypeStruct(shape, kind) for s...]
    ppermute x13, waiting for transfers between devices: 22.5 us -> 21.6 us  [over(): return lax.ppermute(x, 'owner', [(i, i ^ bit) for i in range(owners)])]
    select_n x2, other arithmetic: 0.78 us -> 0.01 us  [body(): jnp.where(up == 0, jnp.concatenate([packed, got], 0), jnp.concatenate([go...]
  transfers between devices with their start and end apart: 19 -> 19, of which waited for: 9 -> 8; matrix products, arithmetic and copies ran while one was open for 2% -> 1% of each run, Pallas kernels for 14% -> 16%
where the time goes in v4:
time: 64.2 us; the launch traced here: 64.1 us
  starting transfers between devices  24.4 us (38%)
  waiting for transfers between devices  22.5 us (35%)
  Pallas kernels  15.8 us (25%)
  between operations  0.73 us (1%)
    ppermute x13, starting transfers between devices, over(): return lax.ppermute(x, 'owner', [(i, i ^ bit) for i in range(owners)])  23.4 us
    ppermute x13, waiting for transfers between devices, over(): return lax.ppermute(x, 'owner', [(i, i ^ bit) for i in range(owners)])  21.6 us
    pallas_call x13, Pallas kernels, whole(): pl.pallas_call(kernel, out_shape=[jax.ShapeDtypeStruct(shape, kind) for s...  15.8 us
  transfers between devices with their start and end apart: 19, of which 8 were waited for; matrix products, arithmetic and copies ran while one was open for 1% of the time, Pallas kernels for 16%

profile of v4, /device:TPU:0, one launch (start us, length us, event | category | flops | bytes accessed | tf_op | source)
XLA Modules:
  0.0 64.1 jit_solution(239525150909357630)
XLA Ops:
  2.2 2.6 %collective-permute-start.8 = (bf16[256,768]{1,0:T(8,128)(2,1)S(1)}, bf16[256,768]{1,0:T(8,128)(2,1)S(1)}, u32[]{:S(2)}, u32[]{:S(2)}) collective-permute-start(bf16[256,768]{1,0:T(8,128)(2,1)S(1)} %get-tuple-element.65), channel_id=1, source_target_pairs={{0,2},{2,0},{4,6},{6,4},{8,10},{10,8},{12,14},{14,12},{1,3},{3,1},... | collective-permute-start | bytes 1179656 | tf_op jit(solution)/shard_map/ppermute | solution.py:283
  4.9 1.6 %collective-permute-start.1 = (f32[16,128]{1,0:T(8,128)S(1)}, f32[16,128]{1,0:T(8,128)S(1)}, u32[]{:S(2)}, u32[]{:S(2)}) collective-permute-start(f32[16,128]{1,0:T(8,128)S(1)} %maximum_select_fusion.2.after), channel_id=1, source_target_pairs={{0,4},{2,6},{4,0},{6,2},{8,12},{10,14},{12,8},{14,10},{1,5},{3,7},... | collective-permute-start | bytes 24584 | tf_op jit(solution)/shard_map/ppermute | solution.py:283
  6.5 1.6 %shard_map.103 = (bf16[512,768]{1,0:T(8,128)(2,1)S(1)}, bf16[768,512]{1,0:T(8,128)(2,1)S(1)}, bf16[512,512]{1,0:T(8,128)(2,1)S(1)}, bf16[153,512]{1,0:T(8,128)(2,1)S(1)}) custom-call(f32[16,128]{1,0:T(8,128)S(1)} %maximum_select_fusion.2.after, bf16[512,768]{1,0:T(8,128)(2,1)} %refs_0_.1, bf16[768,512]{1,0:T(8,128)(2,1)} %refs_1_.1, ...), custom_call_target="tpu_custom_call" | custom-call | flops 1000000 | bytes 1953 | tf_op jit(solution)/shard_map/pallas_call | solution.py:258
  8.0 1.2 %shard_map.104.mine = bf16[153,512]{1,0:T(8,128)(2,1)S(1)} custom-call(bf16[512,768]{1,0:T(8,128)(2,1)S(1)} %get-tuple-element.44.x, bf16[768,512]{1,0:T(8,128)(2,1)S(1)} %get-tuple-element.45.w1, bf16[512,512]{1,0:T(8,128)(2,1)S(1)} %get-tuple-element.46.w2, bf16[153,512]{1,0:T(8,128)(2,1)S(1)} %get-tuple-element.47.w3.w3t, ...), custom_call_target="tpu_custom_call" | custom-call | flops 2000000000 | bytes 3906250 | tf_op jit(solution)/shard_map/pallas_call | solution.py:258
  9.3 2.7 %collective-permute-start.3 = (f32[32,128]{1,0:T(8,128)S(1)}, f32[32,128]{1,0:T(8,128)S(1)}, u32[]{:S(2)}, u32[]{:S(2)}) collective-permute-start(f32[32,128]{1,0:T(8,128)S(1)} %maximum_select_fusion.1), channel_id=1, source_target_pairs={{0,8},{2,10},{4,12},{6,14},{8,0},{10,2},{12,4},{14,6},{1,9},{3,11}... | collective-permute-start | bytes 49160 | tf_op jit(solution)/shard_map/ppermute | solution.py:283
  14.0 2.0 %shard_map.105 = (bf16[1024,128]{1,0:T(8,128)(2,1)S(1)}, bf16[1024,128]{1,0:T(8,128)(2,1)S(1)}, s32[1,128]{1,0:T(1,128)S(1)}) custom-call(f32[64,128]{1,0:T(8,128)S(1)} %maximum_select_fusion.packed), custom_call_target="tpu_custom_call" | custom-call | flops 1000000000 | bytes 1953125 | tf_op jit(solution)/shard_map/pallas_call | solution.py:258
  16.0 2.0 %collective-permute-done.2.theirs = bf16[153,512]{1,0:T(8,128)(2,1)S(1)} collective-permute-done((bf16[153,512]{1,0:T(8,128)(2,1)S(1)}, bf16[153,512]{1,0:T(8,128)(2,1)S(1)}, u32[]{:S(2)}, u32[]{:S(2)}) %collective-permute-start.2) | collective-permute-done | bytes 156704 | tf_op jit(solution)/shard_map/ppermute | solution.py:283
  18.4 1.9 %collective-permute-start.4 = (bf16[153,128]{1,0:T(8,128)(2,1)S(1)}, bf16[153,128]{1,0:T(8,128)(2,1)S(1)}, u32[]{:S(2)}, u32[]{:S(2)}) collective-permute-start(bf16[153,128]{1,0:T(8,128)(2,1)S(1)} %get-tuple-element.53.after), channel_id=1, source_target_pairs={{0,4},{2,6},{4,0},{6,2},{8,12},{10,14},{12,8},{14,10},{1,5},{3,7},... | collective-permute-start | bytes 117512 | tf_op jit(solution)/shard_map/ppermute | solution.py:283
  20.3 1.4 %shard_map.107 = (bf16[768,512]{1,0:T(8,128)(2,1)S(1)}, bf16[512,512]{1,0:T(8,128)(2,1)S(1)}, bf16[512,128]{1,0:T(8,128)(2,1)S(1)}, f32[512,128]{1,0:T(8,128)S(1)}, f32[512,512]{1,0:T(8,128)S(1)}) custom-call(bf16[512,768]{1,0:T(8,128)(2,1)S(1)} %get-tuple-element.44.x, bf16[768,512]{1,0:T(8,128)(2,1)S(1)} %get-tuple-element.45.w1, ...), custom_call_target="tpu_custom_call" | custom-call | flops 2000000000 | bytes 3906250 | tf_op jit(solution)/shard_map/pallas_call | solution.py:258
  21.7 1.6 %collective-permute-start.6 = (f32[64,128]{1,0:T(8,128)S(1)}, f32[64,128]{1,0:T(8,128)S(1)}, u32[]{:S(2)}, u32[]{:S(2)}) collective-permute-start(f32[64,128]{1,0:T(8,128)S(1)} %maximum_select_fusion.packed), channel_id=1, source_target_pairs={{0,2},{2,0},{4,6},{6,4},{8,10},{10,8},{12,14},{14,12},{1,3},{3,1},... | collective-permute-start | bytes 98312 | tf_op jit(solution)/shard_map/ppermute | solution.py:283
  23.3 2.7 %collective-permute-start.5 = (bf16[153,128]{1,0:T(8,128)(2,1)S(1)}, bf16[153,128]{1,0:T(8,128)(2,1)S(1)}, u32[]{:S(2)}, u32[]{:S(2)}) collective-permute-start(bf16[153,128]{1,0:T(8,128)(2,1)S(1)} %get-tuple-element.82), channel_id=1, source_target_pairs={{0,8},{2,10},{4,12},{6,14},{8,0},{10,2},{12,4},{14,6},{1,9},{3,11}... | collective-permute-start | bytes 117512 | tf_op jit(solution)/shard_map/ppermute | solution.py:283
  26.0 2.4 %shard_map.108 = (bf16[1024,128]{1,0:T(8,128)(2,1)S(1)}, bf16[1024,128]{1,0:T(8,128)(2,1)S(1)}, s32[1,128]{1,0:T(1,128)}) custom-call(f32[64,128]{1,0:T(8,128)S(1)} %collective-permute-done.6.packed), custom_call_target="tpu_custom_call" | custom-call | flops 1000000000 | bytes 1953125 | tf_op jit(solution)/shard_map/pallas_call | solution.py:258
  28.5 1.3 %collective-permute-start.7 = (bf16[153,128]{1,0:T(8,128)(2,1)S(1)}, bf16[153,128]{1,0:T(8,128)(2,1)S(1)}, u32[]{:S(2)}, u32[]{:S(2)}) collective-permute-start(bf16[153,128]{1,0:T(8,128)(2,1)S(1)} %get-tuple-element.62), channel_id=1, source_target_pairs={{0,2},{2,0},{4,6},{6,4},{8,10},{10,8},{12,14},{14,12},{1,3},{3,1},... | collective-permute-start | bytes 117512 | tf_op jit(solution)/shard_map/ppermute | solution.py:283
  29.8 1.5 %shard_map.110 = (bf16[768,512]{1,0:T(8,128)(2,1)S(1)}, bf16[512,512]{1,0:T(8,128)(2,1)S(1)}, bf16[512,128]{1,0:T(8,128)(2,1)S(1)}, f32[512,128]{1,0:T(8,128)S(1)}, f32[512,512]{1,0:T(8,128)S(1)}) custom-call(bf16[256,768]{1,0:T(8,128)(2,1)S(1)} %collective-permute-done.8.mine, bf16[256,768]{1,0:T(8,128)(2,1)S(1)} %collective-permute-done.9.theirs, ...), custom_call_target="tpu_custom_call" | custom-call | flops 2000000000 | bytes 3906250 | tf_op jit(solution)/shard_map/pallas_call | solution.py:258
  31.3 1.3 %collective-permute-done.7.far_grad = bf16[153,128]{1,0:T(8,128)(2,1)S(1)} collective-permute-done((bf16[153,128]{1,0:T(8,128)(2,1)S(1)}, bf16[153,128]{1,0:T(8,128)(2,1)S(1)}, u32[]{:S(2)}, u32[]{:S(2)}) %collective-permute-start.7) | collective-permute-done | bytes 39200 | tf_op jit(solution)/shard_map/ppermute | solution.py:283
  32.6 2.7 %shard_map.111 = (bf16[720,128]{1,0:T(8,128)(2,1)S(1)}, f32[720,128]{1,0:T(8,128)S(1)}) custom-call(f32[153,128]{1,0:T(8,128)S(1)} %get-tuple-element.61.grad, bf16[153,128]{1,0:T(8,128)(2,1)S(1)} %collective-permute-done.7.far_grad, bf16[1024,128]{1,0:T(8,128)(2,1)S(1)} %get-tuple-element.50.high, bf16[1024,128]{1,0:T(8,128)(2,1)S(1)} %get-tuple-element.51.low, ...), custom_call_target="tpu_custom_call" | custom-call | flops 1000000 | bytes 1953 | tf_op jit(solution)/shard_map/pallas_call | solution.py:258
  36.3 4.6 %collective-permute-done.10.got = bf16[720,128]{1,0:T(8,128)(2,1)S(1)} collective-permute-done((bf16[720,128]{1,0:T(8,128)(2,1)S(1)}, bf16[720,128]{1,0:T(8,128)(2,1)S(1)}, u32[]{:S(2)}, u32[]{:S(2)}) %collective-permute-start.10) | collective-permute-done | bytes 184352 | tf_op jit(solution)/shard_map/ppermute | solution.py:283
  40.9 3.2 %collective-permute-start.11 = (bf16[720,128]{1,0:T(8,128)(2,1)S(1)}, bf16[720,128]{1,0:T(8,128)(2,1)S(1)}, u32[]{:S(2)}, u32[]{:S(2)}) collective-permute-start(bf16[720,128]{1,0:T(8,128)(2,1)S(1)} %shard_map.112.kept), channel_id=1, source_target_pairs={{0,8},{2,10},{4,12},{6,14},{8,0},{10,2},{12,4},{14,6},{1,9},{3,11}... | collective-permute-start | bytes 552968 | tf_op jit(solution)/shard_map/ppermute | solution.py:283
  44.1 6.0 %collective-permute-done.11.got = bf16[720,128]{1,0:T(8,128)(2,1)S(1)} collective-permute-done((bf16[720,128]{1,0:T(8,128)(2,1)S(1)}, bf16[720,128]{1,0:T(8,128)(2,1)S(1)}, u32[]{:S(2)}, u32[]{:S(2)}) %collective-permute-start.11) | collective-permute-done | bytes 184352 | tf_op jit(solution)/shard_map/ppermute | solution.py:283
  50.8 1.3 %collective-permute-start.13 = (bf16[720,128]{1,0:T(8,128)(2,1)S(1)}, bf16[720,128]{1,0:T(8,128)(2,1)S(1)}, u32[]{:S(2)}, u32[]{:S(2)}) collective-permute-start(bf16[720,128]{1,0:T(8,128)(2,1)S(1)} %shard_map.113.refs_0_), channel_id=1, source_target_pairs={{0,2},{2,0},{4,6},{6,4},{8,10},{10,8},{12,14},{14,12},{1,3},{3,1},... | collective-permute-start | bytes 552968 | tf_op jit(solution)/shard_map/ppermute | solution.py:283
  52.1 3.6 %collective-permute-done.12.refs_1_ = bf16[720,128]{1,0:T(8,128)(2,1)S(1)} collective-permute-done((bf16[720,128]{1,0:T(8,128)(2,1)S(1)}, bf16[720,128]{1,0:T(8,128)(2,1)S(1)}, u32[]{:S(2)}, u32[]{:S(2)}) %collective-permute-start.12) | collective-permute-done | bytes 184352 | tf_op jit(solution)/shard_map/ppermute | solution.py:283
  55.7 1.8 %collective-permute-start.14 = (bf16[720,128]{1,0:T(8,128)(2,1)S(1)}, bf16[720,128]{1,0:T(8,128)(2,1)S(1)}, u32[]{:S(2)}, u32[]{:S(2)}) collective-permute-start(bf16[720,128]{1,0:T(8,128)(2,1)S(1)} %collective-permute-done.12.refs_1_), channel_id=1, source_target_pairs={{0,2},{2,0},{4,6},{6,4},{8,10},{10,8},{12,14},{14,12},{1,3},{3,1},... | collective-permute-start | bytes 552968 | tf_op jit(solution)/shard_map/ppermute | solution.py:283
  58.1 3.2 %collective-permute-done.14.refs_3_ = bf16[720,128]{1,0:T(8,128)(2,1)S(1)} collective-permute-done((bf16[720,128]{1,0:T(8,128)(2,1)S(1)}, bf16[720,128]{1,0:T(8,128)(2,1)S(1)}, u32[]{:S(2)}, u32[]{:S(2)}) %collective-permute-start.14) | collective-permute-done | bytes 184352 | tf_op jit(solution)/shard_map/ppermute | solution.py:283
  62.7 1.4 %shard_map.114 = (bf16[768,512]{1,0:T(8,128)(2,1)}, bf16[512,512]{1,0:T(8,128)(2,1)}, bf16[153,512]{1,0:T(8,128)(2,1)}) custom-call(bf16[720,128]{1,0:T(8,128)(2,1)S(1)} %shard_map.113.refs_0_, bf16[720,128]{1,0:T(8,128)(2,1)S(1)} %collective-permute-done.12.refs_1_, bf16[720,128]{1,0:T(8,128)(2,1)S(1)} %collective-permute-done.13.refs_2_, ...), custom_call_target="tpu_custom_call" | custom-call | flops 1000000 | bytes 1953 | tf_op jit(solution)/shard_map/pallas_call | solution.py:258
  (32 shorter events, 7.9 us)
Async XLA Ops:
  1.7 3.1 %collective-permute-start = (f32[16,64]{1,0:T(8,128)S(1)}, f32[16,64]{1,0:T(8,128)S(1)}, u32[]{:S(2)}, u32[]{:S(2)}) collective-permute-start(f32[16,64]{1,0:T(8,128)S(1)} %get-tuple-element.43), channel_id=1, source_target_pairs={{0,1},{1,0},{2,3},{3,2},{4,5},{5,4},{6,7},{7,6},{8,9},{9,8},{10,11... | collective-permute-start | bytes 12296 | tf_op jit(solution)/shard_map/ppermute | solution.py:286
  2.2 18.0 %collective-permute-start.8 = (bf16[256,768]{1,0:T(8,128)(2,1)S(1)}, bf16[256,768]{1,0:T(8,128)(2,1)S(1)}, u32[]{:S(2)}, u32[]{:S(2)}) collective-permute-start(bf16[256,768]{1,0:T(8,128)(2,1)S(1)} %get-tuple-element.65), channel_id=1, source_target_pairs={{0,2},{2,0},{4,6},{6,4},{8,10},{10,8},{12,14},{14,12},{1,3},{3,1},... | collective-permute-start | bytes 1179656 | tf_op jit(solution)/shard_map/ppermute | solution.py:283
  4.9 4.4 %collective-permute-start.1 = (f32[16,128]{1,0:T(8,128)S(1)}, f32[16,128]{1,0:T(8,128)S(1)}, u32[]{:S(2)}, u32[]{:S(2)}) collective-permute-start(f32[16,128]{1,0:T(8,128)S(1)} %maximum_select_fusion.2.after), channel_id=1, source_target_pairs={{0,4},{2,6},{4,0},{6,2},{8,12},{10,14},{12,8},{14,10},{1,5},{3,7},... | collective-permute-start | bytes 24584 | tf_op jit(solution)/shard_map/ppermute | solution.py:283
  9.3 4.7 %collective-permute-start.3 = (f32[32,128]{1,0:T(8,128)S(1)}, f32[32,128]{1,0:T(8,128)S(1)}, u32[]{:S(2)}, u32[]{:S(2)}) collective-permute-start(f32[32,128]{1,0:T(8,128)S(1)} %maximum_select_fusion.1), channel_id=1, source_target_pairs={{0,8},{2,10},{4,12},{6,14},{8,0},{10,2},{12,4},{14,6},{1,9},{3,11}... | collective-permute-start | bytes 49160 | tf_op jit(solution)/shard_map/ppermute | solution.py:283
  11.9 6.1 %collective-permute-start.2 = (bf16[153,512]{1,0:T(8,128)(2,1)S(1)}, bf16[153,512]{1,0:T(8,128)(2,1)S(1)}, u32[]{:S(2)}, u32[]{:S(2)}) collective-permute-start(bf16[153,512]{1,0:T(8,128)(2,1)S(1)} %shard_map.104.mine), channel_id=1, source_target_pairs={{0,2},{2,0},{4,6},{6,4},{8,10},{10,8},{12,14},{14,12},{1,3},{3,1},... | collective-permute-start | bytes 470024 | tf_op jit(solution)/shard_map/ppermute | solution.py:283
  18.4 5.0 %collective-permute-start.4 = (bf16[153,128]{1,0:T(8,128)(2,1)S(1)}, bf16[153,128]{1,0:T(8,128)(2,1)S(1)}, u32[]{:S(2)}, u32[]{:S(2)}) collective-permute-start(bf16[153,128]{1,0:T(8,128)(2,1)S(1)} %get-tuple-element.53.after), channel_id=1, source_target_pairs={{0,4},{2,6},{4,0},{6,2},{8,12},{10,14},{12,8},{14,10},{1,5},{3,7},... | collective-permute-start | bytes 117512 | tf_op jit(solution)/shard_map/ppermute | solution.py:283
  20.3 9.5 %collective-permute-start.9 = (bf16[256,768]{1,0:T(8,128)(2,1)S(1)}, bf16[256,768]{1,0:T(8,128)(2,1)S(1)}, u32[]{:S(2)}, u32[]{:S(2)}) collective-permute-start(bf16[256,768]{1,0:T(8,128)(2,1)S(1)} %collective-permute-done.8.mine), channel_id=1, source_target_pairs={{0,1},{1,0},{2,3},{3,2},{4,5},{5,4},{6,7},{7,6},{8,9},{9,8},{10,11... | collective-permute-start | bytes 1179656 | tf_op jit(solution)/shard_map/ppermute | solution.py:286
  21.7 4.3 %collective-permute-start.6 = (f32[64,128]{1,0:T(8,128)S(1)}, f32[64,128]{1,0:T(8,128)S(1)}, u32[]{:S(2)}, u32[]{:S(2)}) collective-permute-start(f32[64,128]{1,0:T(8,128)S(1)} %maximum_select_fusion.packed), channel_id=1, source_target_pairs={{0,2},{2,0},{4,6},{6,4},{8,10},{10,8},{12,14},{14,12},{1,3},{3,1},... | collective-permute-start | bytes 98312 | tf_op jit(solution)/shard_map/ppermute | solution.py:283
  23.3 5.1 %collective-permute-start.5 = (bf16[153,128]{1,0:T(8,128)(2,1)S(1)}, bf16[153,128]{1,0:T(8,128)(2,1)S(1)}, u32[]{:S(2)}, u32[]{:S(2)}) collective-permute-start(bf16[153,128]{1,0:T(8,128)(2,1)S(1)} %get-tuple-element.82), channel_id=1, source_target_pairs={{0,8},{2,10},{4,12},{6,14},{8,0},{10,2},{12,4},{14,6},{1,9},{3,11}... | collective-permute-start | bytes 117512 | tf_op jit(solution)/shard_map/ppermute | solution.py:283
  28.5 4.1 %collective-permute-start.7 = (bf16[153,128]{1,0:T(8,128)(2,1)S(1)}, bf16[153,128]{1,0:T(8,128)(2,1)S(1)}, u32[]{:S(2)}, u32[]{:S(2)}) collective-permute-start(bf16[153,128]{1,0:T(8,128)(2,1)S(1)} %get-tuple-element.62), channel_id=1, source_target_pairs={{0,2},{2,0},{4,6},{6,4},{8,10},{10,8},{12,14},{14,12},{1,3},{3,1},... | collective-permute-start | bytes 117512 | tf_op jit(solution)/shard_map/ppermute | solution.py:283
  35.2 5.6 %collective-permute-start.10 = (bf16[720,128]{1,0:T(8,128)(2,1)S(1)}, bf16[720,128]{1,0:T(8,128)(2,1)S(1)}, u32[]{:S(2)}, u32[]{:S(2)}) collective-permute-start(bf16[720,128]{1,0:T(8,128)(2,1)S(1)} %get-tuple-element.77), channel_id=1, source_target_pairs={{0,4},{2,6},{4,0},{6,2},{8,12},{10,14},{12,8},{14,10},{1,5},{3,7},... | collective-permute-start | bytes 552968 | tf_op jit(solution)/shard_map/ppermute | solution.py:283
  40.9 9.2 %collective-permute-start.11 = (bf16[720,128]{1,0:T(8,128)(2,1)S(1)}, bf16[720,128]{1,0:T(8,128)(2,1)S(1)}, u32[]{:S(2)}, u32[]{:S(2)}) collective-permute-start(bf16[720,128]{1,0:T(8,128)(2,1)S(1)} %shard_map.112.kept), channel_id=1, source_target_pairs={{0,8},{2,10},{4,12},{6,14},{8,0},{10,2},{12,4},{14,6},{1,9},{3,11}... | collective-permute-start | bytes 552968 | tf_op jit(solution)/shard_map/ppermute | solution.py:283
  50.1 5.6 %collective-permute-start.12 = (bf16[720,128]{1,0:T(8,128)(2,1)S(1)}, bf16[720,128]{1,0:T(8,128)(2,1)S(1)}, u32[]{:S(2)}, u32[]{:S(2)}) collective-permute-start(bf16[720,128]{1,0:T(8,128)(2,1)S(1)} %shard_map.113.refs_0_), channel_id=1, source_target_pairs={{0,4},{2,6},{4,0},{6,2},{8,12},{10,14},{12,8},{14,10},{1,5},{3,7},... | collective-permute-start | bytes 552968 | tf_op jit(solution)/shard_map/ppermute | solution.py:283
  50.8 7.3 %collective-permute-start.13 = (bf16[720,128]{1,0:T(8,128)(2,1)S(1)}, bf16[720,128]{1,0:T(8,128)(2,1)S(1)}, u32[]{:S(2)}, u32[]{:S(2)}) collective-permute-start(bf16[720,128]{1,0:T(8,128)(2,1)S(1)} %shard_map.113.refs_0_), channel_id=1, source_target_pairs={{0,2},{2,0},{4,6},{6,4},{8,10},{10,8},{12,14},{14,12},{1,3},{3,1},... | collective-permute-start | bytes 552968 | tf_op jit(solution)/shard_map/ppermute | solution.py:283
  55.7 5.5 %collective-permute-start.14 = (bf16[720,128]{1,0:T(8,128)(2,1)S(1)}, bf16[720,128]{1,0:T(8,128)(2,1)S(1)}, u32[]{:S(2)}, u32[]{:S(2)}) collective-permute-start(bf16[720,128]{1,0:T(8,128)(2,1)S(1)} %collective-permute-done.12.refs_1_), channel_id=1, source_target_pairs={{0,2},{2,0},{4,6},{6,4},{8,10},{10,8},{12,14},{14,12},{1,3},{3,1},... | collective-permute-start | bytes 552968 | tf_op jit(solution)/shard_map/ppermute | solution.py:283
  57.6 4.3 %collective-permute-start.15 = (bf16[720,128]{1,0:T(8,128)(2,1)S(1)}, bf16[720,128]{1,0:T(8,128)(2,1)S(1)}, u32[]{:S(2)}, u32[]{:S(2)}) collective-permute-start(bf16[720,128]{1,0:T(8,128)(2,1)S(1)} %shard_map.113.refs_0_), channel_id=1, source_target_pairs={{0,1},{1,0},{2,3},{3,2},{4,5},{5,4},{6,7},{7,6},{8,9},{9,8},{10,11... | collective-permute-start | bytes 552968 | tf_op jit(solution)/shard_map/ppermute | solution.py:286
  57.6 4.3 %collective-permute-start.16 = (bf16[720,128]{1,0:T(8,128)(2,1)S(1)}, bf16[720,128]{1,0:T(8,128)(2,1)S(1)}, u32[]{:S(2)}, u32[]{:S(2)}) collective-permute-start(bf16[720,128]{1,0:T(8,128)(2,1)S(1)} %collective-permute-done.12.refs_1_), channel_id=1, source_target_pairs={{0,1},{1,0},{2,3},{3,2},{4,5},{5,4},{6,7},{7,6},{8,9},{9,8},{10,11... | collective-permute-start | bytes 552968 | tf_op jit(solution)/shard_map/ppermute | solution.py:286
  58.1 3.8 %collective-permute-start.17 = (bf16[720,128]{1,0:T(8,128)(2,1)S(1)}, bf16[720,128]{1,0:T(8,128)(2,1)S(1)}, u32[]{:S(2)}, u32[]{:S(2)}) collective-permute-start(bf16[720,128]{1,0:T(8,128)(2,1)S(1)} %collective-permute-done.13.refs_2_), channel_id=1, source_target_pairs={{0,1},{1,0},{2,3},{3,2},{4,5},{5,4},{6,7},{7,6},{8,9},{9,8},{10,11... | collective-permute-start | bytes 552968 | tf_op jit(solution)/shard_map/ppermute | solution.py:286
  61.3 1.4 %collective-permute-start.18 = (bf16[720,128]{1,0:T(8,128)(2,1)S(1)}, bf16[720,128]{1,0:T(8,128)(2,1)S(1)}, u32[]{:S(2)}, u32[]{:S(2)}) collective-permute-start(bf16[720,128]{1,0:T(8,128)(2,1)S(1)} %collective-permute-done.14.refs_3_), channel_id=1, source_target_pairs={{0,1},{1,0},{2,3},{3,2},{4,5},{5,4},{6,7},{7,6},{8,9},{9,8},{10,11... | collective-permute-start | bytes 552968 | tf_op jit(solution)/shard_map/ppermute | solution.py:286

commit v5 on v4

--- a/solution.py
+++ b/solution.py
@@ -43,11 +43,14 @@
     return copies
 
 
-def pack_kernel(nodes, ids_hbm, wts_hbm, labels_hbm, x_hbm, out, half, ids, wts, labels, sem):
+def pack_kernel(nodes, ids_hbm, wts_hbm, labels_hbm, x_hbm, out, near, late, ids, wts, labels, sem):
     rows, fanout = ids.shape
-    part = half.shape[0]
-    mine = x_hbm.at[pl.ds(pl.multiple_of(lax.axis_index("batch") * part, ROW), part), :]
-    into = launch(sem, ((labels_hbm, labels), (ids_hbm, ids), (wts_hbm, wts), (mine, half)))
+    start = lax.axis_index("batch") * (x_hbm.shape[0] // 2)
+    pairs = ((labels_hbm, labels), (ids_hbm, ids), (wts_hbm, wts))
+    for piece in (near, late):
+        pairs += ((x_hbm.at[pl.ds(pl.multiple_of(start, ROW), piece.shape[0]), :], piece),)
+        start = start + piece.shape[0]
+    into = launch(sem, pairs)
     for c in into[:3]:
         c.wait()
     shape = (rows, rows)
@@ -56,6 +59,7 @@
     out[:, :fanout] = ids[...].astype(F32) + label * nodes
     out[:, fanout:] = wts[...]
     into[3].wait()
+    into[4].wait()
 
 
 def load_kernel(after, *refs):
@@ -91,11 +95,13 @@
     layers(x, w1, w2, xt, h1t, h2, s1, s2, one, two)
 
 
-def peer_kernel(mine, theirs, w1, w2, xt, h1t, h2, s1, s2, x, one, two):
-    half = mine.shape[0]
+def peer_kernel(near, late, far_near, far_late, w1, w2, xt, h1t, h2, s1, s2, x, one, two):
     core = lax.axis_index("batch")
-    x[pl.ds(pl.multiple_of(core * half, half), half), :] = mine[...]
-    x[pl.ds(pl.multiple_of((1 - core) * half, half), half), :] = theirs[...]
+    for side, pieces in ((core, (near, late)), (1 - core, (far_near, far_late))):
+        start = side * (x.shape[0] // 2)
+        for piece in pieces:
+            x[pl.ds(pl.multiple_of(start, ROW), piece.shape[0]), :] = piece[...]
+            start = start + piece.shape[0]
     layers(x, w1, w2, xt, h1t, h2, s1, s2, one, two)
 
 
@@ -286,12 +292,12 @@
         return lax.ppermute(x, "batch", [(0, 1), (1, 0)])
 
     w3t = w_third.T
-    half = node_dev // 2
+    near = 5 * node_dev // 16
     w1_type, w2_type, x_type = (w_first.shape, BF), (w_second.shape, BF), (features.shape, BF)
-    packed, my_half = whole(
+    packed, my_near, my_late = whole(
         functools.partial(pack_kernel, nodes),
-        [((rows, 2 * fanout), F32), ((half, depth), BF)],
-        [((rows, fanout), jnp.int32), ((rows, fanout), F32), ((1, rows), jnp.int32), 4],
+        [((rows, 2 * fanout), F32), ((near, depth), BF), ((node_dev // 2 - near, depth), BF)],
+        [((rows, fanout), jnp.int32), ((rows, fanout), F32), ((1, rows), jnp.int32), 5],
         nbr_ids,
         nbr_weight,
         labels.reshape(1, rows),
@@ -299,7 +305,7 @@
         limit=PACK,
         far_in=range(4),
     )
-    peer_half = over(my_half, 1)
+    peer_near = over(my_near, 1)
     got = other_core(packed)
     packed = jnp.where(core == 0, jnp.concatenate([packed, got], 1), jnp.concatenate([got, packed], 1))
     features, w_first, w_second, w3t = whole(
@@ -323,13 +329,15 @@
         w_second,
         w3t,
         packed,
-        flops=2000000000,
+        flops=1000,
         limit=16,
     )
     for bit in bits:
         got = over(packed, bit)
         if bit == bits[0]:
             got, scores = lax.optimization_barrier((got, scores))
+        if bit == bits[-1]:
+            got, peer_near = lax.optimization_barrier((got, peer_near))
         up = (me // bit) % 2
         packed = jnp.where(up == 0, jnp.concatenate([packed, got], 0), jnp.concatenate([got, packed], 0))
     far_scores = over(scores, 1)
@@ -339,6 +347,8 @@
     tables = [((fanout, targets), jnp.int32), ((fanout, targets), F32)]
     spread_call = functools.partial(whole, functools.partial(spread_kernel, nodes), maps, tables, limit=big, flops=1000000000)
     high, low, label = spread_call(packed)
+    my_late = lax.optimization_barrier((my_late, high))[0]
+    peer_late = over(my_late, 1)
     part, send = whole(
         logit_kernel,
         [((classes, targets), F32), ((classes, targets), BF)],
@@ -359,11 +369,11 @@
     work = [((node_dev, hidden), F32), ((node_dev, hidden), BF)]
     packed = lax.optimization_barrier((packed, send))[0]
     far_packed = over(packed, 1)
-    peer_half = lax.optimization_barrier((peer_half, send))[0]
-    peer_rest = other_core(peer_half)
     xt, h1t, h2, s1, s2 = whole(
-        again_kernel, kept, work, features, w_first, w_second, send, flops=2000000000
-    )
+        again_kernel, kept, work, features, w_first, w_second, send, flops=1000
+    )
+    peer_near, peer_late = lax.optimization_barrier((peer_near, peer_late, s1))[:2]
+    far_near, far_late = other_core(peer_near), other_core(peer_late)
     for bit in bits[:-1]:
         got = over(send, bit)
         if bit == bits[0]:
@@ -373,17 +383,6 @@
     far_packed = lax.optimization_barrier((far_packed, send))[0]
     far_high, far_low, _ = spread_call(far_packed)
     got = over(send, bits[-1])
-    peer_rest = lax.optimization_barrier((peer_rest, got))[0]
-    pxt, ph1t, ph2, ps1, ps2 = whole(
-        peer_kernel,
-        kept,
-        [x_type] + work,
-        peer_half,
-        peer_rest,
-        w_first,
-        w_second,
-        flops=2000000000,
-    )
     got = lax.optimization_barrier((got, far_high))[0]
     grad, grad_send, loss = whole(
         softmax_kernel,
@@ -396,6 +395,19 @@
     at = core * (targets // 2) + (me // 2) * rows
     target_loss = lax.dynamic_slice_in_dim(loss[0], at, rows, 0)
     far_grad = over(grad_send, 1)
+    far_late = lax.optimization_barrier((far_late, grad_send))[0]
+    pxt, ph1t, ph2, ps1, ps2 = whole(
+        peer_kernel,
+        kept,
+        [x_type] + work,
+        peer_near,
+        peer_late,
+        far_near,
+        far_late,
+        w_first,
+        w_second,
+        flops=2000000000,
+    )
 
     step = ROW << (len(bits) - 1)
     stack = -(-(depth + hidden + classes) // step) * step

time: 64.2 us -> 63 us (0.981)
  starting transfers between devices: 24.4 us -> 20 us
  waiting for transfers between devices: 22.5 us -> 25.6 us
    ppermute x13 -> x14, starting transfers between devices: 23.4 us -> 18.4 us  [over(): return lax.ppermute(x, 'owner', [(i, i ^ bit) for i in range(owners)])]
    ppermute x13 -> x14, waiting for transfers between devices: 21.6 us -> 24.8 us  [over(): return lax.ppermute(x, 'owner', [(i, i ^ bit) for i in range(owners)])]
    ppermute x6 -> x7, starting transfers between devices: 1.04 us -> 1.54 us  [other_core(): return lax.ppermute(x, 'batch', [(0, 1), (1, 0)])]
  transfers between devices with their start and end apart: 19 -> 21, of which waited for: 8 -> 11; matrix products, arithmetic and copies ran while one was open for 1% -> 1% of each run, Pallas kernels for 16% -> 17%
where the time goes in v5:
time: 63 us; the launch traced here: 62.8 us
  waiting for transfers between devices  25.6 us (41%)
  starting transfers between devices  20 us (32%)
  Pallas kernels  15.8 us (25%)
  between operations  0.74 us (1%)
    ppermute x14, waiting for transfers between devices, over(): return lax.ppermute(x, 'owner', [(i, i ^ bit) for i in range(owners)])  24.8 us
    ppermute x14, starting transfers between devices, over(): return lax.ppermute(x, 'owner', [(i, i ^ bit) for i in range(owners)])  18.4 us
    pallas_call x13, Pallas kernels, whole(): pl.pallas_call(kernel, out_shape=[jax.ShapeDtypeStruct(shape, kind) for s...  15.8 us
    ppermute x7, starting transfers between devices, other_core(): return lax.ppermute(x, 'batch', [(0, 1), (1, 0)])  1.54 us
  transfers between devices with their start and end apart: 21, of which 11 were waited for; matrix products, arithmetic and copies ran while one was open for 1% of the time, Pallas kernels for 17%

profile of v5, /device:TPU:0, one launch (start us, length us, event | category | flops | bytes accessed | tf_op | source)
XLA Modules:
  0.0 62.8 jit_solution(10656985124545319816)
XLA Ops:
  0.6 1.1 %shard_map.102 = (f32[16,64]{1,0:T(8,128)S(1)}, bf16[160,768]{1,0:T(8,128)(2,1)S(1)}, bf16[96,768]{1,0:T(8,128)(2,1)S(1)}) custom-call(s32[16,32]{1,0:T(8,128)} %ids_hbm.1, f32[16,32]{1,0:T(8,128)} %wts_hbm.1, s32[1,16]{1,0:T(1,128)} %bitcast.6, bf16[512,768]{1,0:T(8,128)(2,1)} %refs_0_.1), custom_call_target="tpu_custom_call" | custom-call | flops 1000000 | bytes 1953 | tf_op jit(solution)/shard_map/pallas_call | solution.py:264
  2.3 2.6 %collective-permute-start.4 = (bf16[160,768]{1,0:T(8,128)(2,1)S(1)}, bf16[160,768]{1,0:T(8,128)(2,1)S(1)}, u32[]{:S(2)}, u32[]{:S(2)}) collective-permute-start(bf16[160,768]{1,0:T(8,128)(2,1)S(1)} %get-tuple-element.55), channel_id=1, source_target_pairs={{0,2},{2,0},{4,6},{6,4},{8,10},{10,8},{12,14},{14,12},{1,3},{3,1},... | collective-permute-start | bytes 737288 | tf_op jit(solution)/shard_map/ppermute | solution.py:289
  4.9 1.6 %collective-permute-start.1 = (f32[16,128]{1,0:T(8,128)S(1)}, f32[16,128]{1,0:T(8,128)S(1)}, u32[]{:S(2)}, u32[]{:S(2)}) collective-permute-start(f32[16,128]{1,0:T(8,128)S(1)} %maximum_select_fusion.2.after), channel_id=1, source_target_pairs={{0,4},{2,6},{4,0},{6,2},{8,12},{10,14},{12,8},{14,10},{1,5},{3,7},... | collective-permute-start | bytes 24584 | tf_op jit(solution)/shard_map/ppermute | solution.py:289
  6.5 1.6 %shard_map.103 = (bf16[512,768]{1,0:T(8,128)(2,1)S(1)}, bf16[768,512]{1,0:T(8,128)(2,1)S(1)}, bf16[512,512]{1,0:T(8,128)(2,1)S(1)}, bf16[153,512]{1,0:T(8,128)(2,1)S(1)}) custom-call(f32[16,128]{1,0:T(8,128)S(1)} %maximum_select_fusion.2.after, bf16[512,768]{1,0:T(8,128)(2,1)} %refs_0_.1, bf16[768,512]{1,0:T(8,128)(2,1)} %refs_1_.1, ...), custom_call_target="tpu_custom_call" | custom-call | flops 1000000 | bytes 1953 | tf_op jit(solution)/shard_map/pallas_call | solution.py:264
  8.1 1.2 %shard_map.104.mine = bf16[153,512]{1,0:T(8,128)(2,1)S(1)} custom-call(bf16[512,768]{1,0:T(8,128)(2,1)S(1)} %get-tuple-element.49.x, bf16[768,512]{1,0:T(8,128)(2,1)S(1)} %get-tuple-element.50.w1, bf16[512,512]{1,0:T(8,128)(2,1)S(1)} %get-tuple-element.51.w2, bf16[153,512]{1,0:T(8,128)(2,1)S(1)} %get-tuple-element.52.w3.w3t, ...), custom_call_target="tpu_custom_call" | custom-call | flops 1000 | bytes 1 | tf_op jit(solution)/shard_map/pallas_call | solution.py:264
  9.3 2.7 %collective-permute-start.3 = (f32[32,128]{1,0:T(8,128)S(1)}, f32[32,128]{1,0:T(8,128)S(1)}, u32[]{:S(2)}, u32[]{:S(2)}) collective-permute-start(f32[32,128]{1,0:T(8,128)S(1)} %maximum_select_fusion.1), channel_id=1, source_target_pairs={{0,8},{2,10},{4,12},{6,14},{8,0},{10,2},{12,4},{14,6},{1,9},{3,11}... | collective-permute-start | bytes 49160 | tf_op jit(solution)/shard_map/ppermute | solution.py:289
  12.0 1.1 %collective-permute-start.2 = (bf16[153,512]{1,0:T(8,128)(2,1)S(1)}, bf16[153,512]{1,0:T(8,128)(2,1)S(1)}, u32[]{:S(2)}, u32[]{:S(2)}) collective-permute-start(bf16[153,512]{1,0:T(8,128)(2,1)S(1)} %shard_map.104.mine), channel_id=1, source_target_pairs={{0,2},{2,0},{4,6},{6,4},{8,10},{10,8},{12,14},{14,12},{1,3},{3,1},... | collective-permute-start | bytes 470024 | tf_op jit(solution)/shard_map/ppermute | solution.py:289
  14.0 2.0 %shard_map.105 = (bf16[1024,128]{1,0:T(8,128)(2,1)S(1)}, bf16[1024,128]{1,0:T(8,128)(2,1)S(1)}, s32[1,128]{1,0:T(1,128)S(1)}) custom-call(f32[64,128]{1,0:T(8,128)S(1)} %maximum_select_fusion.packed), custom_call_target="tpu_custom_call" | custom-call | flops 1000000000 | bytes 1953125 | tf_op jit(solution)/shard_map/pallas_call | solution.py:264
  16.1 1.2 %collective-permute-start.9 = (bf16[96,768]{1,0:T(8,128)(2,1)S(1)}, bf16[96,768]{1,0:T(8,128)(2,1)S(1)}, u32[]{:S(2)}, u32[]{:S(2)}) collective-permute-start(bf16[96,768]{1,0:T(8,128)(2,1)S(1)} %get-tuple-element.74), channel_id=1, source_target_pairs={{0,2},{2,0},{4,6},{6,4},{8,10},{10,8},{12,14},{14,12},{1,3},{3,1},... | collective-permute-start | bytes 442376 | tf_op jit(solution)/shard_map/ppermute | solution.py:289
  18.7 1.4 %shard_map.107 = (bf16[768,512]{1,0:T(8,128)(2,1)S(1)}, bf16[512,512]{1,0:T(8,128)(2,1)S(1)}, bf16[512,128]{1,0:T(8,128)(2,1)S(1)}, f32[512,128]{1,0:T(8,128)S(1)}, f32[512,512]{1,0:T(8,128)S(1)}) custom-call(bf16[512,768]{1,0:T(8,128)(2,1)S(1)} %get-tuple-element.49.x, bf16[768,512]{1,0:T(8,128)(2,1)S(1)} %get-tuple-element.50.w1, ...), custom_call_target="tpu_custom_call" | custom-call | flops 1000 | bytes 1 | tf_op jit(solution)/shard_map/pallas_call | solution.py:264
  20.1 1.1 %collective-permute-start.7 = (f32[64,128]{1,0:T(8,128)S(1)}, f32[64,128]{1,0:T(8,128)S(1)}, u32[]{:S(2)}, u32[]{:S(2)}) collective-permute-start(f32[64,128]{1,0:T(8,128)S(1)} %maximum_select_fusion.packed), channel_id=1, source_target_pairs={{0,2},{2,0},{4,6},{6,4},{8,10},{10,8},{12,14},{14,12},{1,3},{3,1},... | collective-permute-start | bytes 98312 | tf_op jit(solution)/shard_map/ppermute | solution.py:289
  22.7 2.1 %collective-permute-start.6 = (bf16[153,128]{1,0:T(8,128)(2,1)S(1)}, bf16[153,128]{1,0:T(8,128)(2,1)S(1)}, u32[]{:S(2)}, u32[]{:S(2)}) collective-permute-start(bf16[153,128]{1,0:T(8,128)(2,1)S(1)} %get-tuple-element.92), channel_id=1, source_target_pairs={{0,8},{2,10},{4,12},{6,14},{8,0},{10,2},{12,4},{14,6},{1,9},{3,11}... | collective-permute-start | bytes 117512 | tf_op jit(solution)/shard_map/ppermute | solution.py:289
  24.8 2.4 %shard_map.108 = (bf16[1024,128]{1,0:T(8,128)(2,1)S(1)}, bf16[1024,128]{1,0:T(8,128)(2,1)S(1)}, s32[1,128]{1,0:T(1,128)}) custom-call(f32[64,128]{1,0:T(8,128)S(1)} %collective-permute-done.7.packed), custom_call_target="tpu_custom_call" | custom-call | flops 1000000000 | bytes 1953125 | tf_op jit(solution)/shard_map/pallas_call | solution.py:264
  28.2 1.1 %collective-permute-start.8 = (bf16[153,128]{1,0:T(8,128)(2,1)S(1)}, bf16[153,128]{1,0:T(8,128)(2,1)S(1)}, u32[]{:S(2)}, u32[]{:S(2)}) collective-permute-start(bf16[153,128]{1,0:T(8,128)(2,1)S(1)} %get-tuple-element.69), channel_id=1, source_target_pairs={{0,2},{2,0},{4,6},{6,4},{8,10},{10,8},{12,14},{14,12},{1,3},{3,1},... | collective-permute-start | bytes 117512 | tf_op jit(solution)/shard_map/ppermute | solution.py:289
  29.2 1.5 %shard_map.110 = (bf16[768,512]{1,0:T(8,128)(2,1)S(1)}, bf16[512,512]{1,0:T(8,128)(2,1)S(1)}, bf16[512,128]{1,0:T(8,128)(2,1)S(1)}, f32[512,128]{1,0:T(8,128)S(1)}, f32[512,512]{1,0:T(8,128)S(1)}) custom-call(bf16[160,768]{1,0:T(8,128)(2,1)S(1)} %collective-permute-done.4.near, bf16[96,768]{1,0:T(8,128)(2,1)S(1)} %collective-permute-done.9.late, ...), custom_call_target="tpu_custom_call" | custom-call | flops 2000000000 | bytes 3906250 | tf_op jit(solution)/shard_map/pallas_call | solution.py:264
  30.7 1.5 %collective-permute-done.8.far_grad = bf16[153,128]{1,0:T(8,128)(2,1)S(1)} collective-permute-done((bf16[153,128]{1,0:T(8,128)(2,1)S(1)}, bf16[153,128]{1,0:T(8,128)(2,1)S(1)}, u32[]{:S(2)}, u32[]{:S(2)}) %collective-permute-start.8) | collective-permute-done | bytes 39200 | tf_op jit(solution)/shard_map/ppermute | solution.py:289
  32.2 2.7 %shard_map.111 = (bf16[720,128]{1,0:T(8,128)(2,1)S(1)}, f32[720,128]{1,0:T(8,128)S(1)}) custom-call(f32[153,128]{1,0:T(8,128)S(1)} %get-tuple-element.68.grad, bf16[153,128]{1,0:T(8,128)(2,1)S(1)} %collective-permute-done.8.far_grad, bf16[1024,128]{1,0:T(8,128)(2,1)S(1)} %get-tuple-element.57.high, bf16[1024,128]{1,0:T(8,128)(2,1)S(1)} %get-tuple-element.58.low, ...), custom_call_target="tpu_custom_call" | custom-call | flops 1000000 | bytes 1953 | tf_op jit(solution)/shard_map/pallas_call | solution.py:264
  35.2 5.3 %collective-permute-done.12.got = bf16[720,128]{1,0:T(8,128)(2,1)S(1)} collective-permute-done((bf16[720,128]{1,0:T(8,128)(2,1)S(1)}, bf16[720,128]{1,0:T(8,128)(2,1)S(1)}, u32[]{:S(2)}, u32[]{:S(2)}) %collective-permute-start.12) | collective-permute-done | bytes 184352 | tf_op jit(solution)/shard_map/ppermute | solution.py:289
  40.6 2.3 %collective-permute-start.13 = (bf16[720,128]{1,0:T(8,128)(2,1)S(1)}, bf16[720,128]{1,0:T(8,128)(2,1)S(1)}, u32[]{:S(2)}, u32[]{:S(2)}) collective-permute-start(bf16[720,128]{1,0:T(8,128)(2,1)S(1)} %shard_map.112.kept), channel_id=1, source_target_pairs={{0,8},{2,10},{4,12},{6,14},{8,0},{10,2},{12,4},{14,6},{1,9},{3,11}... | collective-permute-start | bytes 552968 | tf_op jit(solution)/shard_map/ppermute | solution.py:289
  42.8 6.0 %collective-permute-done.13.got = bf16[720,128]{1,0:T(8,128)(2,1)S(1)} collective-permute-done((bf16[720,128]{1,0:T(8,128)(2,1)S(1)}, bf16[720,128]{1,0:T(8,128)(2,1)S(1)}, u32[]{:S(2)}, u32[]{:S(2)}) %collective-permute-start.13) | collective-permute-done | bytes 184352 | tf_op jit(solution)/shard_map/ppermute | solution.py:289
  49.0 1.0 %collective-permute-start.15 = (bf16[720,128]{1,0:T(8,128)(2,1)S(1)}, bf16[720,128]{1,0:T(8,128)(2,1)S(1)}, u32[]{:S(2)}, u32[]{:S(2)}) collective-permute-start(bf16[720,128]{1,0:T(8,128)(2,1)S(1)} %shard_map.113.refs_0_), channel_id=1, source_target_pairs={{0,2},{2,0},{4,6},{6,4},{8,10},{10,8},{12,14},{14,12},{1,3},{3,1},... | collective-permute-start | bytes 552968 | tf_op jit(solution)/shard_map/ppermute | solution.py:289
  49.9 4.5 %collective-permute-done.14.refs_1_ = bf16[720,128]{1,0:T(8,128)(2,1)S(1)} collective-permute-done((bf16[720,128]{1,0:T(8,128)(2,1)S(1)}, bf16[720,128]{1,0:T(8,128)(2,1)S(1)}, u32[]{:S(2)}, u32[]{:S(2)}) %collective-permute-start.14) | collective-permute-done | bytes 184352 | tf_op jit(solution)/shard_map/ppermute | solution.py:289
  56.1 3.9 %collective-permute-done.16.refs_3_ = bf16[720,128]{1,0:T(8,128)(2,1)S(1)} collective-permute-done((bf16[720,128]{1,0:T(8,128)(2,1)S(1)}, bf16[720,128]{1,0:T(8,128)(2,1)S(1)}, u32[]{:S(2)}, u32[]{:S(2)}) %collective-permute-start.16) | collective-permute-done | bytes 184352 | tf_op jit(solution)/shard_map/ppermute | solution.py:289
  61.4 1.4 %shard_map.114 = (bf16[768,512]{1,0:T(8,128)(2,1)}, bf16[512,512]{1,0:T(8,128)(2,1)}, bf16[153,512]{1,0:T(8,128)(2,1)}) custom-call(bf16[720,128]{1,0:T(8,128)(2,1)S(1)} %shard_map.113.refs_0_, bf16[720,128]{1,0:T(8,128)(2,1)S(1)} %collective-permute-done.14.refs_1_, bf16[720,128]{1,0:T(8,128)(2,1)S(1)} %collective-permute-done.15.refs_2_, ...), custom_call_target="tpu_custom_call" | custom-call | flops 1000000 | bytes 1953 | tf_op jit(solution)/shard_map/pallas_call | solution.py:264
  (36 shorter events, 8.9 us)
Async XLA Ops:
  1.8 3.1 %collective-permute-start = (f32[16,64]{1,0:T(8,128)S(1)}, f32[16,64]{1,0:T(8,128)S(1)}, u32[]{:S(2)}, u32[]{:S(2)}) collective-permute-start(f32[16,64]{1,0:T(8,128)S(1)} %get-tuple-element.48), channel_id=1, source_target_pairs={{0,1},{1,0},{2,3},{3,2},{4,5},{5,4},{6,7},{7,6},{8,9},{9,8},{10,11... | collective-permute-start | bytes 12296 | tf_op jit(solution)/shard_map/ppermute | solution.py:292
  2.3 11.7 %collective-permute-start.4 = (bf16[160,768]{1,0:T(8,128)(2,1)S(1)}, bf16[160,768]{1,0:T(8,128)(2,1)S(1)}, u32[]{:S(2)}, u32[]{:S(2)}) collective-permute-start(bf16[160,768]{1,0:T(8,128)(2,1)S(1)} %get-tuple-element.55), channel_id=1, source_target_pairs={{0,2},{2,0},{4,6},{6,4},{8,10},{10,8},{12,14},{14,12},{1,3},{3,1},... | collective-permute-start | bytes 737288 | tf_op jit(solution)/shard_map/ppermute | solution.py:289
  4.9 4.4 %collective-permute-start.1 = (f32[16,128]{1,0:T(8,128)S(1)}, f32[16,128]{1,0:T(8,128)S(1)}, u32[]{:S(2)}, u32[]{:S(2)}) collective-permute-start(f32[16,128]{1,0:T(8,128)S(1)} %maximum_select_fusion.2.after), channel_id=1, source_target_pairs={{0,4},{2,6},{4,0},{6,2},{8,12},{10,14},{12,8},{14,10},{1,5},{3,7},... | collective-permute-start | bytes 24584 | tf_op jit(solution)/shard_map/ppermute | solution.py:289
  9.3 4.7 %collective-permute-start.3 = (f32[32,128]{1,0:T(8,128)S(1)}, f32[32,128]{1,0:T(8,128)S(1)}, u32[]{:S(2)}, u32[]{:S(2)}) collective-permute-start(f32[32,128]{1,0:T(8,128)S(1)} %maximum_select_fusion.1), channel_id=1, source_target_pairs={{0,8},{2,10},{4,12},{6,14},{8,0},{10,2},{12,4},{14,6},{1,9},{3,11}... | collective-permute-start | bytes 49160 | tf_op jit(solution)/shard_map/ppermute | solution.py:289
  12.0 5.8 %collective-permute-start.2 = (bf16[153,512]{1,0:T(8,128)(2,1)S(1)}, bf16[153,512]{1,0:T(8,128)(2,1)S(1)}, u32[]{:S(2)}, u32[]{:S(2)}) collective-permute-start(bf16[153,512]{1,0:T(8,128)(2,1)S(1)} %shard_map.104.mine), channel_id=1, source_target_pairs={{0,2},{2,0},{4,6},{6,4},{8,10},{10,8},{12,14},{14,12},{1,3},{3,1},... | collective-permute-start | bytes 470024 | tf_op jit(solution)/shard_map/ppermute | solution.py:289
  16.1 6.1 %collective-permute-start.9 = (bf16[96,768]{1,0:T(8,128)(2,1)S(1)}, bf16[96,768]{1,0:T(8,128)(2,1)S(1)}, u32[]{:S(2)}, u32[]{:S(2)}) collective-permute-start(bf16[96,768]{1,0:T(8,128)(2,1)S(1)} %get-tuple-element.74), channel_id=1, source_target_pairs={{0,2},{2,0},{4,6},{6,4},{8,10},{10,8},{12,14},{14,12},{1,3},{3,1},... | collective-permute-start | bytes 442376 | tf_op jit(solution)/shard_map/ppermute | solution.py:289
  18.1 4.1 %collective-permute-start.5 = (bf16[153,128]{1,0:T(8,128)(2,1)S(1)}, bf16[153,128]{1,0:T(8,128)(2,1)S(1)}, u32[]{:S(2)}, u32[]{:S(2)}) collective-permute-start(bf16[153,128]{1,0:T(8,128)(2,1)S(1)} %get-tuple-element.60.after), channel_id=1, source_target_pairs={{0,4},{2,6},{4,0},{6,2},{8,12},{10,14},{12,8},{14,10},{1,5},{3,7},... | collective-permute-start | bytes 117512 | tf_op jit(solution)/shard_map/ppermute | solution.py:289
  20.1 4.7 %collective-permute-start.7 = (f32[64,128]{1,0:T(8,128)S(1)}, f32[64,128]{1,0:T(8,128)S(1)}, u32[]{:S(2)}, u32[]{:S(2)}) collective-permute-start(f32[64,128]{1,0:T(8,128)S(1)} %maximum_select_fusion.packed), channel_id=1, source_target_pairs={{0,2},{2,0},{4,6},{6,4},{8,10},{10,8},{12,14},{14,12},{1,3},{3,1},... | collective-permute-start | bytes 98312 | tf_op jit(solution)/shard_map/ppermute | solution.py:289
  22.2 7.1 %collective-permute-start.11 = (bf16[96,768]{1,0:T(8,128)(2,1)S(1)}, bf16[96,768]{1,0:T(8,128)(2,1)S(1)}, u32[]{:S(2)}, u32[]{:S(2)}) collective-permute-start(bf16[96,768]{1,0:T(8,128)(2,1)S(1)} %collective-permute-done.9.late), channel_id=1, source_target_pairs={{0,1},{1,0},{2,3},{3,2},{4,5},{5,4},{6,7},{7,6},{8,9},{9,8},{10,11... | collective-permute-start | bytes 442376 | tf_op jit(solution)/shard_map/ppermute | solution.py:292
  22.2 7.1 %collective-permute-start.10 = (bf16[160,768]{1,0:T(8,128)(2,1)S(1)}, bf16[160,768]{1,0:T(8,128)(2,1)S(1)}, u32[]{:S(2)}, u32[]{:S(2)}) collective-permute-start(bf16[160,768]{1,0:T(8,128)(2,1)S(1)} %collective-permute-done.4.near), channel_id=1, source_target_pairs={{0,1},{1,0},{2,3},{3,2},{4,5},{5,4},{6,7},{7,6},{8,9},{9,8},{10,11... | collective-permute-start | bytes 737288 | tf_op jit(solution)/shard_map/ppermute | solution.py:292
  22.7 5.4 %collective-permute-start.6 = (bf16[153,128]{1,0:T(8,128)(2,1)S(1)}, bf16[153,128]{1,0:T(8,128)(2,1)S(1)}, u32[]{:S(2)}, u32[]{:S(2)}) collective-permute-start(bf16[153,128]{1,0:T(8,128)(2,1)S(1)} %get-tuple-element.92), channel_id=1, source_target_pairs={{0,8},{2,10},{4,12},{6,14},{8,0},{10,2},{12,4},{14,6},{1,9},{3,11}... | collective-permute-start | bytes 117512 | tf_op jit(solution)/shard_map/ppermute | solution.py:289
  28.2 4.1 %collective-permute-start.8 = (bf16[153,128]{1,0:T(8,128)(2,1)S(1)}, bf16[153,128]{1,0:T(8,128)(2,1)S(1)}, u32[]{:S(2)}, u32[]{:S(2)}) collective-permute-start(bf16[153,128]{1,0:T(8,128)(2,1)S(1)} %get-tuple-element.69), channel_id=1, source_target_pairs={{0,2},{2,0},{4,6},{6,4},{8,10},{10,8},{12,14},{14,12},{1,3},{3,1},... | collective-permute-start | bytes 117512 | tf_op jit(solution)/shard_map/ppermute | solution.py:289
  34.9 5.6 %collective-permute-start.12 = (bf16[720,128]{1,0:T(8,128)(2,1)S(1)}, bf16[720,128]{1,0:T(8,128)(2,1)S(1)}, u32[]{:S(2)}, u32[]{:S(2)}) collective-permute-start(bf16[720,128]{1,0:T(8,128)(2,1)S(1)} %get-tuple-element.87), channel_id=1, source_target_pairs={{0,4},{2,6},{4,0},{6,2},{8,12},{10,14},{12,8},{14,10},{1,5},{3,7},... | collective-permute-start | bytes 552968 | tf_op jit(solution)/shard_map/ppermute | solution.py:289
  40.6 8.3 %collective-permute-start.13 = (bf16[720,128]{1,0:T(8,128)(2,1)S(1)}, bf16[720,128]{1,0:T(8,128)(2,1)S(1)}, u32[]{:S(2)}, u32[]{:S(2)}) collective-permute-start(bf16[720,128]{1,0:T(8,128)(2,1)S(1)} %shard_map.112.kept), channel_id=1, source_target_pairs={{0,8},{2,10},{4,12},{6,14},{8,0},{10,2},{12,4},{14,6},{1,9},{3,11}... | collective-permute-start | bytes 552968 | tf_op jit(solution)/shard_map/ppermute | solution.py:289
  48.9 5.6 %collective-permute-start.14 = (bf16[720,128]{1,0:T(8,128)(2,1)S(1)}, bf16[720,128]{1,0:T(8,128)(2,1)S(1)}, u32[]{:S(2)}, u32[]{:S(2)}) collective-permute-start(bf16[720,128]{1,0:T(8,128)(2,1)S(1)} %shard_map.113.refs_0_), channel_id=1, source_target_pairs={{0,4},{2,6},{4,0},{6,2},{8,12},{10,14},{12,8},{14,10},{1,5},{3,7},... | collective-permute-start | bytes 552968 | tf_op jit(solution)/shard_map/ppermute | solution.py:289
  49.0 7.1 %collective-permute-start.15 = (bf16[720,128]{1,0:T(8,128)(2,1)S(1)}, bf16[720,128]{1,0:T(8,128)(2,1)S(1)}, u32[]{:S(2)}, u32[]{:S(2)}) collective-permute-start(bf16[720,128]{1,0:T(8,128)(2,1)S(1)} %shard_map.113.refs_0_), channel_id=1, source_target_pairs={{0,2},{2,0},{4,6},{6,4},{8,10},{10,8},{12,14},{14,12},{1,3},{3,1},... | collective-permute-start | bytes 552968 | tf_op jit(solution)/shard_map/ppermute | solution.py:289
  54.5 5.5 %collective-permute-start.16 = (bf16[720,128]{1,0:T(8,128)(2,1)S(1)}, bf16[720,128]{1,0:T(8,128)(2,1)S(1)}, u32[]{:S(2)}, u32[]{:S(2)}) collective-permute-start(bf16[720,128]{1,0:T(8,128)(2,1)S(1)} %collective-permute-done.14.refs_1_), channel_id=1, source_target_pairs={{0,2},{2,0},{4,6},{6,4},{8,10},{10,8},{12,14},{14,12},{1,3},{3,1},... | collective-permute-start | bytes 552968 | tf_op jit(solution)/shard_map/ppermute | solution.py:289
  55.4 5.2 %collective-permute-start.17 = (bf16[720,128]{1,0:T(8,128)(2,1)S(1)}, bf16[720,128]{1,0:T(8,128)(2,1)S(1)}, u32[]{:S(2)}, u32[]{:S(2)}) collective-permute-start(bf16[720,128]{1,0:T(8,128)(2,1)S(1)} %shard_map.113.refs_0_), channel_id=1, source_target_pairs={{0,1},{1,0},{2,3},{3,2},{4,5},{5,4},{6,7},{7,6},{8,9},{9,8},{10,11... | collective-permute-start | bytes 552968 | tf_op jit(solution)/shard_map/ppermute | solution.py:292
  55.4 5.2 %collective-permute-start.18 = (bf16[720,128]{1,0:T(8,128)(2,1)S(1)}, bf16[720,128]{1,0:T(8,128)(2,1)S(1)}, u32[]{:S(2)}, u32[]{:S(2)}) collective-permute-start(bf16[720,128]{1,0:T(8,128)(2,1)S(1)} %collective-permute-done.14.refs_1_), channel_id=1, source_target_pairs={{0,1},{1,0},{2,3},{3,2},{4,5},{5,4},{6,7},{7,6},{8,9},{9,8},{10,11... | collective-permute-start | bytes 552968 | tf_op jit(solution)/shard_map/ppermute | solution.py:292
  56.1 4.5 %collective-permute-start.19 = (bf16[720,128]{1,0:T(8,128)(2,1)S(1)}, bf16[720,128]{1,0:T(8,128)(2,1)S(1)}, u32[]{:S(2)}, u32[]{:S(2)}) collective-permute-start(bf16[720,128]{1,0:T(8,128)(2,1)S(1)} %collective-permute-done.15.refs_2_), channel_id=1, source_target_pairs={{0,1},{1,0},{2,3},{3,2},{4,5},{5,4},{6,7},{7,6},{8,9},{9,8},{10,11... | collective-permute-start | bytes 552968 | tf_op jit(solution)/shard_map/ppermute | solution.py:292
  60.0 1.4 %collective-permute-start.20 = (bf16[720,128]{1,0:T(8,128)(2,1)S(1)}, bf16[720,128]{1,0:T(8,128)(2,1)S(1)}, u32[]{:S(2)}, u32[]{:S(2)}) collective-permute-start(bf16[720,128]{1,0:T(8,128)(2,1)S(1)} %collective-permute-done.16.refs_3_), channel_id=1, source_target_pairs={{0,1},{1,0},{2,3},{3,2},{4,5},{5,4},{6,7},{7,6},{8,9},{9,8},{10,11... | collective-permute-start | bytes 552968 | tf_op jit(solution)/shard_map/ppermute | solution.py:292

commit v6 on v5

--- a/solution.py
+++ b/solution.py
@@ -19,6 +19,10 @@
 
 def nt(a, b):
     return lax.dot_general(a, b, (((1,), (1,)), ((), ())), preferred_element_type=F32)
+
+
+def tn(a, b):
+    return lax.dot_general(a, b, (((0,), (0,)), ((), ())), preferred_element_type=F32)
 
 
 def split(v):
@@ -181,15 +185,18 @@
     cols = pl.ds(device_slice(), LANE)
     w2_rows = w2[cols, :]
     sides = (slice(0, n), slice(n, 2 * n))
-    left = [jnp.concatenate([high[at], low[at], high[at], far_high[at], far_low[at]], axis=1) for at in sides]
-    right = jnp.concatenate([top, top, rest, far, far], axis=1)
-    g = [nt(v, right).astype(BF) for v in left]
+    own = jnp.concatenate([top, top], axis=1)
+    other = jnp.concatenate([rest, far], axis=1)
+    g = []
+    for at in sides:
+        total = nt(jnp.concatenate([high[at], low[at]], axis=1), own)
+        total += nt(jnp.concatenate([high[at], far_high[at]], axis=1), other)
+        g.append((total + nt(far_low[at], far)).astype(BF))
     b2 = [(nn(v, w3t[...]) * s[...]).astype(BF) for v, s in zip(g, (s2, ps2))]
     two[0] = b2[0]
     two[1] = b2[1]
     b1 = [(nt(v, w2_rows) * s[...]).astype(BF) for v, s in zip(b2, (s1, ps1))]
-    gt = [nt(right, v).astype(BF) for v in left]
-    acc[depth + hidden : depth + hidden + classes] = nn(gt[0], h2[...]) + nn(gt[1], ph2[...])
+    acc[depth + hidden : depth + hidden + classes] = tn(g[0], h2[...]) + tn(g[1], ph2[...])
     acc[depth : depth + hidden] = nn(h1t[...], two[0, :, cols]) + nn(ph1t[...], two[1, :, cols])
     acc[:depth] = nn(xt[...], b1[0]) + nn(pxt[...], b1[1])
     blank = acc.shape[0] - (depth + hidden + classes)

time: 63 us -> 62.6 us (level)
  no operation moved by 1% of the time
where the time goes in v6:
time: 62.6 us; the launch traced here: 62.4 us
  waiting for transfers between devices  25.6 us (41%)
  starting transfers between devices  20 us (32%)
  Pallas kernels  15.4 us (25%)
  between operations  0.74 us (1%)
    ppermute x14, waiting for transfers between devices, over(): return lax.ppermute(x, 'owner', [(i, i ^ bit) for i in range(owners)])  24.8 us
    ppermute x14, starting transfers between devices, over(): return lax.ppermute(x, 'owner', [(i, i ^ bit) for i in range(owners)])  18.4 us
    pallas_call x13, Pallas kernels, whole(): pl.pallas_call(kernel, out_shape=[jax.ShapeDtypeStruct(shape, kind) for s...  15.4 us
    ppermute x7, starting transfers between devices, other_core(): return lax.ppermute(x, 'batch', [(0, 1), (1, 0)])  1.54 us
  transfers between devices with their start and end apart: 21, of which 11 were waited for; matrix products, arithmetic and copies ran while one was open for 1% of the time, Pallas kernels for 17%

profile of v6, /device:TPU:0, one launch (start us, length us, event | category | flops | bytes accessed | tf_op | source)
XLA Modules:
  0.0 62.4 jit_solution(10598615750629543770)
XLA Ops:
  0.6 1.1 %shard_map.102 = (f32[16,64]{1,0:T(8,128)S(1)}, bf16[160,768]{1,0:T(8,128)(2,1)S(1)}, bf16[96,768]{1,0:T(8,128)(2,1)S(1)}) custom-call(s32[16,32]{1,0:T(8,128)} %ids_hbm.1, f32[16,32]{1,0:T(8,128)} %wts_hbm.1, s32[1,16]{1,0:T(1,128)} %bitcast.6, bf16[512,768]{1,0:T(8,128)(2,1)} %refs_0_.1), custom_call_target="tpu_custom_call" | custom-call | flops 1000000 | bytes 1953 | tf_op jit(solution)/shard_map/pallas_call | solution.py:271
  2.3 2.6 %collective-permute-start.4 = (bf16[160,768]{1,0:T(8,128)(2,1)S(1)}, bf16[160,768]{1,0:T(8,128)(2,1)S(1)}, u32[]{:S(2)}, u32[]{:S(2)}) collective-permute-start(bf16[160,768]{1,0:T(8,128)(2,1)S(1)} %get-tuple-element.55), channel_id=1, source_target_pairs={{0,2},{2,0},{4,6},{6,4},{8,10},{10,8},{12,14},{14,12},{1,3},{3,1},... | collective-permute-start | bytes 737288 | tf_op jit(solution)/shard_map/ppermute | solution.py:296
  4.9 1.6 %collective-permute-start.1 = (f32[16,128]{1,0:T(8,128)S(1)}, f32[16,128]{1,0:T(8,128)S(1)}, u32[]{:S(2)}, u32[]{:S(2)}) collective-permute-start(f32[16,128]{1,0:T(8,128)S(1)} %maximum_select_fusion.2.after), channel_id=1, source_target_pairs={{0,4},{2,6},{4,0},{6,2},{8,12},{10,14},{12,8},{14,10},{1,5},{3,7},... | collective-permute-start | bytes 24584 | tf_op jit(solution)/shard_map/ppermute | solution.py:296
  6.5 1.6 %shard_map.103 = (bf16[512,768]{1,0:T(8,128)(2,1)S(1)}, bf16[768,512]{1,0:T(8,128)(2,1)S(1)}, bf16[512,512]{1,0:T(8,128)(2,1)S(1)}, bf16[153,512]{1,0:T(8,128)(2,1)S(1)}) custom-call(f32[16,128]{1,0:T(8,128)S(1)} %maximum_select_fusion.2.after, bf16[512,768]{1,0:T(8,128)(2,1)} %refs_0_.1, bf16[768,512]{1,0:T(8,128)(2,1)} %refs_1_.1, ...), custom_call_target="tpu_custom_call" | custom-call | flops 1000000 | bytes 1953 | tf_op jit(solution)/shard_map/pallas_call | solution.py:271
  8.1 1.2 %shard_map.104.mine = bf16[153,512]{1,0:T(8,128)(2,1)S(1)} custom-call(bf16[512,768]{1,0:T(8,128)(2,1)S(1)} %get-tuple-element.49.x, bf16[768,512]{1,0:T(8,128)(2,1)S(1)} %get-tuple-element.50.w1, bf16[512,512]{1,0:T(8,128)(2,1)S(1)} %get-tuple-element.51.w2, bf16[153,512]{1,0:T(8,128)(2,1)S(1)} %get-tuple-element.52.w3.w3t, ...), custom_call_target="tpu_custom_call" | custom-call | flops 1000 | bytes 1 | tf_op jit(solution)/shard_map/pallas_call | solution.py:271
  9.3 2.7 %collective-permute-start.3 = (f32[32,128]{1,0:T(8,128)S(1)}, f32[32,128]{1,0:T(8,128)S(1)}, u32[]{:S(2)}, u32[]{:S(2)}) collective-permute-start(f32[32,128]{1,0:T(8,128)S(1)} %maximum_select_fusion.1), channel_id=1, source_target_pairs={{0,8},{2,10},{4,12},{6,14},{8,0},{10,2},{12,4},{14,6},{1,9},{3,11}... | collective-permute-start | bytes 49160 | tf_op jit(solution)/shard_map/ppermute | solution.py:296
  12.0 1.1 %collective-permute-start.2 = (bf16[153,512]{1,0:T(8,128)(2,1)S(1)}, bf16[153,512]{1,0:T(8,128)(2,1)S(1)}, u32[]{:S(2)}, u32[]{:S(2)}) collective-permute-start(bf16[153,512]{1,0:T(8,128)(2,1)S(1)} %shard_map.104.mine), channel_id=1, source_target_pairs={{0,2},{2,0},{4,6},{6,4},{8,10},{10,8},{12,14},{14,12},{1,3},{3,1},... | collective-permute-start | bytes 470024 | tf_op jit(solution)/shard_map/ppermute | solution.py:296
  14.0 2.0 %shard_map.105 = (bf16[1024,128]{1,0:T(8,128)(2,1)S(1)}, bf16[1024,128]{1,0:T(8,128)(2,1)S(1)}, s32[1,128]{1,0:T(1,128)S(1)}) custom-call(f32[64,128]{1,0:T(8,128)S(1)} %maximum_select_fusion.packed), custom_call_target="tpu_custom_call" | custom-call | flops 1000000000 | bytes 1953125 | tf_op jit(solution)/shard_map/pallas_call | solution.py:271
  16.1 1.2 %collective-permute-start.9 = (bf16[96,768]{1,0:T(8,128)(2,1)S(1)}, bf16[96,768]{1,0:T(8,128)(2,1)S(1)}, u32[]{:S(2)}, u32[]{:S(2)}) collective-permute-start(bf16[96,768]{1,0:T(8,128)(2,1)S(1)} %get-tuple-element.74), channel_id=1, source_target_pairs={{0,2},{2,0},{4,6},{6,4},{8,10},{10,8},{12,14},{14,12},{1,3},{3,1},... | collective-permute-start | bytes 442376 | tf_op jit(solution)/shard_map/ppermute | solution.py:296
  18.7 1.4 %shard_map.107 = (bf16[768,512]{1,0:T(8,128)(2,1)S(1)}, bf16[512,512]{1,0:T(8,128)(2,1)S(1)}, bf16[512,128]{1,0:T(8,128)(2,1)S(1)}, f32[512,128]{1,0:T(8,128)S(1)}, f32[512,512]{1,0:T(8,128)S(1)}) custom-call(bf16[512,768]{1,0:T(8,128)(2,1)S(1)} %get-tuple-element.49.x, bf16[768,512]{1,0:T(8,128)(2,1)S(1)} %get-tuple-element.50.w1, ...), custom_call_target="tpu_custom_call" | custom-call | flops 1000 | bytes 1 | tf_op jit(solution)/shard_map/pallas_call | solution.py:271
  20.1 1.1 %collective-permute-start.7 = (f32[64,128]{1,0:T(8,128)S(1)}, f32[64,128]{1,0:T(8,128)S(1)}, u32[]{:S(2)}, u32[]{:S(2)}) collective-permute-start(f32[64,128]{1,0:T(8,128)S(1)} %maximum_select_fusion.packed), channel_id=1, source_target_pairs={{0,2},{2,0},{4,6},{6,4},{8,10},{10,8},{12,14},{14,12},{1,3},{3,1},... | collective-permute-start | bytes 98312 | tf_op jit(solution)/shard_map/ppermute | solution.py:296
  22.7 2.1 %collective-permute-start.6 = (bf16[153,128]{1,0:T(8,128)(2,1)S(1)}, bf16[153,128]{1,0:T(8,128)(2,1)S(1)}, u32[]{:S(2)}, u32[]{:S(2)}) collective-permute-start(bf16[153,128]{1,0:T(8,128)(2,1)S(1)} %get-tuple-element.92), channel_id=1, source_target_pairs={{0,8},{2,10},{4,12},{6,14},{8,0},{10,2},{12,4},{14,6},{1,9},{3,11}... | collective-permute-start | bytes 117512 | tf_op jit(solution)/shard_map/ppermute | solution.py:296
  24.8 2.4 %shard_map.108 = (bf16[1024,128]{1,0:T(8,128)(2,1)S(1)}, bf16[1024,128]{1,0:T(8,128)(2,1)S(1)}, s32[1,128]{1,0:T(1,128)}) custom-call(f32[64,128]{1,0:T(8,128)S(1)} %collective-permute-done.7.packed), custom_call_target="tpu_custom_call" | custom-call | flops 1000000000 | bytes 1953125 | tf_op jit(solution)/shard_map/pallas_call | solution.py:271
  28.2 1.1 %collective-permute-start.8 = (bf16[153,128]{1,0:T(8,128)(2,1)S(1)}, bf16[153,128]{1,0:T(8,128)(2,1)S(1)}, u32[]{:S(2)}, u32[]{:S(2)}) collective-permute-start(bf16[153,128]{1,0:T(8,128)(2,1)S(1)} %get-tuple-element.69), channel_id=1, source_target_pairs={{0,2},{2,0},{4,6},{6,4},{8,10},{10,8},{12,14},{14,12},{1,3},{3,1},... | collective-permute-start | bytes 117512 | tf_op jit(solution)/shard_map/ppermute | solution.py:296
  29.2 1.5 %shard_map.110 = (bf16[768,512]{1,0:T(8,128)(2,1)S(1)}, bf16[512,512]{1,0:T(8,128)(2,1)S(1)}, bf16[512,128]{1,0:T(8,128)(2,1)S(1)}, f32[512,128]{1,0:T(8,128)S(1)}, f32[512,512]{1,0:T(8,128)S(1)}) custom-call(bf16[160,768]{1,0:T(8,128)(2,1)S(1)} %collective-permute-done.4.near, bf16[96,768]{1,0:T(8,128)(2,1)S(1)} %collective-permute-done.9.late, ...), custom_call_target="tpu_custom_call" | custom-call | flops 2000000000 | bytes 3906250 | tf_op jit(solution)/shard_map/pallas_call | solution.py:271
  30.7 1.5 %collective-permute-done.8.far_grad = bf16[153,128]{1,0:T(8,128)(2,1)S(1)} collective-permute-done((bf16[153,128]{1,0:T(8,128)(2,1)S(1)}, bf16[153,128]{1,0:T(8,128)(2,1)S(1)}, u32[]{:S(2)}, u32[]{:S(2)}) %collective-permute-start.8) | collective-permute-done | bytes 39200 | tf_op jit(solution)/shard_map/ppermute | solution.py:296
  32.2 2.3 %shard_map.111 = (bf16[720,128]{1,0:T(8,128)(2,1)S(1)}, f32[720,128]{1,0:T(8,128)S(1)}) custom-call(f32[153,128]{1,0:T(8,128)S(1)} %get-tuple-element.68.grad, bf16[153,128]{1,0:T(8,128)(2,1)S(1)} %collective-permute-done.8.far_grad, bf16[1024,128]{1,0:T(8,128)(2,1)S(1)} %get-tuple-element.57.high, bf16[1024,128]{1,0:T(8,128)(2,1)S(1)} %get-tuple-element.58.low, ...), custom_call_target="tpu_custom_call" | custom-call | flops 1000000 | bytes 1953 | tf_op jit(solution)/shard_map/pallas_call | solution.py:271
  34.8 5.3 %collective-permute-done.12.got = bf16[720,128]{1,0:T(8,128)(2,1)S(1)} collective-permute-done((bf16[720,128]{1,0:T(8,128)(2,1)S(1)}, bf16[720,128]{1,0:T(8,128)(2,1)S(1)}, u32[]{:S(2)}, u32[]{:S(2)}) %collective-permute-start.12) | collective-permute-done | bytes 184352 | tf_op jit(solution)/shard_map/ppermute | solution.py:296
  40.1 2.3 %collective-permute-start.13 = (bf16[720,128]{1,0:T(8,128)(2,1)S(1)}, bf16[720,128]{1,0:T(8,128)(2,1)S(1)}, u32[]{:S(2)}, u32[]{:S(2)}) collective-permute-start(bf16[720,128]{1,0:T(8,128)(2,1)S(1)} %shard_map.112.kept), channel_id=1, source_target_pairs={{0,8},{2,10},{4,12},{6,14},{8,0},{10,2},{12,4},{14,6},{1,9},{3,11}... | collective-permute-start | bytes 552968 | tf_op jit(solution)/shard_map/ppermute | solution.py:296
  42.4 6.0 %collective-permute-done.13.got = bf16[720,128]{1,0:T(8,128)(2,1)S(1)} collective-permute-done((bf16[720,128]{1,0:T(8,128)(2,1)S(1)}, bf16[720,128]{1,0:T(8,128)(2,1)S(1)}, u32[]{:S(2)}, u32[]{:S(2)}) %collective-permute-start.13) | collective-permute-done | bytes 184352 | tf_op jit(solution)/shard_map/ppermute | solution.py:296
  48.5 1.0 %collective-permute-start.15 = (bf16[720,128]{1,0:T(8,128)(2,1)S(1)}, bf16[720,128]{1,0:T(8,128)(2,1)S(1)}, u32[]{:S(2)}, u32[]{:S(2)}) collective-permute-start(bf16[720,128]{1,0:T(8,128)(2,1)S(1)} %shard_map.113.refs_0_), channel_id=1, source_target_pairs={{0,2},{2,0},{4,6},{6,4},{8,10},{10,8},{12,14},{14,12},{1,3},{3,1},... | collective-permute-start | bytes 552968 | tf_op jit(solution)/shard_map/ppermute | solution.py:296
  49.5 4.5 %collective-permute-done.14.refs_1_ = bf16[720,128]{1,0:T(8,128)(2,1)S(1)} collective-permute-done((bf16[720,128]{1,0:T(8,128)(2,1)S(1)}, bf16[720,128]{1,0:T(8,128)(2,1)S(1)}, u32[]{:S(2)}, u32[]{:S(2)}) %collective-permute-start.14) | collective-permute-done | bytes 184352 | tf_op jit(solution)/shard_map/ppermute | solution.py:296
  55.7 3.9 %collective-permute-done.16.refs_3_ = bf16[720,128]{1,0:T(8,128)(2,1)S(1)} collective-permute-done((bf16[720,128]{1,0:T(8,128)(2,1)S(1)}, bf16[720,128]{1,0:T(8,128)(2,1)S(1)}, u32[]{:S(2)}, u32[]{:S(2)}) %collective-permute-start.16) | collective-permute-done | bytes 184352 | tf_op jit(solution)/shard_map/ppermute | solution.py:296
  61.0 1.4 %shard_map.114 = (bf16[768,512]{1,0:T(8,128)(2,1)}, bf16[512,512]{1,0:T(8,128)(2,1)}, bf16[153,512]{1,0:T(8,128)(2,1)}) custom-call(bf16[720,128]{1,0:T(8,128)(2,1)S(1)} %shard_map.113.refs_0_, bf16[720,128]{1,0:T(8,128)(2,1)S(1)} %collective-permute-done.14.refs_1_, bf16[720,128]{1,0:T(8,128)(2,1)S(1)} %collective-permute-done.15.refs_2_, ...), custom_call_target="tpu_custom_call" | custom-call | flops 1000000 | bytes 1953 | tf_op jit(solution)/shard_map/pallas_call | solution.py:271
  (36 shorter events, 8.9 us)
Async XLA Ops:
  1.8 3.1 %collective-permute-start = (f32[16,64]{1,0:T(8,128)S(1)}, f32[16,64]{1,0:T(8,128)S(1)}, u32[]{:S(2)}, u32[]{:S(2)}) collective-permute-start(f32[16,64]{1,0:T(8,128)S(1)} %get-tuple-element.48), channel_id=1, source_target_pairs={{0,1},{1,0},{2,3},{3,2},{4,5},{5,4},{6,7},{7,6},{8,9},{9,8},{10,11... | collective-permute-start | bytes 12296 | tf_op jit(solution)/shard_map/ppermute | solution.py:299
  2.3 11.7 %collective-permute-start.4 = (bf16[160,768]{1,0:T(8,128)(2,1)S(1)}, bf16[160,768]{1,0:T(8,128)(2,1)S(1)}, u32[]{:S(2)}, u32[]{:S(2)}) collective-permute-start(bf16[160,768]{1,0:T(8,128)(2,1)S(1)} %get-tuple-element.55), channel_id=1, source_target_pairs={{0,2},{2,0},{4,6},{6,4},{8,10},{10,8},{12,14},{14,12},{1,3},{3,1},... | collective-permute-start | bytes 737288 | tf_op jit(solution)/shard_map/ppermute | solution.py:296
  4.9 4.4 %collective-permute-start.1 = (f32[16,128]{1,0:T(8,128)S(1)}, f32[16,128]{1,0:T(8,128)S(1)}, u32[]{:S(2)}, u32[]{:S(2)}) collective-permute-start(f32[16,128]{1,0:T(8,128)S(1)} %maximum_select_fusion.2.after), channel_id=1, source_target_pairs={{0,4},{2,6},{4,0},{6,2},{8,12},{10,14},{12,8},{14,10},{1,5},{3,7},... | collective-permute-start | bytes 24584 | tf_op jit(solution)/shard_map/ppermute | solution.py:296
  9.3 4.7 %collective-permute-start.3 = (f32[32,128]{1,0:T(8,128)S(1)}, f32[32,128]{1,0:T(8,128)S(1)}, u32[]{:S(2)}, u32[]{:S(2)}) collective-permute-start(f32[32,128]{1,0:T(8,128)S(1)} %maximum_select_fusion.1), channel_id=1, source_target_pairs={{0,8},{2,10},{4,12},{6,14},{8,0},{10,2},{12,4},{14,6},{1,9},{3,11}... | collective-permute-start | bytes 49160 | tf_op jit(solution)/shard_map/ppermute | solution.py:296
  12.0 5.8 %collective-permute-start.2 = (bf16[153,512]{1,0:T(8,128)(2,1)S(1)}, bf16[153,512]{1,0:T(8,128)(2,1)S(1)}, u32[]{:S(2)}, u32[]{:S(2)}) collective-permute-start(bf16[153,512]{1,0:T(8,128)(2,1)S(1)} %shard_map.104.mine), channel_id=1, source_target_pairs={{0,2},{2,0},{4,6},{6,4},{8,10},{10,8},{12,14},{14,12},{1,3},{3,1},... | collective-permute-start | bytes 470024 | tf_op jit(solution)/shard_map/ppermute | solution.py:296
  16.1 6.1 %collective-permute-start.9 = (bf16[96,768]{1,0:T(8,128)(2,1)S(1)}, bf16[96,768]{1,0:T(8,128)(2,1)S(1)}, u32[]{:S(2)}, u32[]{:S(2)}) collective-permute-start(bf16[96,768]{1,0:T(8,128)(2,1)S(1)} %get-tuple-element.74), channel_id=1, source_target_pairs={{0,2},{2,0},{4,6},{6,4},{8,10},{10,8},{12,14},{14,12},{1,3},{3,1},... | collective-permute-start | bytes 442376 | tf_op jit(solution)/shard_map/ppermute | solution.py:296
  18.1 4.1 %collective-permute-start.5 = (bf16[153,128]{1,0:T(8,128)(2,1)S(1)}, bf16[153,128]{1,0:T(8,128)(2,1)S(1)}, u32[]{:S(2)}, u32[]{:S(2)}) collective-permute-start(bf16[153,128]{1,0:T(8,128)(2,1)S(1)} %get-tuple-element.60.after), channel_id=1, source_target_pairs={{0,4},{2,6},{4,0},{6,2},{8,12},{10,14},{12,8},{14,10},{1,5},{3,7},... | collective-permute-start | bytes 117512 | tf_op jit(solution)/shard_map/ppermute | solution.py:296
  20.1 4.7 %collective-permute-start.7 = (f32[64,128]{1,0:T(8,128)S(1)}, f32[64,128]{1,0:T(8,128)S(1)}, u32[]{:S(2)}, u32[]{:S(2)}) collective-permute-start(f32[64,128]{1,0:T(8,128)S(1)} %maximum_select_fusion.packed), channel_id=1, source_target_pairs={{0,2},{2,0},{4,6},{6,4},{8,10},{10,8},{12,14},{14,12},{1,3},{3,1},... | collective-permute-start | bytes 98312 | tf_op jit(solution)/shard_map/ppermute | solution.py:296
  22.2 7.1 %collective-permute-start.11 = (bf16[96,768]{1,0:T(8,128)(2,1)S(1)}, bf16[96,768]{1,0:T(8,128)(2,1)S(1)}, u32[]{:S(2)}, u32[]{:S(2)}) collective-permute-start(bf16[96,768]{1,0:T(8,128)(2,1)S(1)} %collective-permute-done.9.late), channel_id=1, source_target_pairs={{0,1},{1,0},{2,3},{3,2},{4,5},{5,4},{6,7},{7,6},{8,9},{9,8},{10,11... | collective-permute-start | bytes 442376 | tf_op jit(solution)/shard_map/ppermute | solution.py:299
  22.2 7.1 %collective-permute-start.10 = (bf16[160,768]{1,0:T(8,128)(2,1)S(1)}, bf16[160,768]{1,0:T(8,128)(2,1)S(1)}, u32[]{:S(2)}, u32[]{:S(2)}) collective-permute-start(bf16[160,768]{1,0:T(8,128)(2,1)S(1)} %collective-permute-done.4.near), channel_id=1, source_target_pairs={{0,1},{1,0},{2,3},{3,2},{4,5},{5,4},{6,7},{7,6},{8,9},{9,8},{10,11... | collective-permute-start | bytes 737288 | tf_op jit(solution)/shard_map/ppermute | solution.py:299
  22.7 5.4 %collective-permute-start.6 = (bf16[153,128]{1,0:T(8,128)(2,1)S(1)}, bf16[153,128]{1,0:T(8,128)(2,1)S(1)}, u32[]{:S(2)}, u32[]{:S(2)}) collective-permute-start(bf16[153,128]{1,0:T(8,128)(2,1)S(1)} %get-tuple-element.92), channel_id=1, source_target_pairs={{0,8},{2,10},{4,12},{6,14},{8,0},{10,2},{12,4},{14,6},{1,9},{3,11}... | collective-permute-start | bytes 117512 | tf_op jit(solution)/shard_map/ppermute | solution.py:296
  28.2 4.1 %collective-permute-start.8 = (bf16[153,128]{1,0:T(8,128)(2,1)S(1)}, bf16[153,128]{1,0:T(8,128)(2,1)S(1)}, u32[]{:S(2)}, u32[]{:S(2)}) collective-permute-start(bf16[153,128]{1,0:T(8,128)(2,1)S(1)} %get-tuple-element.69), channel_id=1, source_target_pairs={{0,2},{2,0},{4,6},{6,4},{8,10},{10,8},{12,14},{14,12},{1,3},{3,1},... | collective-permute-start | bytes 117512 | tf_op jit(solution)/shard_map/ppermute | solution.py:296
  34.5 5.6 %collective-permute-start.12 = (bf16[720,128]{1,0:T(8,128)(2,1)S(1)}, bf16[720,128]{1,0:T(8,128)(2,1)S(1)}, u32[]{:S(2)}, u32[]{:S(2)}) collective-permute-start(bf16[720,128]{1,0:T(8,128)(2,1)S(1)} %get-tuple-element.87), channel_id=1, source_target_pairs={{0,4},{2,6},{4,0},{6,2},{8,12},{10,14},{12,8},{14,10},{1,5},{3,7},... | collective-permute-start | bytes 552968 | tf_op jit(solution)/shard_map/ppermute | solution.py:296
  40.1 8.3 %collective-permute-start.13 = (bf16[720,128]{1,0:T(8,128)(2,1)S(1)}, bf16[720,128]{1,0:T(8,128)(2,1)S(1)}, u32[]{:S(2)}, u32[]{:S(2)}) collective-permute-start(bf16[720,128]{1,0:T(8,128)(2,1)S(1)} %shard_map.112.kept), channel_id=1, source_target_pairs={{0,8},{2,10},{4,12},{6,14},{8,0},{10,2},{12,4},{14,6},{1,9},{3,11}... | collective-permute-start | bytes 552968 | tf_op jit(solution)/shard_map/ppermute | solution.py:296
  48.5 5.6 %collective-permute-start.14 = (bf16[720,128]{1,0:T(8,128)(2,1)S(1)}, bf16[720,128]{1,0:T(8,128)(2,1)S(1)}, u32[]{:S(2)}, u32[]{:S(2)}) collective-permute-start(bf16[720,128]{1,0:T(8,128)(2,1)S(1)} %shard_map.113.refs_0_), channel_id=1, source_target_pairs={{0,4},{2,6},{4,0},{6,2},{8,12},{10,14},{12,8},{14,10},{1,5},{3,7},... | collective-permute-start | bytes 552968 | tf_op jit(solution)/shard_map/ppermute | solution.py:296
  48.5 7.1 %collective-permute-start.15 = (bf16[720,128]{1,0:T(8,128)(2,1)S(1)}, bf16[720,128]{1,0:T(8,128)(2,1)S(1)}, u32[]{:S(2)}, u32[]{:S(2)}) collective-permute-start(bf16[720,128]{1,0:T(8,128)(2,1)S(1)} %shard_map.113.refs_0_), channel_id=1, source_target_pairs={{0,2},{2,0},{4,6},{6,4},{8,10},{10,8},{12,14},{14,12},{1,3},{3,1},... | collective-permute-start | bytes 552968 | tf_op jit(solution)/shard_map/ppermute | solution.py:296
  54.1 5.5 %collective-permute-start.16 = (bf16[720,128]{1,0:T(8,128)(2,1)S(1)}, bf16[720,128]{1,0:T(8,128)(2,1)S(1)}, u32[]{:S(2)}, u32[]{:S(2)}) collective-permute-start(bf16[720,128]{1,0:T(8,128)(2,1)S(1)} %collective-permute-done.14.refs_1_), channel_id=1, source_target_pairs={{0,2},{2,0},{4,6},{6,4},{8,10},{10,8},{12,14},{14,12},{1,3},{3,1},... | collective-permute-start | bytes 552968 | tf_op jit(solution)/shard_map/ppermute | solution.py:296
  55.0 5.2 %collective-permute-start.17 = (bf16[720,128]{1,0:T(8,128)(2,1)S(1)}, bf16[720,128]{1,0:T(8,128)(2,1)S(1)}, u32[]{:S(2)}, u32[]{:S(2)}) collective-permute-start(bf16[720,128]{1,0:T(8,128)(2,1)S(1)} %shard_map.113.refs_0_), channel_id=1, source_target_pairs={{0,1},{1,0},{2,3},{3,2},{4,5},{5,4},{6,7},{7,6},{8,9},{9,8},{10,11... | collective-permute-start | bytes 552968 | tf_op jit(solution)/shard_map/ppermute | solution.py:299
  55.0 5.2 %collective-permute-start.18 = (bf16[720,128]{1,0:T(8,128)(2,1)S(1)}, bf16[720,128]{1,0:T(8,128)(2,1)S(1)}, u32[]{:S(2)}, u32[]{:S(2)}) collective-permute-start(bf16[720,128]{1,0:T(8,128)(2,1)S(1)} %collective-permute-done.14.refs_1_), channel_id=1, source_target_pairs={{0,1},{1,0},{2,3},{3,2},{4,5},{5,4},{6,7},{7,6},{8,9},{9,8},{10,11... | collective-permute-start | bytes 552968 | tf_op jit(solution)/shard_map/ppermute | solution.py:299
  55.7 4.5 %collective-permute-start.19 = (bf16[720,128]{1,0:T(8,128)(2,1)S(1)}, bf16[720,128]{1,0:T(8,128)(2,1)S(1)}, u32[]{:S(2)}, u32[]{:S(2)}) collective-permute-start(bf16[720,128]{1,0:T(8,128)(2,1)S(1)} %collective-permute-done.15.refs_2_), channel_id=1, source_target_pairs={{0,1},{1,0},{2,3},{3,2},{4,5},{5,4},{6,7},{7,6},{8,9},{9,8},{10,11... | collective-permute-start | bytes 552968 | tf_op jit(solution)/shard_map/ppermute | solution.py:299
  59.6 1.4 %collective-permute-start.20 = (bf16[720,128]{1,0:T(8,128)(2,1)S(1)}, bf16[720,128]{1,0:T(8,128)(2,1)S(1)}, u32[]{:S(2)}, u32[]{:S(2)}) collective-permute-start(bf16[720,128]{1,0:T(8,128)(2,1)S(1)} %collective-permute-done.16.refs_3_), channel_id=1, source_target_pairs={{0,1},{1,0},{2,3},{3,2},{4,5},{5,4},{6,7},{7,6},{8,9},{9,8},{10,11... | collective-permute-start | bytes 552968 | tf_op jit(solution)/shard_map/ppermute | solution.py:299

commit v7 on v6

--- a/solution.py
+++ b/solution.py
@@ -130,7 +130,7 @@
     label[...] = cls[0:1].astype(jnp.int32)
     ids[...] = (coded - cls * nodes).astype(jnp.int32)
     me = lax.axis_index("owner")
-    block = 64
+    block = 128
     per_side = node_dev // block
 
     def step(i, carry):

time: 62.6 us -> 62.7 us (level)
  waiting for transfers between devices: 25.6 us -> 26.5 us
    ppermute x14, waiting for transfers between devices: 24.8 us -> 25.7 us  [over(): return lax.ppermute(x, 'owner', [(i, i ^ bit) for i in range(owners)])]
  transfers between devices with their start and end apart: 21 -> 21, of which waited for: 11 -> 11; matrix products, arithmetic and copies ran while one was open for 1% -> 1% of each run, Pallas kernels for 17% -> 16%
where the time goes in v7:
time: 62.7 us; the launch traced here: 62.5 us
  waiting for transfers between devices  26.5 us (42%)
  starting transfers between devices  19.5 us (31%)
  Pallas kernels  15 us (24%)
  between operations  0.75 us (1%)
    ppermute x14, waiting for transfers between devices, over(): return lax.ppermute(x, 'owner', [(i, i ^ bit) for i in range(owners)])  25.7 us
    ppermute x14, starting transfers between devices, over(): return lax.ppermute(x, 'owner', [(i, i ^ bit) for i in range(owners)])  18 us
    pallas_call x13, Pallas kernels, whole(): pl.pallas_call(kernel, out_shape=[jax.ShapeDtypeStruct(shape, kind) for s...  15 us
    ppermute x7, starting transfers between devices, other_core(): return lax.ppermute(x, 'batch', [(0, 1), (1, 0)])  1.54 us
  transfers between devices with their start and end apart: 21, of which 11 were waited for; matrix products, arithmetic and copies ran while one was open for 1% of the time, Pallas kernels for 16%

profile of v7, /device:TPU:0, one launch (start us, length us, event | category | flops | bytes accessed | tf_op | source)
XLA Modules:
  0.0 62.5 jit_solution(13779142354431126642)
XLA Ops:
  0.6 1.1 %shard_map.102 = (f32[16,64]{1,0:T(8,128)S(1)}, bf16[160,768]{1,0:T(8,128)(2,1)S(1)}, bf16[96,768]{1,0:T(8,128)(2,1)S(1)}) custom-call(s32[16,32]{1,0:T(8,128)} %ids_hbm.1, f32[16,32]{1,0:T(8,128)} %wts_hbm.1, s32[1,16]{1,0:T(1,128)} %bitcast.6, bf16[512,768]{1,0:T(8,128)(2,1)} %refs_0_.1), custom_call_target="tpu_custom_call" | custom-call | flops 1000000 | bytes 1953 | tf_op jit(solution)/shard_map/pallas_call | solution.py:271
  2.3 2.6 %collective-permute-start.4 = (bf16[160,768]{1,0:T(8,128)(2,1)S(1)}, bf16[160,768]{1,0:T(8,128)(2,1)S(1)}, u32[]{:S(2)}, u32[]{:S(2)}) collective-permute-start(bf16[160,768]{1,0:T(8,128)(2,1)S(1)} %get-tuple-element.55), channel_id=1, source_target_pairs={{0,2},{2,0},{4,6},{6,4},{8,10},{10,8},{12,14},{14,12},{1,3},{3,1},... | collective-permute-start | bytes 737288 | tf_op jit(solution)/shard_map/ppermute | solution.py:296
  4.9 1.6 %collective-permute-start.1 = (f32[16,128]{1,0:T(8,128)S(1)}, f32[16,128]{1,0:T(8,128)S(1)}, u32[]{:S(2)}, u32[]{:S(2)}) collective-permute-start(f32[16,128]{1,0:T(8,128)S(1)} %maximum_select_fusion.2.after), channel_id=1, source_target_pairs={{0,4},{2,6},{4,0},{6,2},{8,12},{10,14},{12,8},{14,10},{1,5},{3,7},... | collective-permute-start | bytes 24584 | tf_op jit(solution)/shard_map/ppermute | solution.py:296
  6.5 1.6 %shard_map.103 = (bf16[512,768]{1,0:T(8,128)(2,1)S(1)}, bf16[768,512]{1,0:T(8,128)(2,1)S(1)}, bf16[512,512]{1,0:T(8,128)(2,1)S(1)}, bf16[153,512]{1,0:T(8,128)(2,1)S(1)}) custom-call(f32[16,128]{1,0:T(8,128)S(1)} %maximum_select_fusion.2.after, bf16[512,768]{1,0:T(8,128)(2,1)} %refs_0_.1, bf16[768,512]{1,0:T(8,128)(2,1)} %refs_1_.1, ...), custom_call_target="tpu_custom_call" | custom-call | flops 1000000 | bytes 1953 | tf_op jit(solution)/shard_map/pallas_call | solution.py:271
  8.1 1.2 %shard_map.104.mine = bf16[153,512]{1,0:T(8,128)(2,1)S(1)} custom-call(bf16[512,768]{1,0:T(8,128)(2,1)S(1)} %get-tuple-element.49.x, bf16[768,512]{1,0:T(8,128)(2,1)S(1)} %get-tuple-element.50.w1, bf16[512,512]{1,0:T(8,128)(2,1)S(1)} %get-tuple-element.51.w2, bf16[153,512]{1,0:T(8,128)(2,1)S(1)} %get-tuple-element.52.w3.w3t, ...), custom_call_target="tpu_custom_call" | custom-call | flops 1000 | bytes 1 | tf_op jit(solution)/shard_map/pallas_call | solution.py:271
  9.3 2.7 %collective-permute-start.3 = (f32[32,128]{1,0:T(8,128)S(1)}, f32[32,128]{1,0:T(8,128)S(1)}, u32[]{:S(2)}, u32[]{:S(2)}) collective-permute-start(f32[32,128]{1,0:T(8,128)S(1)} %maximum_select_fusion.1), channel_id=1, source_target_pairs={{0,8},{2,10},{4,12},{6,14},{8,0},{10,2},{12,4},{14,6},{1,9},{3,11}... | collective-permute-start | bytes 49160 | tf_op jit(solution)/shard_map/ppermute | solution.py:296
  12.0 1.1 %collective-permute-start.2 = (bf16[153,512]{1,0:T(8,128)(2,1)S(1)}, bf16[153,512]{1,0:T(8,128)(2,1)S(1)}, u32[]{:S(2)}, u32[]{:S(2)}) collective-permute-start(bf16[153,512]{1,0:T(8,128)(2,1)S(1)} %shard_map.104.mine), channel_id=1, source_target_pairs={{0,2},{2,0},{4,6},{6,4},{8,10},{10,8},{12,14},{14,12},{1,3},{3,1},... | collective-permute-start | bytes 470024 | tf_op jit(solution)/shard_map/ppermute | solution.py:296
  14.0 1.9 %shard_map.105 = (bf16[1024,128]{1,0:T(8,128)(2,1)S(1)}, bf16[1024,128]{1,0:T(8,128)(2,1)S(1)}, s32[1,128]{1,0:T(1,128)S(1)}) custom-call(f32[64,128]{1,0:T(8,128)S(1)} %maximum_select_fusion.packed), custom_call_target="tpu_custom_call" | custom-call | flops 1000000000 | bytes 1953125 | tf_op jit(solution)/shard_map/pallas_call | solution.py:271
  15.9 1.2 %collective-permute-start.9 = (bf16[96,768]{1,0:T(8,128)(2,1)S(1)}, bf16[96,768]{1,0:T(8,128)(2,1)S(1)}, u32[]{:S(2)}, u32[]{:S(2)}) collective-permute-start(bf16[96,768]{1,0:T(8,128)(2,1)S(1)} %get-tuple-element.74), channel_id=1, source_target_pairs={{0,2},{2,0},{4,6},{6,4},{8,10},{10,8},{12,14},{14,12},{1,3},{3,1},... | collective-permute-start | bytes 442376 | tf_op jit(solution)/shard_map/ppermute | solution.py:296
  18.8 1.4 %shard_map.107 = (bf16[768,512]{1,0:T(8,128)(2,1)S(1)}, bf16[512,512]{1,0:T(8,128)(2,1)S(1)}, bf16[512,128]{1,0:T(8,128)(2,1)S(1)}, f32[512,128]{1,0:T(8,128)S(1)}, f32[512,512]{1,0:T(8,128)S(1)}) custom-call(bf16[512,768]{1,0:T(8,128)(2,1)S(1)} %get-tuple-element.49.x, bf16[768,512]{1,0:T(8,128)(2,1)S(1)} %get-tuple-element.50.w1, ...), custom_call_target="tpu_custom_call" | custom-call | flops 1000 | bytes 1 | tf_op jit(solution)/shard_map/pallas_call | solution.py:271
  20.2 1.1 %collective-permute-start.7 = (f32[64,128]{1,0:T(8,128)S(1)}, f32[64,128]{1,0:T(8,128)S(1)}, u32[]{:S(2)}, u32[]{:S(2)}) collective-permute-start(f32[64,128]{1,0:T(8,128)S(1)} %maximum_select_fusion.packed), channel_id=1, source_target_pairs={{0,2},{2,0},{4,6},{6,4},{8,10},{10,8},{12,14},{14,12},{1,3},{3,1},... | collective-permute-start | bytes 98312 | tf_op jit(solution)/shard_map/ppermute | solution.py:296
  22.8 1.8 %collective-permute-start.6 = (bf16[153,128]{1,0:T(8,128)(2,1)S(1)}, bf16[153,128]{1,0:T(8,128)(2,1)S(1)}, u32[]{:S(2)}, u32[]{:S(2)}) collective-permute-start(bf16[153,128]{1,0:T(8,128)(2,1)S(1)} %get-tuple-element.92), channel_id=1, source_target_pairs={{0,8},{2,10},{4,12},{6,14},{8,0},{10,2},{12,4},{14,6},{1,9},{3,11}... | collective-permute-start | bytes 117512 | tf_op jit(solution)/shard_map/ppermute | solution.py:296
  24.7 2.2 %shard_map.108 = (bf16[1024,128]{1,0:T(8,128)(2,1)S(1)}, bf16[1024,128]{1,0:T(8,128)(2,1)S(1)}, s32[1,128]{1,0:T(1,128)}) custom-call(f32[64,128]{1,0:T(8,128)S(1)} %collective-permute-done.7.packed), custom_call_target="tpu_custom_call" | custom-call | flops 1000000000 | bytes 1953125 | tf_op jit(solution)/shard_map/pallas_call | solution.py:271
  26.9 1.4 %collective-permute-done.6.got = bf16[153,128]{1,0:T(8,128)(2,1)S(1)} collective-permute-done((bf16[153,128]{1,0:T(8,128)(2,1)S(1)}, bf16[153,128]{1,0:T(8,128)(2,1)S(1)}, u32[]{:S(2)}, u32[]{:S(2)}) %collective-permute-start.6) | collective-permute-done | bytes 39200 | tf_op jit(solution)/shard_map/ppermute | solution.py:296
  28.3 1.1 %collective-permute-start.8 = (bf16[153,128]{1,0:T(8,128)(2,1)S(1)}, bf16[153,128]{1,0:T(8,128)(2,1)S(1)}, u32[]{:S(2)}, u32[]{:S(2)}) collective-permute-start(bf16[153,128]{1,0:T(8,128)(2,1)S(1)} %get-tuple-element.69), channel_id=1, source_target_pairs={{0,2},{2,0},{4,6},{6,4},{8,10},{10,8},{12,14},{14,12},{1,3},{3,1},... | collective-permute-start | bytes 117512 | tf_op jit(solution)/shard_map/ppermute | solution.py:296
  29.4 1.5 %shard_map.110 = (bf16[768,512]{1,0:T(8,128)(2,1)S(1)}, bf16[512,512]{1,0:T(8,128)(2,1)S(1)}, bf16[512,128]{1,0:T(8,128)(2,1)S(1)}, f32[512,128]{1,0:T(8,128)S(1)}, f32[512,512]{1,0:T(8,128)S(1)}) custom-call(bf16[160,768]{1,0:T(8,128)(2,1)S(1)} %collective-permute-done.4.near, bf16[96,768]{1,0:T(8,128)(2,1)S(1)} %collective-permute-done.9.late, ...), custom_call_target="tpu_custom_call" | custom-call | flops 2000000000 | bytes 3906250 | tf_op jit(solution)/shard_map/pallas_call | solution.py:271
  30.9 1.5 %collective-permute-done.8.far_grad = bf16[153,128]{1,0:T(8,128)(2,1)S(1)} collective-permute-done((bf16[153,128]{1,0:T(8,128)(2,1)S(1)}, bf16[153,128]{1,0:T(8,128)(2,1)S(1)}, u32[]{:S(2)}, u32[]{:S(2)}) %collective-permute-start.8) | collective-permute-done | bytes 39200 | tf_op jit(solution)/shard_map/ppermute | solution.py:296
  32.4 2.3 %shard_map.111 = (bf16[720,128]{1,0:T(8,128)(2,1)S(1)}, f32[720,128]{1,0:T(8,128)S(1)}) custom-call(f32[153,128]{1,0:T(8,128)S(1)} %get-tuple-element.68.grad, bf16[153,128]{1,0:T(8,128)(2,1)S(1)} %collective-permute-done.8.far_grad, bf16[1024,128]{1,0:T(8,128)(2,1)S(1)} %get-tuple-element.57.high, bf16[1024,128]{1,0:T(8,128)(2,1)S(1)} %get-tuple-element.58.low, ...), custom_call_target="tpu_custom_call" | custom-call | flops 1000000 | bytes 1953 | tf_op jit(solution)/shard_map/pallas_call | solution.py:271
  34.9 5.3 %collective-permute-done.12.got = bf16[720,128]{1,0:T(8,128)(2,1)S(1)} collective-permute-done((bf16[720,128]{1,0:T(8,128)(2,1)S(1)}, bf16[720,128]{1,0:T(8,128)(2,1)S(1)}, u32[]{:S(2)}, u32[]{:S(2)}) %collective-permute-start.12) | collective-permute-done | bytes 184352 | tf_op jit(solution)/shard_map/ppermute | solution.py:296
  40.3 2.1 %collective-permute-start.13 = (bf16[720,128]{1,0:T(8,128)(2,1)S(1)}, bf16[720,128]{1,0:T(8,128)(2,1)S(1)}, u32[]{:S(2)}, u32[]{:S(2)}) collective-permute-start(bf16[720,128]{1,0:T(8,128)(2,1)S(1)} %shard_map.112.kept), channel_id=1, source_target_pairs={{0,8},{2,10},{4,12},{6,14},{8,0},{10,2},{12,4},{14,6},{1,9},{3,11}... | collective-permute-start | bytes 552968 | tf_op jit(solution)/shard_map/ppermute | solution.py:296
  42.4 6.1 %collective-permute-done.13.got = bf16[720,128]{1,0:T(8,128)(2,1)S(1)} collective-permute-done((bf16[720,128]{1,0:T(8,128)(2,1)S(1)}, bf16[720,128]{1,0:T(8,128)(2,1)S(1)}, u32[]{:S(2)}, u32[]{:S(2)}) %collective-permute-start.13) | collective-permute-done | bytes 184352 | tf_op jit(solution)/shard_map/ppermute | solution.py:296
  49.6 4.6 %collective-permute-done.14.refs_1_ = bf16[720,128]{1,0:T(8,128)(2,1)S(1)} collective-permute-done((bf16[720,128]{1,0:T(8,128)(2,1)S(1)}, bf16[720,128]{1,0:T(8,128)(2,1)S(1)}, u32[]{:S(2)}, u32[]{:S(2)}) %collective-permute-start.14) | collective-permute-done | bytes 184352 | tf_op jit(solution)/shard_map/ppermute | solution.py:296
  55.8 3.9 %collective-permute-done.16.refs_3_ = bf16[720,128]{1,0:T(8,128)(2,1)S(1)} collective-permute-done((bf16[720,128]{1,0:T(8,128)(2,1)S(1)}, bf16[720,128]{1,0:T(8,128)(2,1)S(1)}, u32[]{:S(2)}, u32[]{:S(2)}) %collective-permute-start.16) | collective-permute-done | bytes 184352 | tf_op jit(solution)/shard_map/ppermute | solution.py:296
  61.2 1.4 %shard_map.114 = (bf16[768,512]{1,0:T(8,128)(2,1)}, bf16[512,512]{1,0:T(8,128)(2,1)}, bf16[153,512]{1,0:T(8,128)(2,1)}) custom-call(bf16[720,128]{1,0:T(8,128)(2,1)S(1)} %shard_map.113.refs_0_, bf16[720,128]{1,0:T(8,128)(2,1)S(1)} %collective-permute-done.14.refs_1_, bf16[720,128]{1,0:T(8,128)(2,1)S(1)} %collective-permute-done.15.refs_2_, ...), custom_call_target="tpu_custom_call" | custom-call | flops 1000000 | bytes 1953 | tf_op jit(solution)/shard_map/pallas_call | solution.py:271
  (36 shorter events, 9.3 us)
Async XLA Ops:
  1.8 3.1 %collective-permute-start = (f32[16,64]{1,0:T(8,128)S(1)}, f32[16,64]{1,0:T(8,128)S(1)}, u32[]{:S(2)}, u32[]{:S(2)}) collective-permute-start(f32[16,64]{1,0:T(8,128)S(1)} %get-tuple-element.48), channel_id=1, source_target_pairs={{0,1},{1,0},{2,3},{3,2},{4,5},{5,4},{6,7},{7,6},{8,9},{9,8},{10,11... | collective-permute-start | bytes 12296 | tf_op jit(solution)/shard_map/ppermute | solution.py:299
  2.3 11.7 %collective-permute-start.4 = (bf16[160,768]{1,0:T(8,128)(2,1)S(1)}, bf16[160,768]{1,0:T(8,128)(2,1)S(1)}, u32[]{:S(2)}, u32[]{:S(2)}) collective-permute-start(bf16[160,768]{1,0:T(8,128)(2,1)S(1)} %get-tuple-element.55), channel_id=1, source_target_pairs={{0,2},{2,0},{4,6},{6,4},{8,10},{10,8},{12,14},{14,12},{1,3},{3,1},... | collective-permute-start | bytes 737288 | tf_op jit(solution)/shard_map/ppermute | solution.py:296
  4.9 4.4 %collective-permute-start.1 = (f32[16,128]{1,0:T(8,128)S(1)}, f32[16,128]{1,0:T(8,128)S(1)}, u32[]{:S(2)}, u32[]{:S(2)}) collective-permute-start(f32[16,128]{1,0:T(8,128)S(1)} %maximum_select_fusion.2.after), channel_id=1, source_target_pairs={{0,4},{2,6},{4,0},{6,2},{8,12},{10,14},{12,8},{14,10},{1,5},{3,7},... | collective-permute-start | bytes 24584 | tf_op jit(solution)/shard_map/ppermute | solution.py:296
  9.3 4.7 %collective-permute-start.3 = (f32[32,128]{1,0:T(8,128)S(1)}, f32[32,128]{1,0:T(8,128)S(1)}, u32[]{:S(2)}, u32[]{:S(2)}) collective-permute-start(f32[32,128]{1,0:T(8,128)S(1)} %maximum_select_fusion.1), channel_id=1, source_target_pairs={{0,8},{2,10},{4,12},{6,14},{8,0},{10,2},{12,4},{14,6},{1,9},{3,11}... | collective-permute-start | bytes 49160 | tf_op jit(solution)/shard_map/ppermute | solution.py:296
  12.0 5.9 %collective-permute-start.2 = (bf16[153,512]{1,0:T(8,128)(2,1)S(1)}, bf16[153,512]{1,0:T(8,128)(2,1)S(1)}, u32[]{:S(2)}, u32[]{:S(2)}) collective-permute-start(bf16[153,512]{1,0:T(8,128)(2,1)S(1)} %shard_map.104.mine), channel_id=1, source_target_pairs={{0,2},{2,0},{4,6},{6,4},{8,10},{10,8},{12,14},{14,12},{1,3},{3,1},... | collective-permute-start | bytes 470024 | tf_op jit(solution)/shard_map/ppermute | solution.py:296
  15.9 6.4 %collective-permute-start.9 = (bf16[96,768]{1,0:T(8,128)(2,1)S(1)}, bf16[96,768]{1,0:T(8,128)(2,1)S(1)}, u32[]{:S(2)}, u32[]{:S(2)}) collective-permute-start(bf16[96,768]{1,0:T(8,128)(2,1)S(1)} %get-tuple-element.74), channel_id=1, source_target_pairs={{0,2},{2,0},{4,6},{6,4},{8,10},{10,8},{12,14},{14,12},{1,3},{3,1},... | collective-permute-start | bytes 442376 | tf_op jit(solution)/shard_map/ppermute | solution.py:296
  18.2 4.1 %collective-permute-start.5 = (bf16[153,128]{1,0:T(8,128)(2,1)S(1)}, bf16[153,128]{1,0:T(8,128)(2,1)S(1)}, u32[]{:S(2)}, u32[]{:S(2)}) collective-permute-start(bf16[153,128]{1,0:T(8,128)(2,1)S(1)} %get-tuple-element.60.after), channel_id=1, source_target_pairs={{0,4},{2,6},{4,0},{6,2},{8,12},{10,14},{12,8},{14,10},{1,5},{3,7},... | collective-permute-start | bytes 117512 | tf_op jit(solution)/shard_map/ppermute | solution.py:296
  20.2 4.4 %collective-permute-start.7 = (f32[64,128]{1,0:T(8,128)S(1)}, f32[64,128]{1,0:T(8,128)S(1)}, u32[]{:S(2)}, u32[]{:S(2)}) collective-permute-start(f32[64,128]{1,0:T(8,128)S(1)} %maximum_select_fusion.packed), channel_id=1, source_target_pairs={{0,2},{2,0},{4,6},{6,4},{8,10},{10,8},{12,14},{14,12},{1,3},{3,1},... | collective-permute-start | bytes 98312 | tf_op jit(solution)/shard_map/ppermute | solution.py:296
  22.3 7.1 %collective-permute-start.11 = (bf16[96,768]{1,0:T(8,128)(2,1)S(1)}, bf16[96,768]{1,0:T(8,128)(2,1)S(1)}, u32[]{:S(2)}, u32[]{:S(2)}) collective-permute-start(bf16[96,768]{1,0:T(8,128)(2,1)S(1)} %collective-permute-done.9.late), channel_id=1, source_target_pairs={{0,1},{1,0},{2,3},{3,2},{4,5},{5,4},{6,7},{7,6},{8,9},{9,8},{10,11... | collective-permute-start | bytes 442376 | tf_op jit(solution)/shard_map/ppermute | solution.py:299
  22.3 7.1 %collective-permute-start.10 = (bf16[160,768]{1,0:T(8,128)(2,1)S(1)}, bf16[160,768]{1,0:T(8,128)(2,1)S(1)}, u32[]{:S(2)}, u32[]{:S(2)}) collective-permute-start(bf16[160,768]{1,0:T(8,128)(2,1)S(1)} %collective-permute-done.4.near), channel_id=1, source_target_pairs={{0,1},{1,0},{2,3},{3,2},{4,5},{5,4},{6,7},{7,6},{8,9},{9,8},{10,11... | collective-permute-start | bytes 737288 | tf_op jit(solution)/shard_map/ppermute | solution.py:299
  22.8 5.4 %collective-permute-start.6 = (bf16[153,128]{1,0:T(8,128)(2,1)S(1)}, bf16[153,128]{1,0:T(8,128)(2,1)S(1)}, u32[]{:S(2)}, u32[]{:S(2)}) collective-permute-start(bf16[153,128]{1,0:T(8,128)(2,1)S(1)} %get-tuple-element.92), channel_id=1, source_target_pairs={{0,8},{2,10},{4,12},{6,14},{8,0},{10,2},{12,4},{14,6},{1,9},{3,11}... | collective-permute-start | bytes 117512 | tf_op jit(solution)/shard_map/ppermute | solution.py:296
  28.3 4.1 %collective-permute-start.8 = (bf16[153,128]{1,0:T(8,128)(2,1)S(1)}, bf16[153,128]{1,0:T(8,128)(2,1)S(1)}, u32[]{:S(2)}, u32[]{:S(2)}) collective-permute-start(bf16[153,128]{1,0:T(8,128)(2,1)S(1)} %get-tuple-element.69), channel_id=1, source_target_pairs={{0,2},{2,0},{4,6},{6,4},{8,10},{10,8},{12,14},{14,12},{1,3},{3,1},... | collective-permute-start | bytes 117512 | tf_op jit(solution)/shard_map/ppermute | solution.py:296
  34.6 5.6 %collective-permute-start.12 = (bf16[720,128]{1,0:T(8,128)(2,1)S(1)}, bf16[720,128]{1,0:T(8,128)(2,1)S(1)}, u32[]{:S(2)}, u32[]{:S(2)}) collective-permute-start(bf16[720,128]{1,0:T(8,128)(2,1)S(1)} %get-tuple-element.87), channel_id=1, source_target_pairs={{0,4},{2,6},{4,0},{6,2},{8,12},{10,14},{12,8},{14,10},{1,5},{3,7},... | collective-permute-start | bytes 552968 | tf_op jit(solution)/shard_map/ppermute | solution.py:296
  40.3 8.3 %collective-permute-start.13 = (bf16[720,128]{1,0:T(8,128)(2,1)S(1)}, bf16[720,128]{1,0:T(8,128)(2,1)S(1)}, u32[]{:S(2)}, u32[]{:S(2)}) collective-permute-start(bf16[720,128]{1,0:T(8,128)(2,1)S(1)} %shard_map.112.kept), channel_id=1, source_target_pairs={{0,8},{2,10},{4,12},{6,14},{8,0},{10,2},{12,4},{14,6},{1,9},{3,11}... | collective-permute-start | bytes 552968 | tf_op jit(solution)/shard_map/ppermute | solution.py:296
  48.6 5.6 %collective-permute-start.14 = (bf16[720,128]{1,0:T(8,128)(2,1)S(1)}, bf16[720,128]{1,0:T(8,128)(2,1)S(1)}, u32[]{:S(2)}, u32[]{:S(2)}) collective-permute-start(bf16[720,128]{1,0:T(8,128)(2,1)S(1)} %shard_map.113.refs_0_), channel_id=1, source_target_pairs={{0,4},{2,6},{4,0},{6,2},{8,12},{10,14},{12,8},{14,10},{1,5},{3,7},... | collective-permute-start | bytes 552968 | tf_op jit(solution)/shard_map/ppermute | solution.py:296
  48.7 7.1 %collective-permute-start.15 = (bf16[720,128]{1,0:T(8,128)(2,1)S(1)}, bf16[720,128]{1,0:T(8,128)(2,1)S(1)}, u32[]{:S(2)}, u32[]{:S(2)}) collective-permute-start(bf16[720,128]{1,0:T(8,128)(2,1)S(1)} %shard_map.113.refs_0_), channel_id=1, source_target_pairs={{0,2},{2,0},{4,6},{6,4},{8,10},{10,8},{12,14},{14,12},{1,3},{3,1},... | collective-permute-start | bytes 552968 | tf_op jit(solution)/shard_map/ppermute | solution.py:296
  54.2 5.5 %collective-permute-start.16 = (bf16[720,128]{1,0:T(8,128)(2,1)S(1)}, bf16[720,128]{1,0:T(8,128)(2,1)S(1)}, u32[]{:S(2)}, u32[]{:S(2)}) collective-permute-start(bf16[720,128]{1,0:T(8,128)(2,1)S(1)} %collective-permute-done.14.refs_1_), channel_id=1, source_target_pairs={{0,2},{2,0},{4,6},{6,4},{8,10},{10,8},{12,14},{14,12},{1,3},{3,1},... | collective-permute-start | bytes 552968 | tf_op jit(solution)/shard_map/ppermute | solution.py:296
  55.1 5.2 %collective-permute-start.17 = (bf16[720,128]{1,0:T(8,128)(2,1)S(1)}, bf16[720,128]{1,0:T(8,128)(2,1)S(1)}, u32[]{:S(2)}, u32[]{:S(2)}) collective-permute-start(bf16[720,128]{1,0:T(8,128)(2,1)S(1)} %shard_map.113.refs_0_), channel_id=1, source_target_pairs={{0,1},{1,0},{2,3},{3,2},{4,5},{5,4},{6,7},{7,6},{8,9},{9,8},{10,11... | collective-permute-start | bytes 552968 | tf_op jit(solution)/shard_map/ppermute | solution.py:299
  55.1 5.2 %collective-permute-start.18 = (bf16[720,128]{1,0:T(8,128)(2,1)S(1)}, bf16[720,128]{1,0:T(8,128)(2,1)S(1)}, u32[]{:S(2)}, u32[]{:S(2)}) collective-permute-start(bf16[720,128]{1,0:T(8,128)(2,1)S(1)} %collective-permute-done.14.refs_1_), channel_id=1, source_target_pairs={{0,1},{1,0},{2,3},{3,2},{4,5},{5,4},{6,7},{7,6},{8,9},{9,8},{10,11... | collective-permute-start | bytes 552968 | tf_op jit(solution)/shard_map/ppermute | solution.py:299
  55.8 4.5 %collective-permute-start.19 = (bf16[720,128]{1,0:T(8,128)(2,1)S(1)}, bf16[720,128]{1,0:T(8,128)(2,1)S(1)}, u32[]{:S(2)}, u32[]{:S(2)}) collective-permute-start(bf16[720,128]{1,0:T(8,128)(2,1)S(1)} %collective-permute-done.15.refs_2_), channel_id=1, source_target_pairs={{0,1},{1,0},{2,3},{3,2},{4,5},{5,4},{6,7},{7,6},{8,9},{9,8},{10,11... | collective-permute-start | bytes 552968 | tf_op jit(solution)/shard_map/ppermute | solution.py:299
  59.7 1.4 %collective-permute-start.20 = (bf16[720,128]{1,0:T(8,128)(2,1)S(1)}, bf16[720,128]{1,0:T(8,128)(2,1)S(1)}, u32[]{:S(2)}, u32[]{:S(2)}) collective-permute-start(bf16[720,128]{1,0:T(8,128)(2,1)S(1)} %collective-permute-done.16.refs_3_), channel_id=1, source_target_pairs={{0,1},{1,0},{2,3},{3,2},{4,5},{5,4},{6,7},{7,6},{8,9},{9,8},{10,11... | collective-permute-start | bytes 552968 | tf_op jit(solution)/shard_map/ppermute | solution.py:299
